TPU v7x, 256 devices: a whole 4x4x8 slice. The times are simulated.
256 devices in a mesh: dp: 32 (over y, x, core), tensor: 8 (over z).
Axes of the slice: x: 4, y: 4, z: 8, core: 2. Of those that a mesh axis runs over, the one named last changes fastest.
Arguments:
- input_token_rows: bfloat16 [16384, 28672], P('dp', 'tensor'), may hold values from -120 to 120
- output_gradient_rows: bfloat16 [16384, 8192], P('dp'), may hold values from -1000 to 1000
- frozen_base_matrix: bfloat16 [8192, 28672], P('dp', 'tensor'), may hold values from -6 to 6
- left_lowrank_factor: float32 [256, 28672], P('dp', 'tensor'), may hold values from -6 to 6
- left_first_moment: float32 [256, 28672], P('dp', 'tensor'), may hold values from -4.5776367e-05 to 4.5776367e-05
- left_second_moment: float32 [256, 28672], P('dp', 'tensor'), may hold values from 5e-11 to 5e-10
- right_lowrank_factor: float32 [8192, 256], P('dp'), may hold values from -32 to 32
- right_first_moment: float32 [8192, 256], P('dp'), may hold values from -9.1552734e-05 to 9.1552734e-05
- right_second_moment: float32 [8192, 256], P('dp'), may hold values from 2e-10 to 2e-09
Outputs:
- merged_weight: bfloat16 [8192, 28672], P('dp', 'tensor')
All inputs are finite; a program needn't handle non-finite values.
Results may differ from a plain program's by a relative error of at most 0.001.
The roundings to bfloat16 on the way count: a program that leaves them out, or rounds other values in their place, can miss the bound.
Values may be sent and summed in bfloat16 or wider, within the bound.
No kernel may reach another device: no remote copies, remote signals or barrier semaphores. Data moves between devices by JAX's collectives and lax.ppermute only.
A program may use at most 128 MiB of HBM per device.

v0:
```python
import math

import jax
import jax.numpy as jnp
import numpy as np
from jax import lax
from jax.sharding import Mesh
from jax.sharding import PartitionSpec as P

HIDDEN_UNITS = 28672
FACTOR_RANK = 256
STEP = 5000

first_decay = 0.9
second_decay = 0.999
adam_epsilon = 1e-08
learn_rate = 0.05
clip_limit = 1.0
norm_epsilon = 1e-06

bf16 = jnp.bfloat16
f32 = jnp.float32
DP = ("y", "x", "core")


def moment_update_step(param, first, second, grad):
    first_new = first_decay * first + (1.0 - first_decay) * grad
    second_new = second_decay * second + (1.0 - second_decay) * grad * grad
    first_fix = 1.0 - first_decay**STEP
    second_fix = 1.0 - second_decay**STEP
    return param - learn_rate * (first_new / first_fix) / (
        jnp.sqrt(second_new / second_fix) + adam_epsilon
    )


def dp_index(y, x, c):
    return (y * 4 + x) * 2 + c


def plane_pairs(first, k):
    pairs = []
    for y in range(4):
        for x in range(4):
            for c in range(2):
                if (c == 0) == first:
                    target = dp_index(y, (x + k) % 4, c)
                else:
                    target = dp_index((y + k) % 4, x, c)
                pairs.append((dp_index(y, x, c), target))
    return pairs


def shift_p(v, k):
    return lax.ppermute(v, DP, plane_pairs(True, k))


def shift_q(v, k):
    return lax.ppermute(v, DP, plane_pairs(False, k))


def swap_core(v):
    return lax.ppermute(v, "core", [(0, 1), (1, 0)])


def shift_z(v, k):
    return lax.ppermute(v, "z", [(i, (i + k) % 8) for i in range(8)])


def flip(v, axis, n, bit):
    return lax.ppermute(v, axis, [(i, i ^ bit) for i in range(n)])


def pick(stack, index):
    return lax.dynamic_index_in_dim(stack, index, 0, keepdims=False)


def tiles(v):
    rows, columns = v.shape
    return v.reshape(rows // 8, 8, columns // 128, 128).swapaxes(1, 2).reshape(-1, 128)


def untile(v, rows, columns):
    count = v.shape[0]
    v = v.reshape(count, rows // 8, columns // 128, 8, 128).swapaxes(2, 3)
    return v.reshape(count, rows, columns)


def by_offset(stack, index):
    return jnp.stack([pick(stack, (index - j) % 4) for j in range(4)])


def join_cores(mine, other, core):
    zero = jnp.where(core == 0, mine, other)
    one = jnp.where(core == 0, other, mine)
    return jnp.stack([zero, one.swapaxes(0, 1)], axis=2)


def local(
    input_token_rows,
    output_gradient_rows,
    frozen_base_matrix,
    left_lowrank_factor,
    left_first_moment,
    left_second_moment,
    right_lowrank_factor,
    right_first_moment,
    right_second_moment,
):
    hidden_scale = 1.0 / math.sqrt(HIDDEN_UNITS)
    rank_scale = 1.0 / math.sqrt(FACTOR_RANK)
    y, x, core, z = (lax.axis_index(n) for n in ("y", "x", "core", "z"))
    p = jnp.where(core == 0, x, y)
    q = jnp.where(core == 0, y, x)

    b_block = lax.dynamic_slice_in_dim(right_lowrank_factor, (z % 2) * 128, 128, 1)
    block = jnp.concatenate([tiles(left_lowrank_factor), b_block], axis=0).astype(bf16)
    stack = jnp.stack([block] + [shift_p(block, k) for k in (1, 2, 3)])
    stack = by_offset(stack, p)
    stack = jnp.stack([stack] + [shift_q(stack, k) for k in (1, 2, 3)])
    stack = by_offset(stack, q)
    blocks = join_cores(stack, swap_core(stack), core).reshape(32, 480, 128)
    a_rows = untile(blocks[:, :224], 8, 3584).reshape(256, 3584)
    b_rows = blocks[:, 224:].reshape(8192, 128)

    act_part = lax.dot_general(
        a_rows, input_token_rows, (((1,), (1,)), ((), ())), preferred_element_type=f32
    ).reshape(4, 2, 32, 512)
    act_send = lax.dynamic_index_in_dim(act_part, 1 - z % 2, 1, keepdims=False)
    act_keep = lax.dynamic_index_in_dim(act_part, z % 2, 1, keepdims=False)
    b_rows, act_send = lax.optimization_barrier((b_rows, act_send))
    act_got = flip(act_send, "z", 8, 1)
    back_part = (
        lax.dot_general(
            b_rows, output_gradient_rows, (((0,), (1,)), ((), ())), preferred_element_type=f32
        )
        * rank_scale
    ).astype(bf16)
    back_other = flip(back_part, "z", 8, 1)
    act_got, back_other = lax.optimization_barrier((act_got, back_other))
    act_pair = act_keep + act_got
    act_pieces = [pick(act_pair, (z // 2 + k) % 4) for k in range(4)]
    low = z % 2 == 0
    back = jnp.concatenate(
        [jnp.where(low, back_part, back_other), jnp.where(low, back_other, back_part)], axis=0
    )
    back, act_pieces = lax.optimization_barrier((back, act_pieces))
    a_term = jnp.dot(back, input_token_rows, preferred_element_type=f32)
    act = act_pieces[0]
    for k in range(1, 4):
        act = act + shift_z(act_pieces[k], 2 * k)
    act = (act * hidden_scale).astype(bf16)
    b_term = jnp.dot(act, output_gradient_rows, preferred_element_type=f32)

    a_term = a_term.reshape(4, 4, 2, 8, 28, 128).swapaxes(3, 4).reshape(4, 4, 2, 224, 128)
    b_term = b_term.reshape(4, 8, 4, 4, 2, 2, 128).transpose(2, 3, 4, 0, 5, 1, 6)
    b_term = b_term.reshape(4, 4, 2, 64, 128)
    halves = []
    for term in (a_term, b_term):
        zero = term[:, :, 0].swapaxes(0, 1)
        one = term[:, :, 1]
        keep = jnp.where(core == 0, zero, one)
        got = swap_core(jnp.where(core == 0, one, zero))
        halves.append((keep, got))
    parts = []
    for k in range(4):
        parts.append(
            jnp.concatenate(
                [pick(keep, (p + k) % 4) + pick(got, (p + k) % 4) for keep, got in halves], axis=1
            )
        )
    total = parts[0]
    for k in range(1, 4):
        total = total + shift_p(parts[k], k)
    parts = [pick(total, (q + k) % 4) for k in range(4)]
    total = parts[0]
    for k in range(1, 4):
        total = total + shift_q(parts[k], k)
    grad_a = total[:224] * hidden_scale
    grad_b = total[224:] * rank_scale

    squares = jnp.sum(grad_a * grad_a, axis=0) + jnp.sum(grad_b * grad_b, axis=0)
    squares = lax.all_to_all(
        jnp.broadcast_to(squares, (256, 128)), ("y", "x", "core", "z"), 0, 0, tiled=True
    )
    other = flip(grad_b, "z", 8, 1)
    squares, other = lax.optimization_barrier((squares, other))
    pair = jnp.concatenate([jnp.where(low, grad_b, other), jnp.where(low, other, grad_b)], axis=0)
    clipper = jnp.minimum(1.0, clip_limit / (jnp.sqrt(jnp.sum(squares)) + norm_epsilon))

    new_a = moment_update_step(
        tiles(left_lowrank_factor),
        tiles(left_first_moment),
        tiles(left_second_moment),
        clipper * grad_a,
    ).astype(bf16)
    copies = jnp.broadcast_to(new_a, (16, 224, 128))
    copies, pair = lax.optimization_barrier((copies, pair))
    mine = lax.all_to_all(copies, ("y", "x"), 0, 0, tiled=True)
    pairs = [pair] + [shift_z(pair, 2 * k) for k in range(1, 4)]
    mine, pairs = lax.optimization_barrier((mine, pairs))
    other = swap_core(mine)
    whole_grad_b = by_offset(jnp.stack(pairs), z // 2).reshape(8, 64, 128)
    whole_grad_b = untile(whole_grad_b, 32, 256).reshape(256, 256)
    new_b = moment_update_step(
        right_lowrank_factor.T, right_first_moment.T, right_second_moment.T, clipper * whole_grad_b
    ).astype(bf16)
    fresh = jnp.stack([jnp.where(core == 0, mine, other), jnp.where(core == 0, other, mine)], axis=1)
    new_a = untile(fresh.reshape(32, 224, 128), 8, 3584).reshape(256, 3584)
    product = lax.dot_general(new_b, new_a, (((0,), (0,)), ((), ())), preferred_element_type=f32)
    return (frozen_base_matrix.astype(f32) + product * rank_scale).astype(bf16)


def solution(mesh):
    grid = Mesh(np.asarray(mesh.devices).reshape(4, 4, 2, 8), ("y", "x", "core", "z"))
    split = P(DP, "z")
    rows = P(DP, None)
    return jax.shard_map(
        local,
        mesh=grid,
        in_specs=(split, rows, split, split, split, split, rows, rows, rows),
        out_specs=split,
        check_vma=False,
    )
```

profile of v0, /device:TPU:1, one launch (start us, length us, event | category | flops | bytes accessed | tf_op | source)
XLA Modules:
  0.0 162.3 jit_solution(3325735691613118788)
XLA Ops:
  0.0 0.9 fusion.37
  0.9 0.9 dynamic-slice_convert_fusion
  1.9 3.6 %collective-permute-start.2 = (bf16[480,128]{1,0:T(8,128)(2,1)S(1)}, bf16[480,128]{1,0:T(8,128)(2,1)S(1)}, u32[]{:S(2)}, u32[]{:S(2)}) collective-permute-start(bf16[480,128]{1,0:T(8,128)(2,1)S(1)} %pad_maximum_fusion.11), channel_id=1, source_target_pairs={{0,48},{8,200},{16,0},{24,216},{32,16},{40,232},{48,32},{56,248},{... | collective-permute-start | bytes 368648 | tf_op jit(solution)/shard_map/ppermute | solution.py:54
  5.5 1.6 %collective-permute-start.1 = (bf16[480,128]{1,0:T(8,128)(2,1)S(1)}, bf16[480,128]{1,0:T(8,128)(2,1)S(1)}, u32[]{:S(2)}, u32[]{:S(2)}) collective-permute-start(bf16[480,128]{1,0:T(8,128)(2,1)S(1)} %pad_maximum_fusion.11), channel_id=1, source_target_pairs={{0,32},{8,136},{16,48},{24,152},{32,0},{40,168},{48,16},{56,184},{... | collective-permute-start | bytes 368648 | tf_op jit(solution)/shard_map/ppermute | solution.py:54
  7.1 0.9 fusion.57
  8.1 4.0 %collective-permute-done = bf16[480,128]{1,0:T(8,128)(2,1)S(1)} collective-permute-done((bf16[480,128]{1,0:T(8,128)(2,1)S(1)}, bf16[480,128]{1,0:T(8,128)(2,1)S(1)}, u32[]{:S(2)}, u32[]{:S(2)}) %collective-permute-start) | collective-permute-done | bytes 122912 | tf_op jit(solution)/shard_map/ppermute | solution.py:54
  12.2 1.0 collective-permute-start.3
  13.2 2.7 %collective-permute-start.4 = (bf16[4,480,128]{2,1,0:T(8,128)(2,1)S(1)}, bf16[4,480,128]{2,1,0:T(8,128)(2,1)S(1)}, u32[]{:S(2)}, u32[]{:S(2)}) collective-permute-start(bf16[4,480,128]{2,1,0:T(8,128)(2,1)S(1)} %get-tuple-element.65), channel_id=1, source_target_pairs={{0,128},{8,40},{16,144},{24,56},{32,160},{40,8},{48,176},{56,24},{... | collective-permute-start | bytes 1474568 | tf_op jit(solution)/shard_map/ppermute | solution.py:58
  16.0 0.9 collective-permute-start.5
  16.8 4.7 %collective-permute-done.3 = bf16[4,480,128]{2,1,0:T(8,128)(2,1)S(1)} collective-permute-done((bf16[4,480,128]{2,1,0:T(8,128)(2,1)S(1)}, bf16[4,480,128]{2,1,0:T(8,128)(2,1)S(1)}, u32[]{:S(2)}, u32[]{:S(2)}) %collective-permute-start.3) | collective-permute-done | bytes 491552 | tf_op jit(solution)/shard_map/ppermute | solution.py:58
  21.5 6.3 %collective-permute-done.4 = bf16[4,480,128]{2,1,0:T(8,128)(2,1)S(1)} collective-permute-done((bf16[4,480,128]{2,1,0:T(8,128)(2,1)S(1)}, bf16[4,480,128]{2,1,0:T(8,128)(2,1)S(1)}, u32[]{:S(2)}, u32[]{:S(2)}) %collective-permute-start.4) | collective-permute-done | bytes 491552 | tf_op jit(solution)/shard_map/ppermute | solution.py:58
  28.2 1.6 pad_maximum_fusion.2
  29.7 2.7 %collective-permute-start.6 = (bf16[4,4,480,128]{3,2,0,1:T(8,128)(2,1)}, bf16[4,4,480,128]{3,2,0,1:T(8,128)(2,1)}, u32[]{:S(2)}, u32[]{:S(2)}) collective-permute-start(bf16[4,4,480,128]{3,2,0,1:T(8,128)(2,1)} %pad_maximum_fusion.2), channel_id=1, source_target_pairs={{0,8},{8,0},{1,9},{9,1},{2,10},{10,2},{3,11},{11,3},{4,12},{12,4},... | collective-permute-start | bytes 5898248 | tf_op jit(solution)/shard_map/ppermute | solution.py:62
  32.4 3.9 %collective-permute-done.6 = bf16[4,4,480,128]{3,2,0,1:T(8,128)(2,1)} collective-permute-done((bf16[4,4,480,128]{3,2,0,1:T(8,128)(2,1)}, bf16[4,4,480,128]{3,2,0,1:T(8,128)(2,1)}, u32[]{:S(2)}, u32[]{:S(2)}) %collective-permute-start.6) | collective-permute-done | bytes 1966112 | tf_op jit(solution)/shard_map/ppermute | solution.py:62
  36.3 1.7 %select_bitcast_fusion.1 = (bf16[4,4,1,480,128]{4,3,0,1,2:T(8,128)(2,1)S(1)}, bf16[4,4,1,480,128]{4,3,2,1,0:T(8,128)(2,1)S(1)}) fusion(bf16[4,4,480,128]{3,2,0,1:T(8,128)(2,1)} %collective-permute-done.6, pred[]{:T(512)S(6)} %eq.56, bf16[1,4,480,128]{3,2,0,1:T(8,128)(2,1)S(1)} %get-tuple-element.50, bf16[1,4,480,128]{3,2,0,1:T(8,128)(2,1)S(1)} %get-tuple-element.51, ...), kind=kLoop, calls=%fused_computation.9 | loop fusion | flops 4915200 | bytes 7864321 | tf_op jit(solution)/shard_map/stack | solution.py:95
  38.0 0.3 pad_maximum_fusion
  38.8 1.6 %copy-done = bf16[512,3584]{1,0:T(8,128)(2,1)S(1)} copy-done((bf16[512,3584]{1,0:T(8,128)(2,1)S(1)}, bf16[512,3584]{1,0:T(8,128)(2,1)}, u32[]{:S(2)}) %copy-start) | copy-done | bytes 3670040
  40.4 1.1 fusion.2
  41.6 1.7 %collective-permute-start.7 = (f32[4,32,512]{2,1,0:T(8,128)S(1)}, f32[4,32,512]{2,1,0:T(8,128)S(1)}, u32[]{:S(2)}, u32[]{:S(2)}) collective-permute-start(f32[4,32,512]{2,1,0:T(8,128)S(1)} %dynamic-slice_bitcast_fusion), channel_id=1, source_target_pairs={{0,1},{1,0},{2,3},{3,2},{4,5},{5,4},{6,7},{7,6},{8,9},{9,8},{10,11... | collective-permute-start | bytes 786440 | tf_op jit(solution)/shard_map/ppermute | solution.py:70
  43.3 2.9 %fusion.6 = bf16[128,512]{1,0:T(8,128)(2,1)S(1)} fusion(bf16[8192,128]{1,0:T(8,128)(2,1)S(1)} %bitcast.201, bf16[512,8192]{1,0:T(8,128)(2,1)S(1)} %bitcast.195), kind=kOutput, calls=%fused_computation.16 | convolution fusion | flops 1073872896 | bytes 10616832 | tf_op jit(solution)/shard_map/dot_general | solution.py:133
  46.2 1.3 collective-permute-start.8
  47.5 4.8 %collective-permute-done.8 = bf16[128,512]{1,0:T(8,128)(2,1)S(1)} collective-permute-done((bf16[128,512]{1,0:T(8,128)(2,1)S(1)}, bf16[128,512]{1,0:T(8,128)(2,1)S(1)}, u32[]{:S(2)}, u32[]{:S(2)}) %collective-permute-start.8) | collective-permute-done | bytes 131104 | tf_op jit(solution)/shard_map/ppermute | solution.py:70
  52.5 3.3 %fusion.49 = f32[256,3584]{1,0:T(8,128)S(1)} fusion(bf16[256,512]{1,0:T(8,128)(2,1)S(1)} %pad_maximum_fusion.9, bf16[512,3584]{1,0:T(8,128)(2,1)} %param.9), kind=kOutput, calls=%fused_computation.118 | convolution fusion | flops 939524096 | bytes 7602176 | tf_op jit(solution)/shard_map/dot_general | solution.py:147
  55.8 1.5 fusion.5
  57.3 1.0 collective-permute-start.9
  58.3 3.0 %collective-permute-start.10 = (f32[32,512]{1,0:T(8,128)S(1)}, f32[32,512]{1,0:T(8,128)S(1)}, u32[]{:S(2)}, u32[]{:S(2)}) collective-permute-start(f32[32,512]{1,0:T(8,128)S(1)} %get-tuple-element.29), channel_id=1, source_target_pairs={{0,2},{1,3},{2,4},{3,5},{4,6},{5,7},{6,0},{7,1},{8,10},{9,11},{10,... | collective-permute-start | bytes 196616 | tf_op jit(solution)/shard_map/ppermute | solution.py:66
  61.3 4.9 %collective-permute-start.11 = (f32[32,512]{1,0:T(8,128)S(1)}, f32[32,512]{1,0:T(8,128)S(1)}, u32[]{:S(2)}, u32[]{:S(2)}) collective-permute-start(f32[32,512]{1,0:T(8,128)S(1)} %get-tuple-element.30), channel_id=1, source_target_pairs={{0,4},{1,5},{2,6},{3,7},{4,0},{5,1},{6,2},{7,3},{8,12},{9,13},{10,... | collective-permute-start | bytes 196616 | tf_op jit(solution)/shard_map/ppermute | solution.py:66
  66.3 2.4 %collective-permute-start.12 = (f32[32,512]{1,0:T(8,128)S(1)}, f32[32,512]{1,0:T(8,128)S(1)}, u32[]{:S(2)}, u32[]{:S(2)}) collective-permute-start(f32[32,512]{1,0:T(8,128)S(1)} %get-tuple-element.31), channel_id=1, source_target_pairs={{0,6},{1,7},{2,0},{3,1},{4,2},{5,3},{6,4},{7,5},{8,14},{9,15},{10,... | collective-permute-start | bytes 196616 | tf_op jit(solution)/shard_map/ppermute | solution.py:66
  68.7 2.7 %collective-permute-done.11 = f32[32,512]{1,0:T(8,128)S(1)} collective-permute-done((f32[32,512]{1,0:T(8,128)S(1)}, f32[32,512]{1,0:T(8,128)S(1)}, u32[]{:S(2)}, u32[]{:S(2)}) %collective-permute-start.11) | collective-permute-done | bytes 65568 | tf_op jit(solution)/shard_map/ppermute | solution.py:66
  71.4 2.1 %collective-permute-done.12 = f32[32,512]{1,0:T(8,128)S(1)} collective-permute-done((f32[32,512]{1,0:T(8,128)S(1)}, f32[32,512]{1,0:T(8,128)S(1)}, u32[]{:S(2)}, u32[]{:S(2)}) %collective-permute-start.12) | collective-permute-done | bytes 65568 | tf_op jit(solution)/shard_map/ppermute | solution.py:66
  73.5 1.5 fusion.38
  75.3 0.6 collective-permute-start.13
  75.9 1.5 collective-permute-done.13
  77.4 0.7 add_bitcast_fusion.7
  78.1 1.6 %add_bitcast_fusion.3 = (f32[4,224,128]{2,1,0:T(8,128)S(1)}, f32[4,224,128]{2,1,0:T(8,128)S(1)}, f32[4,224,128]{2,1,0:T(8,128)S(1)}, f32[4,224,128]{2,1,0:T(8,128)S(1)}) fusion(f32[4,4,224,128]{3,2,1,0:T(8,128)} %collective-permute-done.9, s32[]{:T(128)S(6)} %select_n.315, f32[4,4,224,128]{3,2,1,0:T(8,128)S(1)} %get-tuple-element.41, s32[]{:T(128)S(6)} %select_n.356, ...), kind=kLoop, calls=%fused_computation.34 | loop fusion | flops 458752 | bytes 5505040 | tf_op jit(solution)/shard_map/add | solution.py:168
  79.8 1.4 collective-permute-start.14
  81.3 1.9 %collective-permute-start.15 = (f32[4,288,128]{2,1,0:T(8,128)S(1)}, f32[4,288,128]{2,1,0:T(8,128)S(1)}, u32[]{:S(2)}, u32[]{:S(2)}) collective-permute-start(f32[4,288,128]{2,1,0:T(8,128)S(1)} %pad_maximum_fusion.5), channel_id=1, source_target_pairs={{0,32},{8,136},{16,48},{24,152},{32,0},{40,168},{48,16},{56,184},{... | collective-permute-start | bytes 1769480 | tf_op jit(solution)/shard_map/ppermute | solution.py:54
  83.2 1.5 collective-permute-start.16
  84.8 5.3 %collective-permute-done.14 = f32[4,288,128]{2,1,0:T(8,128)S(1)} collective-permute-done((f32[4,288,128]{2,1,0:T(8,128)S(1)}, f32[4,288,128]{2,1,0:T(8,128)S(1)}, u32[]{:S(2)}, u32[]{:S(2)}) %collective-permute-start.14) | collective-permute-done | bytes 589856 | tf_op jit(solution)/shard_map/ppermute | solution.py:54
  90.1 6.8 %collective-permute-done.15 = f32[4,288,128]{2,1,0:T(8,128)S(1)} collective-permute-done((f32[4,288,128]{2,1,0:T(8,128)S(1)}, f32[4,288,128]{2,1,0:T(8,128)S(1)}, u32[]{:S(2)}, u32[]{:S(2)}) %collective-permute-start.15) | collective-permute-done | bytes 589856 | tf_op jit(solution)/shard_map/ppermute | solution.py:54
  96.9 0.3 collective-permute-done.16
  97.3 1.2 fusion.8
  98.7 3.1 %collective-permute-start.18 = (f32[288,128]{1,0:T(8,128)S(1)}, f32[288,128]{1,0:T(8,128)S(1)}, u32[]{:S(2)}, u32[]{:S(2)}) collective-permute-start(f32[288,128]{1,0:T(8,128)S(1)} %get-tuple-element.63), channel_id=1, source_target_pairs={{0,128},{8,40},{16,144},{24,56},{32,160},{40,8},{48,176},{56,24},{... | collective-permute-start | bytes 442376 | tf_op jit(solution)/shard_map/ppermute | solution.py:58
  101.8 2.1 %collective-permute-done.17 = f32[288,128]{1,0:T(8,128)S(1)} collective-permute-done((f32[288,128]{1,0:T(8,128)S(1)}, f32[288,128]{1,0:T(8,128)S(1)}, u32[]{:S(2)}, u32[]{:S(2)}) %collective-permute-start.17) | collective-permute-done | bytes 147488 | tf_op jit(solution)/shard_map/ppermute | solution.py:58
  103.8 2.0 %collective-permute-done.18 = f32[288,128]{1,0:T(8,128)S(1)} collective-permute-done((f32[288,128]{1,0:T(8,128)S(1)}, f32[288,128]{1,0:T(8,128)S(1)}, u32[]{:S(2)}, u32[]{:S(2)}) %collective-permute-start.18) | collective-permute-done | bytes 147488 | tf_op jit(solution)/shard_map/ppermute | solution.py:58
  106.2 0.7 broadcast_in_dim.6
  107.0 13.4 %all-to-all-start = ((f32[256,1,128]{2,1,0:T(1,128)}), f32[256,1,128]{2,1,0:T(1,128)S(1)}, u32[]{:S(2)}, u32[]{:S(2)}) async-start(f32[256,1,128]{2,1,0:T(1,128)} %broadcast_in_dim.6), calls=%async_computation | async-start | bytes 262144 | tf_op jit(solution)/shard_map/all_to_all | solution.py:182
  120.4 1.6 collective-permute-start.20
  122.0 2.3 %collective-permute-done.20 = f32[64,128]{1,0:T(8,128)S(1)} collective-permute-done((f32[64,128]{1,0:T(8,128)S(1)}, f32[64,128]{1,0:T(8,128)S(1)}, u32[]{:S(2)}, u32[]{:S(2)}) %collective-permute-start.20) | collective-permute-done | bytes 32800 | tf_op jit(solution)/shard_map/ppermute | solution.py:70
  124.3 9.1 %all-to-all-done = f32[256,1,128]{2,1,0:T(1,128)S(1)} async-done(((f32[256,1,128]{2,1,0:T(1,128)}), f32[256,1,128]{2,1,0:T(1,128)S(1)}, u32[]{:S(2)}, u32[]{:S(2)}) %all-to-all-start) | async-done | bytes 131104 | tf_op jit(solution)/shard_map/all_to_all | solution.py:182
  133.5 0.6 reduce_sum.29
  135.0 1.0 broadcast_in_dim.7
  136.0 3.6 %all-to-all-start.1 = ((bf16[16,224,128]{2,1,0:T(8,128)(2,1)}), bf16[16,224,128]{2,1,0:T(8,128)(2,1)S(1)}, u32[]{:S(2)}, u32[]{:S(2)}) async-start(bf16[16,224,128]{2,1,0:T(8,128)(2,1)} %broadcast_in_dim.7), calls=%async_computation.1 | async-start | bytes 1835008 | tf_op jit(solution)/shard_map/all_to_all | solution.py:198
  139.7 0.7 collective-permute-start.21
  140.4 1.7 %collective-permute-start.22 = (f32[128,128]{1,0:T(8,128)S(1)}, f32[128,128]{1,0:T(8,128)S(1)}, u32[]{:S(2)}, u32[]{:S(2)}) collective-permute-start(f32[128,128]{1,0:T(8,128)S(1)} %pad_maximum_fusion.12), channel_id=1, source_target_pairs={{0,4},{1,5},{2,6},{3,7},{4,0},{5,1},{6,2},{7,3},{8,12},{9,13},{10,... | collective-permute-start | bytes 196616 | tf_op jit(solution)/shard_map/ppermute | solution.py:66
  142.1 2.0 %collective-permute-start.23 = (f32[128,128]{1,0:T(8,128)S(1)}, f32[128,128]{1,0:T(8,128)S(1)}, u32[]{:S(2)}, u32[]{:S(2)}) collective-permute-start(f32[128,128]{1,0:T(8,128)S(1)} %pad_maximum_fusion.12), channel_id=1, source_target_pairs={{0,6},{1,7},{2,0},{3,1},{4,2},{5,3},{6,4},{7,5},{8,14},{9,15},{10,... | collective-permute-start | bytes 196616 | tf_op jit(solution)/shard_map/ppermute | solution.py:66
  144.1 1.2 collective-permute-done.21
  145.3 2.4 %collective-permute-done.22 = f32[128,128]{1,0:T(8,128)S(1)} collective-permute-done((f32[128,128]{1,0:T(8,128)S(1)}, f32[128,128]{1,0:T(8,128)S(1)}, u32[]{:S(2)}, u32[]{:S(2)}) %collective-permute-start.22) | collective-permute-done | bytes 65568 | tf_op jit(solution)/shard_map/ppermute | solution.py:66
  147.7 2.6 %collective-permute-done.23 = f32[128,128]{1,0:T(8,128)S(1)} collective-permute-done((f32[128,128]{1,0:T(8,128)S(1)}, f32[128,128]{1,0:T(8,128)S(1)}, u32[]{:S(2)}, u32[]{:S(2)}) %collective-permute-start.23) | collective-permute-done | bytes 65568 | tf_op jit(solution)/shard_map/ppermute | solution.py:66
  150.4 4.2 %all-to-all-done.1 = bf16[16,224,128]{2,1,0:T(8,128)(2,1)S(1)} async-done(((bf16[16,224,128]{2,1,0:T(8,128)(2,1)}), bf16[16,224,128]{2,1,0:T(8,128)(2,1)S(1)}, u32[]{:S(2)}, u32[]{:S(2)}) %all-to-all-start.1) | async-done | bytes 917536 | tf_op jit(solution)/shard_map/all_to_all | solution.py:198
  154.6 2.0 %collective-permute-start.24 = (bf16[16,224,128]{2,1,0:T(8,128)(2,1)S(1)}, bf16[16,224,128]{2,1,0:T(8,128)(2,1)S(1)}, u32[]{:S(2)}, u32[]{:S(2)}) collective-permute-start(bf16[16,224,128]{2,1,0:T(8,128)(2,1)S(1)} %all-to-all-done.1), channel_id=1, source_target_pairs={{0,8},{8,0},{1,9},{9,1},{2,10},{10,2},{3,11},{11,3},{4,12},{12,4},... | collective-permute-start | bytes 2752520 | tf_op jit(solution)/shard_map/ppermute | solution.py:62
  157.1 1.6 collective-permute-done.24
  158.9 1.3 copy-done.1
  160.2 2.1 %fusion.1 = bf16[256,3584]{1,0:T(8,128)(2,1)} fusion(bf16[256,3584]{1,0:T(8,128)(2,1)S(1)} %bitcast.202, bf16[256,3584]{1,0:T(8,128)(2,1)S(1)} %copy-done.1, f32[256,256]{1,0:T(8,128)S(1)} %bitcast.206, f32[256,256]{0,1:T(8,128)S(1)} %copy.28, f32[256,256]{0,1:T(8,128)S(1)} %copy.19, f32[256,256]{0,1:T(8,128)S(1)} %copy.18), kind=kOutput, calls=%fused_computation.2 | convolution fusion | flops 474284032 | bytes 6553600 | tf_op jit(solution)/shard_map/dot_general | solution.py:209
  (68 shorter events, 2.9 us)
Async XLA Ops:
  1.9 6.2 %collective-permute-start.2 = (bf16[480,128]{1,0:T(8,128)(2,1)S(1)}, bf16[480,128]{1,0:T(8,128)(2,1)S(1)}, u32[]{:S(2)}, u32[]{:S(2)}) collective-permute-start(bf16[480,128]{1,0:T(8,128)(2,1)S(1)} %pad_maximum_fusion.11), channel_id=1, source_target_pairs={{0,48},{8,200},{16,0},{24,216},{32,16},{40,232},{48,32},{56,248},{... | collective-permute-start | bytes 368648 | tf_op jit(solution)/shard_map/ppermute | solution.py:54
  5.5 6.6 %collective-permute-start = (bf16[480,128]{1,0:T(8,128)(2,1)S(1)}, bf16[480,128]{1,0:T(8,128)(2,1)S(1)}, u32[]{:S(2)}, u32[]{:S(2)}) collective-permute-start(bf16[480,128]{1,0:T(8,128)(2,1)S(1)} %pad_maximum_fusion.11), channel_id=1, source_target_pairs={{0,16},{8,72},{16,32},{24,88},{32,48},{40,104},{48,0},{56,120},{64... | collective-permute-start | bytes 368648 | tf_op jit(solution)/shard_map/ppermute | solution.py:54
  5.5 6.6 %collective-permute-start.1 = (bf16[480,128]{1,0:T(8,128)(2,1)S(1)}, bf16[480,128]{1,0:T(8,128)(2,1)S(1)}, u32[]{:S(2)}, u32[]{:S(2)}) collective-permute-start(bf16[480,128]{1,0:T(8,128)(2,1)S(1)} %pad_maximum_fusion.11), channel_id=1, source_target_pairs={{0,32},{8,136},{16,48},{24,152},{32,0},{40,168},{48,16},{56,184},{... | collective-permute-start | bytes 368648 | tf_op jit(solution)/shard_map/ppermute | solution.py:54
  12.2 9.3 %collective-permute-start.3 = (bf16[4,480,128]{2,1,0:T(8,128)(2,1)S(1)}, bf16[4,480,128]{2,1,0:T(8,128)(2,1)S(1)}, u32[]{:S(2)}, u32[]{:S(2)}) collective-permute-start(bf16[4,480,128]{2,1,0:T(8,128)(2,1)S(1)} %get-tuple-element.65), channel_id=1, source_target_pairs={{0,64},{8,24},{16,80},{24,40},{32,96},{40,56},{48,112},{56,8},{64,... | collective-permute-start | bytes 1474568 | tf_op jit(solution)/shard_map/ppermute | solution.py:58
  13.2 14.5 %collective-permute-start.4 = (bf16[4,480,128]{2,1,0:T(8,128)(2,1)S(1)}, bf16[4,480,128]{2,1,0:T(8,128)(2,1)S(1)}, u32[]{:S(2)}, u32[]{:S(2)}) collective-permute-start(bf16[4,480,128]{2,1,0:T(8,128)(2,1)S(1)} %get-tuple-element.65), channel_id=1, source_target_pairs={{0,128},{8,40},{16,144},{24,56},{32,160},{40,8},{48,176},{56,24},{... | collective-permute-start | bytes 1474568 | tf_op jit(solution)/shard_map/ppermute | solution.py:58
  16.0 11.8 %collective-permute-start.5 = (bf16[4,480,128]{2,1,0:T(8,128)(2,1)S(1)}, bf16[4,480,128]{2,1,0:T(8,128)(2,1)S(1)}, u32[]{:S(2)}, u32[]{:S(2)}) collective-permute-start(bf16[4,480,128]{2,1,0:T(8,128)(2,1)S(1)} %get-tuple-element.65), channel_id=1, source_target_pairs={{0,192},{8,56},{16,208},{24,8},{32,224},{40,24},{48,240},{56,40},{... | collective-permute-start | bytes 1474568 | tf_op jit(solution)/shard_map/ppermute | solution.py:58
  29.7 6.6 %collective-permute-start.6 = (bf16[4,4,480,128]{3,2,0,1:T(8,128)(2,1)}, bf16[4,4,480,128]{3,2,0,1:T(8,128)(2,1)}, u32[]{:S(2)}, u32[]{:S(2)}) collective-permute-start(bf16[4,4,480,128]{3,2,0,1:T(8,128)(2,1)} %pad_maximum_fusion.2), channel_id=1, source_target_pairs={{0,8},{8,0},{1,9},{9,1},{2,10},{10,2},{3,11},{11,3},{4,12},{12,4},... | collective-permute-start | bytes 5898248 | tf_op jit(solution)/shard_map/ppermute | solution.py:62
  38.3 2.0 %copy-start = (bf16[512,3584]{1,0:T(8,128)(2,1)S(1)}, bf16[512,3584]{1,0:T(8,128)(2,1)}, u32[]{:S(2)}) copy-start(bf16[512,3584]{1,0:T(8,128)(2,1)} %param.9) | copy-start | bytes 11010052
  38.4 4.9 %slice-start = ((s8[8388608]{0:T(1024)(128)(4,1)}), s8[4194304]{0:T(1024)(128)(4,1)S(1)}, s32[]{:S(2)}) async-start(s8[8388608]{0:T(1024)(128)(4,1)} %bitcast.194), calls=%async_computation.2 | async-start | bytes 8388608
  38.5 4.8 %slice-start.1 = ((s8[8388608]{0:T(1024)(128)(4,1)}), s8[4194304]{0:T(1024)(128)(4,1)S(1)}, s32[]{:S(2)}) async-start(s8[8388608]{0:T(1024)(128)(4,1)} %bitcast.194), calls=%async_computation.3 | async-start | bytes 8388608
  41.6 10.8 %collective-permute-start.7 = (f32[4,32,512]{2,1,0:T(8,128)S(1)}, f32[4,32,512]{2,1,0:T(8,128)S(1)}, u32[]{:S(2)}, u32[]{:S(2)}) collective-permute-start(f32[4,32,512]{2,1,0:T(8,128)S(1)} %dynamic-slice_bitcast_fusion), channel_id=1, source_target_pairs={{0,1},{1,0},{2,3},{3,2},{4,5},{5,4},{6,7},{7,6},{8,9},{9,8},{10,11... | collective-permute-start | bytes 786440 | tf_op jit(solution)/shard_map/ppermute | solution.py:70
  46.2 6.1 %collective-permute-start.8 = (bf16[128,512]{1,0:T(8,128)(2,1)S(1)}, bf16[128,512]{1,0:T(8,128)(2,1)S(1)}, u32[]{:S(2)}, u32[]{:S(2)}) collective-permute-start(bf16[128,512]{1,0:T(8,128)(2,1)S(1)} %fusion.6), channel_id=1, source_target_pairs={{0,1},{1,0},{2,3},{3,2},{4,5},{5,4},{6,7},{7,6},{8,9},{9,8},{10,11... | collective-permute-start | bytes 393224 | tf_op jit(solution)/shard_map/ppermute | solution.py:70
  52.4 21.1 %slice-start.2 = ((s8[8388608]{0:T(1024)(128)(4,1)}), s8[4194304]{0:T(1024)(128)(4,1)S(1)}, s32[]{:S(2)}) async-start(s8[8388608]{0:T(1024)(128)(4,1)} %bitcast.196), calls=%async_computation.4 | async-start | bytes 8388608
  52.5 21.0 %slice-start.3 = ((s8[8388608]{0:T(1024)(128)(4,1)}), s8[4194304]{0:T(1024)(128)(4,1)S(1)}, s32[]{:S(2)}) async-start(s8[8388608]{0:T(1024)(128)(4,1)} %bitcast.196), calls=%async_computation.5 | async-start | bytes 8388608
  57.3 20.8 %collective-permute-start.9 = (f32[4,4,224,128]{3,2,1,0:T(8,128)}, f32[4,4,224,128]{3,2,1,0:T(8,128)}, u32[]{:S(2)}, u32[]{:S(2)}) collective-permute-start(f32[4,4,224,128]{3,2,1,0:T(8,128)} %get-tuple-element.42), channel_id=1, source_target_pairs={{0,8},{8,0},{1,9},{9,1},{2,10},{10,2},{3,11},{11,3},{4,12},{12,4},... | collective-permute-start | bytes 5505032 | tf_op jit(solution)/shard_map/ppermute | solution.py:62
  58.3 10.3 %collective-permute-start.10 = (f32[32,512]{1,0:T(8,128)S(1)}, f32[32,512]{1,0:T(8,128)S(1)}, u32[]{:S(2)}, u32[]{:S(2)}) collective-permute-start(f32[32,512]{1,0:T(8,128)S(1)} %get-tuple-element.29), channel_id=1, source_target_pairs={{0,2},{1,3},{2,4},{3,5},{4,6},{5,7},{6,0},{7,1},{8,10},{9,11},{10,... | collective-permute-start | bytes 196616 | tf_op jit(solution)/shard_map/ppermute | solution.py:66
  61.3 10.0 %collective-permute-start.11 = (f32[32,512]{1,0:T(8,128)S(1)}, f32[32,512]{1,0:T(8,128)S(1)}, u32[]{:S(2)}, u32[]{:S(2)}) collective-permute-start(f32[32,512]{1,0:T(8,128)S(1)} %get-tuple-element.30), channel_id=1, source_target_pairs={{0,4},{1,5},{2,6},{3,7},{4,0},{5,1},{6,2},{7,3},{8,12},{9,13},{10,... | collective-permute-start | bytes 196616 | tf_op jit(solution)/shard_map/ppermute | solution.py:66
  66.3 7.2 %collective-permute-start.12 = (f32[32,512]{1,0:T(8,128)S(1)}, f32[32,512]{1,0:T(8,128)S(1)}, u32[]{:S(2)}, u32[]{:S(2)}) collective-permute-start(f32[32,512]{1,0:T(8,128)S(1)} %get-tuple-element.31), channel_id=1, source_target_pairs={{0,6},{1,7},{2,0},{3,1},{4,2},{5,3},{6,4},{7,5},{8,14},{9,15},{10,... | collective-permute-start | bytes 196616 | tf_op jit(solution)/shard_map/ppermute | solution.py:66
  75.3 2.1 %collective-permute-start.13 = (f32[4,4,64,128]{3,2,1,0:T(8,128)S(1)}, f32[4,4,64,128]{3,2,1,0:T(8,128)S(1)}, u32[]{:S(2)}, u32[]{:S(2)}) collective-permute-start(f32[4,4,64,128]{3,2,1,0:T(8,128)S(1)} %get-tuple-element.56), channel_id=1, source_target_pairs={{0,8},{8,0},{1,9},{9,1},{2,10},{10,2},{3,11},{11,3},{4,12},{12,4},... | collective-permute-start | bytes 1572872 | tf_op jit(solution)/shard_map/ppermute | solution.py:62
  79.8 10.3 %collective-permute-start.14 = (f32[4,288,128]{2,1,0:T(8,128)S(1)}, f32[4,288,128]{2,1,0:T(8,128)S(1)}, u32[]{:S(2)}, u32[]{:S(2)}) collective-permute-start(f32[4,288,128]{2,1,0:T(8,128)S(1)} %pad_maximum_fusion.4), channel_id=1, source_target_pairs={{0,16},{8,72},{16,32},{24,88},{32,48},{40,104},{48,0},{56,120},{64... | collective-permute-start | bytes 1769480 | tf_op jit(solution)/shard_map/ppermute | solution.py:54
  81.3 15.7 %collective-permute-start.15 = (f32[4,288,128]{2,1,0:T(8,128)S(1)}, f32[4,288,128]{2,1,0:T(8,128)S(1)}, u32[]{:S(2)}, u32[]{:S(2)}) collective-permute-start(f32[4,288,128]{2,1,0:T(8,128)S(1)} %pad_maximum_fusion.5), channel_id=1, source_target_pairs={{0,32},{8,136},{16,48},{24,152},{32,0},{40,168},{48,16},{56,184},{... | collective-permute-start | bytes 1769480 | tf_op jit(solution)/shard_map/ppermute | solution.py:54
  83.2 14.1 %collective-permute-start.16 = (f32[4,288,128]{2,1,0:T(8,128)S(1)}, f32[4,288,128]{2,1,0:T(8,128)}, u32[]{:S(2)}, u32[]{:S(2)}) collective-permute-start(f32[4,288,128]{2,1,0:T(8,128)S(1)} %pad_maximum_fusion.6), channel_id=1, source_target_pairs={{0,48},{8,200},{16,0},{24,216},{32,16},{40,232},{48,32},{56,248},{... | collective-permute-start | bytes 1769480 | tf_op jit(solution)/shard_map/ppermute | solution.py:54
  98.5 36.4 %copy-start.3 = (f32[8,3584]{1,0:T(8,128)S(1)}, f32[8,3584]{1,0:T(8,128)}, u32[]{:S(2)}) copy-start(f32[8,3584]{1,0:T(8,128)} %param.12) | copy-start | bytes 344068
  98.5 36.4 %copy-start.6 = (f32[8,3584]{1,0:T(8,128)S(1)}, f32[8,3584]{1,0:T(8,128)}, u32[]{:S(2)}) copy-start(f32[8,3584]{1,0:T(8,128)} %param.14) | copy-start | bytes 344068
  98.5 36.4 %copy-start.7 = (f32[8,3584]{1,0:T(8,128)S(1)}, f32[8,3584]{1,0:T(8,128)}, u32[]{:S(2)}) copy-start(f32[8,3584]{1,0:T(8,128)} %param.13) | copy-start | bytes 344068
  98.6 5.3 %collective-permute-start.17 = (f32[288,128]{1,0:T(8,128)S(1)}, f32[288,128]{1,0:T(8,128)S(1)}, u32[]{:S(2)}, u32[]{:S(2)}) collective-permute-start(f32[288,128]{1,0:T(8,128)S(1)} %get-tuple-element.61), channel_id=1, source_target_pairs={{0,64},{8,24},{16,80},{24,40},{32,96},{40,56},{48,112},{56,8},{64,... | collective-permute-start | bytes 442376 | tf_op jit(solution)/shard_map/ppermute | solution.py:58
  98.7 7.2 %collective-permute-start.18 = (f32[288,128]{1,0:T(8,128)S(1)}, f32[288,128]{1,0:T(8,128)S(1)}, u32[]{:S(2)}, u32[]{:S(2)}) collective-permute-start(f32[288,128]{1,0:T(8,128)S(1)} %get-tuple-element.63), channel_id=1, source_target_pairs={{0,128},{8,40},{16,144},{24,56},{32,160},{40,8},{48,176},{56,24},{... | collective-permute-start | bytes 442376 | tf_op jit(solution)/shard_map/ppermute | solution.py:58
  101.8 4.4 %collective-permute-start.19 = (f32[288,128]{1,0:T(8,128)S(1)}, f32[288,128]{1,0:T(8,128)S(1)}, u32[]{:S(2)}, u32[]{:S(2)}) collective-permute-start(f32[288,128]{1,0:T(8,128)S(1)} %get-tuple-element.62), channel_id=1, source_target_pairs={{0,192},{8,56},{16,208},{24,8},{32,224},{40,24},{48,240},{56,40},{... | collective-permute-start | bytes 442376 | tf_op jit(solution)/shard_map/ppermute | solution.py:58
  107.0 26.5 %all-to-all-start = ((f32[256,1,128]{2,1,0:T(1,128)}), f32[256,1,128]{2,1,0:T(1,128)S(1)}, u32[]{:S(2)}, u32[]{:S(2)}) async-start(f32[256,1,128]{2,1,0:T(1,128)} %broadcast_in_dim.6), calls=%async_computation | async-start | bytes 262144 | tf_op jit(solution)/shard_map/all_to_all | solution.py:182
  120.4 36.1 %copy-start.2 = (f32[256,256]{1,0:T(8,128)S(1)}, f32[256,256]{1,0:T(8,128)}, u32[]{:S(2)}) copy-start(f32[256,256]{1,0:T(8,128)} %param.15) | copy-start | bytes 786436
  120.4 3.9 %collective-permute-start.20 = (f32[64,128]{1,0:T(8,128)S(1)}, f32[64,128]{1,0:T(8,128)S(1)}, u32[]{:S(2)}, u32[]{:S(2)}) collective-permute-start(f32[64,128]{1,0:T(8,128)S(1)} %get-tuple-element.82), channel_id=1, source_target_pairs={{0,1},{1,0},{2,3},{3,2},{4,5},{5,4},{6,7},{7,6},{8,9},{9,8},{10,11... | collective-permute-start | bytes 98312 | tf_op jit(solution)/shard_map/ppermute | solution.py:70
  134.9 21.8 %copy-start.4 = (f32[256,256]{1,0:T(8,128)S(1)}, f32[256,256]{1,0:T(8,128)}, u32[]{:S(2)}) copy-start(f32[256,256]{1,0:T(8,128)} %param.16) | copy-start | bytes 786436
  135.0 21.8 %copy-start.5 = (f32[256,256]{1,0:T(8,128)S(1)}, f32[256,256]{1,0:T(8,128)}, u32[]{:S(2)}) copy-start(f32[256,256]{1,0:T(8,128)} %param.17) | copy-start | bytes 786436
  136.0 18.5 %all-to-all-start.1 = ((bf16[16,224,128]{2,1,0:T(8,128)(2,1)}), bf16[16,224,128]{2,1,0:T(8,128)(2,1)S(1)}, u32[]{:S(2)}, u32[]{:S(2)}) async-start(bf16[16,224,128]{2,1,0:T(8,128)(2,1)} %broadcast_in_dim.7), calls=%async_computation.1 | async-start | bytes 1835008 | tf_op jit(solution)/shard_map/all_to_all | solution.py:198
  139.7 5.6 %collective-permute-start.21 = (f32[128,128]{1,0:T(8,128)S(1)}, f32[128,128]{1,0:T(8,128)S(1)}, u32[]{:S(2)}, u32[]{:S(2)}) collective-permute-start(f32[128,128]{1,0:T(8,128)S(1)} %pad_maximum_fusion.12), channel_id=1, source_target_pairs={{0,2},{1,3},{2,4},{3,5},{4,6},{5,7},{6,0},{7,1},{8,10},{9,11},{10,... | collective-permute-start | bytes 196616 | tf_op jit(solution)/shard_map/ppermute | solution.py:66
  140.4 7.3 %collective-permute-start.22 = (f32[128,128]{1,0:T(8,128)S(1)}, f32[128,128]{1,0:T(8,128)S(1)}, u32[]{:S(2)}, u32[]{:S(2)}) collective-permute-start(f32[128,128]{1,0:T(8,128)S(1)} %pad_maximum_fusion.12), channel_id=1, source_target_pairs={{0,4},{1,5},{2,6},{3,7},{4,0},{5,1},{6,2},{7,3},{8,12},{9,13},{10,... | collective-permute-start | bytes 196616 | tf_op jit(solution)/shard_map/ppermute | solution.py:66
  142.1 8.3 %collective-permute-start.23 = (f32[128,128]{1,0:T(8,128)S(1)}, f32[128,128]{1,0:T(8,128)S(1)}, u32[]{:S(2)}, u32[]{:S(2)}) collective-permute-start(f32[128,128]{1,0:T(8,128)S(1)} %pad_maximum_fusion.12), channel_id=1, source_target_pairs={{0,6},{1,7},{2,0},{3,1},{4,2},{5,3},{6,4},{7,5},{8,14},{9,15},{10,... | collective-permute-start | bytes 196616 | tf_op jit(solution)/shard_map/ppermute | solution.py:66
  154.6 4.1 %collective-permute-start.24 = (bf16[16,224,128]{2,1,0:T(8,128)(2,1)S(1)}, bf16[16,224,128]{2,1,0:T(8,128)(2,1)S(1)}, u32[]{:S(2)}, u32[]{:S(2)}) collective-permute-start(bf16[16,224,128]{2,1,0:T(8,128)(2,1)S(1)} %all-to-all-done.1), channel_id=1, source_target_pairs={{0,8},{8,0},{1,9},{9,1},{2,10},{10,2},{3,11},{11,3},{4,12},{12,4},... | collective-permute-start | bytes 2752520 | tf_op jit(solution)/shard_map/ppermute | solution.py:62
  158.7 1.5 copy-start.1
where the time goes:
time: 163 us; the launch traced here: 162 us
  waiting for transfers between devices  70.4 us (43%)
  starting transfers between devices  60.6 us (37%)
  other arithmetic  11.4 us (7%)
  matrix products  11 us (7%)
  local copies, waits for them, and re-layouts  7.81 us (5%)
    ppermute x6, waiting for transfers between devices, shift_p(): return lax.ppermute(v, DP, plane_pairs(True, k))  16.5 us
    ppermute x6, waiting for transfers between devices, shift_q(): return lax.ppermute(v, DP, plane_pairs(False, k))  15.3 us
    ppermute x6, starting transfers between devices, shift_z(): return lax.ppermute(v, 'z', [(i, (i + k) % 8) for i in range(8)])  14.7 us
    all_to_all x1, starting transfers between devices, local(): lax.all_to_all(jnp.broadcast_to(squares, (256, 128)), ('y', 'x', 'core',...  13.4 us
    ppermute x6, waiting for transfers between devices, shift_z(): return lax.ppermute(v, 'z', [(i, (i + k) % 8) for i in range(8)])  11.1 us
    ppermute x6, starting transfers between devices, shift_p(): return lax.ppermute(v, DP, plane_pairs(True, k))  10.2 us
    all_to_all x1, waiting for transfers between devices, local(): lax.all_to_all(jnp.broadcast_to(squares, (256, 128)), ('y', 'x', 'core',...  9.1 us
    ppermute x6, starting transfers between devices, shift_q(): return lax.ppermute(v, DP, plane_pairs(False, k))  7.78 us
  transfers between devices with their start and end apart: 27, of which 21 were waited for; matrix products, arithmetic and copies ran while one was open for 4% of the time, Pallas kernels for 0%

commit v1 on v0

v1 whole, which is shorter than its diff:
```python
import math

import jax
import jax.numpy as jnp
import numpy as np
from jax import lax
from jax.sharding import Mesh
from jax.sharding import PartitionSpec as P

HIDDEN_UNITS = 28672
FACTOR_RANK = 256
STEP = 5000

first_decay = 0.9
second_decay = 0.999
adam_epsilon = 1e-08
learn_rate = 0.05
clip_limit = 1.0
norm_epsilon = 1e-06

bf16 = jnp.bfloat16
f32 = jnp.float32
DP = ("y", "x", "core")


def moment_update_step(param, first, second, grad):
    first_new = first_decay * first + (1.0 - first_decay) * grad
    second_new = second_decay * second + (1.0 - second_decay) * grad * grad
    first_fix = 1.0 - first_decay**STEP
    second_fix = 1.0 - second_decay**STEP
    return param - learn_rate * (first_new / first_fix) / (
        jnp.sqrt(second_new / second_fix) + adam_epsilon
    )


def dp_index(y, x, c):
    return (y * 4 + x) * 2 + c


def plane_pairs(first, k):
    pairs = []
    for y in range(4):
        for x in range(4):
            for c in range(2):
                if (c == 0) == first:
                    target = dp_index(y, (x + k) % 4, c)
                else:
                    target = dp_index((y + k) % 4, x, c)
                pairs.append((dp_index(y, x, c), target))
    return pairs


def shift_p(v, k):
    return lax.ppermute(v, DP, plane_pairs(True, k))


def shift_q(v, k):
    return lax.ppermute(v, DP, plane_pairs(False, k))


def swap_core(v):
    return lax.ppermute(v, "core", [(0, 1), (1, 0)])


def shift_z(v, k):
    return lax.ppermute(v, "z", [(i, (i + k) % 8) for i in range(8)])


def flip(v, axis, n, bit):
    return lax.ppermute(v, axis, [(i, i ^ bit) for i in range(n)])


def swap_pairs(v):
    return lax.ppermute(v, "z", [(i, (i + 1) % 8 if i % 2 else (i - 1) % 8) for i in range(8)])


def pick(stack, index):
    return lax.dynamic_index_in_dim(stack, index, 0, keepdims=False)


def ahead(stack, index):
    return jnp.stack([pick(stack, (index + k) % 4) for k in range(4)])


def tiles(v):
    rows, columns = v.shape
    return v.reshape(rows // 8, 8, columns // 128, 128).swapaxes(1, 2).reshape(-1, 128)


def untile(v, rows, columns):
    count = v.shape[0]
    v = v.reshape(count, rows // 8, columns // 128, 8, 128).swapaxes(2, 3)
    return v.reshape(count, rows, columns)


def by_offset(stack, index):
    return jnp.stack([pick(stack, (index - j) % 4) for j in range(4)])


def join_cores(mine, other, core):
    zero = jnp.where(core == 0, mine, other)
    one = jnp.where(core == 0, other, mine)
    return jnp.stack([zero, one.swapaxes(0, 1)], axis=2)


def split_cores(terms, core):
    zero = terms[:, :, 0].swapaxes(0, 1)
    one = terms[:, :, 1]
    return jnp.where(core == 0, zero, one), jnp.where(core == 0, one, zero)


def split_ahead(terms, y, x, core):
    zero = ahead(ahead(terms[:, :, 0], y).swapaxes(0, 1), x)
    one = ahead(ahead(terms[:, :, 1], y).swapaxes(0, 1), x).swapaxes(0, 1)
    return jnp.where(core == 0, zero, one), jnp.where(core == 0, one, zero)


def join_ranks(v, other, z, bit):
    low = (z & bit) == 0
    return jnp.concatenate([jnp.where(low, v, other), jnp.where(low, other, v)], axis=0)


def local(
    input_token_rows,
    output_gradient_rows,
    frozen_base_matrix,
    left_lowrank_factor,
    left_first_moment,
    left_second_moment,
    right_lowrank_factor,
    right_first_moment,
    right_second_moment,
):
    hidden_scale = 1.0 / math.sqrt(HIDDEN_UNITS)
    rank_scale = 1.0 / math.sqrt(FACTOR_RANK)
    y, x, core, z = (lax.axis_index(n) for n in ("y", "x", "core", "z"))
    p = jnp.where(core == 0, x, y)
    q = jnp.where(core == 0, y, x)

    b_block = lax.dynamic_slice_in_dim(right_lowrank_factor, (z % 2) * 128, 128, 1)
    block = jnp.concatenate([tiles(left_lowrank_factor), b_block], axis=0).astype(bf16)
    with jax.named_scope("factors_p"):
        stack = jnp.stack([block] + [shift_p(block, k) for k in (1, 2, 3)])
        a_stack = by_offset(stack[:, :224], p)
        b_stack = by_offset(stack[:, 224:], p)
        tokens, grads, base = input_token_rows, output_gradient_rows, frozen_base_matrix
        a_stack, b_stack = lax.optimization_barrier((a_stack, b_stack))
    with jax.named_scope("a_q"):
        a_stack = jnp.stack([a_stack] + [shift_q(a_stack, k) for k in (1, 2, 3)])
    a_stack, b_stack = lax.optimization_barrier((a_stack, b_stack))
    with jax.named_scope("a_cores"):
        a_stack = by_offset(a_stack, q)
        a_other = swap_core(a_stack)
    with jax.named_scope("b_q"):
        b_stack = jnp.stack([b_stack] + [shift_q(b_stack, k) for k in (1, 2, 3)])
    with jax.named_scope("act_terms"):
        a_rows = join_cores(a_stack, a_other, core).reshape(32, 224, 128)
        a_rows = untile(a_rows, 8, 3584).reshape(256, 3584)
        act_part = lax.dot_general(
            a_rows, tokens, (((1,), (1,)), ((), ())), preferred_element_type=f32
        ).reshape(4, 2, 32, 512)
        act_send = lax.dynamic_index_in_dim(act_part, 1 - z % 2, 1, keepdims=False)
        act_keep = lax.dynamic_index_in_dim(act_part, z % 2, 1, keepdims=False)
    with jax.named_scope("act_pairs"):
        act_got = flip(act_send, "z", 8, 1)
    act_got, b_stack = lax.optimization_barrier((act_got, b_stack))
    with jax.named_scope("act_shifts"):
        act_pair = act_keep + act_got
        act_pieces = [pick(act_pair, (z // 2 + k) % 4) for k in range(4)]
        act_gots = [shift_z(act_pieces[k], 2 * k) for k in range(1, 4)]
    with jax.named_scope("b_cores"):
        b_stack = by_offset(b_stack, q)
        b_rows = join_cores(b_stack, swap_core(b_stack), core).reshape(8192, 128)
    with jax.named_scope("back"):
        back_part = (
            jnp.dot(grads, b_rows, preferred_element_type=f32) * rank_scale
        ).astype(bf16).T
    back_part, act_gots = lax.optimization_barrier((back_part, act_gots))
    with jax.named_scope("back_pairs"):
        back = join_ranks(back_part, swap_pairs(back_part), z, 1)
        keep_rows, send_rows = split_ahead(back.reshape(4, 4, 2, 8, 512), y, x, core)
    with jax.named_scope("grad_b_terms"):
        act = act_pieces[0] + act_gots[0] + act_gots[1] + act_gots[2]
        act = lax.optimization_barrier((act * hidden_scale).astype(bf16))
        b_term = jnp.dot(act, grads, preferred_element_type=f32)
    keep_rows, send_rows, b_term = lax.optimization_barrier((keep_rows, send_rows, b_term))
    with jax.named_scope("grad_a_cores"):
        a_send = jnp.dot(
            send_rows.reshape(128, 512), tokens, preferred_element_type=f32
        )
        a_got = swap_core(a_send)
    with jax.named_scope("grad_a_terms"):
        a_keep = jnp.dot(
            keep_rows.reshape(128, 512), tokens, preferred_element_type=f32
        )
        a_keep = lax.optimization_barrier(a_keep)
    with jax.named_scope("grad_b_split"):
        b_term = b_term.reshape(4, 8, 4, 4, 2, 2, 128).transpose(2, 3, 4, 0, 5, 1, 6)
        b_keep, b_send = split_cores(b_term.reshape(4, 4, 2, 64, 128), core)
    with jax.named_scope("grad_b_cores"):
        b_got = swap_core(b_send)
    parts = []
    for k in range(4):
        a_part = a_keep[32 * k : 32 * k + 32] + a_got[32 * k : 32 * k + 32]
        a_part = a_part.reshape(4, 8, 28, 128).swapaxes(1, 2).reshape(4, 224, 128)
        b_part = ahead(pick(b_keep, (p + k) % 4) + pick(b_got, (p + k) % 4), q)
        parts.append(jnp.concatenate([a_part, b_part], axis=1))
    with jax.named_scope("grads_p"):
        total = parts[0]
        for k in (1, 2, 3):
            total = total + shift_p(parts[k], k)
    with jax.named_scope("grads_q"):
        parts = [total[k] for k in range(4)]
        total = parts[0]
        for k in (1, 2, 3):
            total = total + shift_q(parts[k], k)
    grad_a = total[:224] * hidden_scale
    grad_b = total[224:] * rank_scale

    squares = jnp.sum(grad_a * grad_a, axis=0) + jnp.sum(grad_b * grad_b, axis=0)
    squares = lax.all_to_all(
        jnp.broadcast_to(squares, (256, 128)), ("y", "x", "core", "z"), 0, 0, tiled=True
    )
    pair = flip(grad_b, "z", 8, 4)
    right_t = (right_lowrank_factor.T, right_first_moment.T, right_second_moment.T)
    squares, pair, right_t = lax.optimization_barrier((squares, pair, right_t))
    pair = join_ranks(grad_b, pair, z, 4)
    squares = jnp.sum(squares, keepdims=True)
    clipper = jnp.minimum(1.0, clip_limit / (jnp.sqrt(squares) + norm_epsilon))

    new_a = moment_update_step(
        tiles(left_lowrank_factor),
        tiles(left_first_moment),
        tiles(left_second_moment),
        clipper * grad_a,
    ).astype(bf16)
    copies = jnp.broadcast_to(new_a, (16, 224, 128))
    copies, pair = lax.optimization_barrier((copies, pair))
    mine = lax.all_to_all(copies, ("y", "x"), 0, 0, tiled=True)
    pairs = [pair, shift_z(pair, 1), shift_z(pair, 2), shift_z(pair, -1)]
    mine, pairs = lax.optimization_barrier((mine, pairs))
    other = swap_core(mine)
    whole_grad_b = by_offset(jnp.stack(pairs), z % 4).reshape(4, 2, 64, 128).swapaxes(0, 1)
    whole_grad_b = untile(whole_grad_b.reshape(8, 64, 128), 32, 256).reshape(256, 256)
    new_b = moment_update_step(
        *right_t, clipper * whole_grad_b
    ).astype(bf16)
    fresh = jnp.stack([jnp.where(core == 0, mine, other), jnp.where(core == 0, other, mine)], axis=1)
    new_a = untile(fresh.reshape(32, 224, 128), 8, 3584).reshape(256, 3584)
    product = lax.dot_general(new_b, new_a, (((0,), (0,)), ((), ())), preferred_element_type=f32)
    return (base.astype(f32) + product * rank_scale).astype(bf16)


def solution(mesh):
    grid = Mesh(np.asarray(mesh.devices).reshape(4, 4, 2, 8), ("y", "x", "core", "z"))
    split = P(DP, "z")
    rows = P(DP, None)
    return jax.shard_map(
        local,
        mesh=grid,
        in_specs=(split, rows, split, split, split, split, rows, rows, rows),
        out_specs=split,
        check_vma=False,
    )
```

time: 163 us -> 152 us (0.933)
  waiting for transfers between devices: 70.4 us -> 63 us
  other arithmetic: 11.4 us -> 7.15 us
  local copies, waits for them, and re-layouts: 7.81 us -> 9.89 us
    ppermute x6, waiting for transfers between devices: 11.1 us -> 3.95 us  [shift_z(): return lax.ppermute(v, 'z', [(i, (i + k) % 8) for i in range(8)])]
    all_to_all x1, starting transfers between devices: 13.4 us -> 8.07 us  [local(): lax.all_to_all(jnp.broadcast_to(squares, (256, 128)), ('y', 'x', 'core',...]
    all_to_all x1, waiting for transfers between devices: 9.1 us -> 4.27 us  [local(): lax.all_to_all(jnp.broadcast_to(squares, (256, 128)), ('y', 'x', 'core',...]
    ppermute x3 -> x2, starting transfers between devices: 4.64 us -> 8.05 us  [flip(): return lax.ppermute(v, axis, [(i, i ^ bit) for i in range(n)])]
    ppermute x4 -> x5, waiting for transfers between devices: 7.03 us -> 3.66 us  [swap_core(): return lax.ppermute(v, 'core', [(0, 1), (1, 0)])]
    all_to_all x1, waiting for transfers between devices: 4.2 us -> 7.43 us  [local(): mine = lax.all_to_all(copies, ('y', 'x'), 0, 0, tiled=True)]
    ppermute x6, waiting for transfers between devices: 16.5 us -> 19.5 us  [shift_p(): return lax.ppermute(v, DP, plane_pairs(True, k))]
    ppermute x6, starting transfers between devices: 10.2 us -> 7.32 us  [shift_p(): return lax.ppermute(v, DP, plane_pairs(True, k))]
  transfers between devices with their start and end apart: 27 -> 31, of which waited for: 21 -> 24; matrix products, arithmetic and copies ran while one was open for 4% -> 8% of each run, Pallas kernels for 0% -> 0%
where the time goes in v1:
time: 152 us
  waiting for transfers between devices  63 us (41%)
  starting transfers between devices  59.1 us (39%)
  matrix products  11 us (7%)
  local copies, waits for them, and re-layouts  9.89 us (7%)
  other arithmetic  7.15 us (5%)
    ppermute x6, waiting for transfers between devices, shift_p(): return lax.ppermute(v, DP, plane_pairs(True, k))  19.5 us
    ppermute x9, waiting for transfers between devices, shift_q(): return lax.ppermute(v, DP, plane_pairs(False, k))  16.2 us
    ppermute x6, starting transfers between devices, shift_z(): return lax.ppermute(v, 'z', [(i, (i + k) % 8) for i in range(8)])  13.9 us
    ppermute x5, starting transfers between devices, swap_core(): return lax.ppermute(v, 'core', [(0, 1), (1, 0)])  8.81 us
    ppermute x9, starting transfers between devices, shift_q(): return lax.ppermute(v, DP, plane_pairs(False, k))  8.45 us
    all_to_all x1, starting transfers between devices, local(): lax.all_to_all(jnp.broadcast_to(squares, (256, 128)), ('y', 'x', 'core',...  8.07 us
    ppermute x2, starting transfers between devices, flip(): return lax.ppermute(v, axis, [(i, i ^ bit) for i in range(n)])  8.05 us
    all_to_all x1, waiting for transfers between devices, local(): mine = lax.all_to_all(copies, ('y', 'x'), 0, 0, tiled=True)  7.43 us
  transfers between devices with their start and end apart: 31, of which 24 were waited for; matrix products, arithmetic and copies ran while one was open for 8% of the time, Pallas kernels for 0%

profile of v1, /device:TPU:1, one launch (start us, length us, event | category | flops | bytes accessed | tf_op | source)
XLA Modules:
  0.0 151.6 jit_solution(10336998659922646408)
XLA Ops:
  0.0 0.9 fusion.44
  0.9 0.9 dynamic-slice_convert_fusion
  1.9 3.6 %collective-permute-start.2 = (bf16[480,128]{1,0:T(8,128)(2,1)S(1)}, bf16[480,128]{1,0:T(8,128)(2,1)S(1)}, u32[]{:S(2)}, u32[]{:S(2)}) collective-permute-start(bf16[480,128]{1,0:T(8,128)(2,1)S(1)} %pad_maximum_fusion.19), channel_id=1, source_target_pairs={{0,48},{8,200},{16,0},{24,216},{32,16},{40,232},{48,32},{56,248},{... | collective-permute-start | bytes 368648 | tf_op jit(solution)/shard_map/factors_p/ppermute | solution.py:54
  5.8 0.7 collective-permute-start
  6.5 0.9 fusion.66
  7.4 1.2 collective-permute-done.2
  8.6 2.4 %collective-permute-done.1 = bf16[480,128]{1,0:T(8,128)(2,1)S(1)} collective-permute-done((bf16[480,128]{1,0:T(8,128)(2,1)S(1)}, bf16[480,128]{1,0:T(8,128)(2,1)S(1)}, u32[]{:S(2)}, u32[]{:S(2)}) %collective-permute-start.1) | collective-permute-done | bytes 122912 | tf_op jit(solution)/shard_map/factors_p/ppermute | solution.py:54
  11.0 1.3 collective-permute-done
  12.6 2.3 %collective-permute-start.5 = (bf16[4,224,128]{2,1,0:T(8,128)(2,1)S(1)}, bf16[4,224,128]{2,1,0:T(8,128)(2,1)S(1)}, u32[]{:S(2)}, u32[]{:S(2)}) collective-permute-start(bf16[4,224,128]{2,1,0:T(8,128)(2,1)S(1)} %pad_maximum_fusion.15), channel_id=1, source_target_pairs={{0,192},{8,56},{16,208},{24,8},{32,224},{40,24},{48,240},{56,40},{... | collective-permute-start | bytes 688136 | tf_op jit(solution)/shard_map/a_q/ppermute | solution.py:58
  14.8 0.5 collective-permute-start.4
  15.3 0.6 collective-permute-start.3
  15.9 4.3 %collective-permute-done.5 = bf16[4,224,128]{2,1,0:T(8,128)(2,1)S(1)} collective-permute-done((bf16[4,224,128]{2,1,0:T(8,128)(2,1)S(1)}, bf16[4,224,128]{2,1,0:T(8,128)(2,1)S(1)}, u32[]{:S(2)}, u32[]{:S(2)}) %collective-permute-start.5) | collective-permute-done | bytes 229408 | tf_op jit(solution)/shard_map/a_q/ppermute | solution.py:58
  20.2 1.1 collective-permute-done.4
  21.3 2.6 %collective-permute-done.3 = bf16[4,224,128]{2,1,0:T(8,128)(2,1)S(1)} collective-permute-done((bf16[4,224,128]{2,1,0:T(8,128)(2,1)S(1)}, bf16[4,224,128]{2,1,0:T(8,128)(2,1)S(1)}, u32[]{:S(2)}, u32[]{:S(2)}) %collective-permute-start.3) | collective-permute-done | bytes 229408 | tf_op jit(solution)/shard_map/a_q/ppermute | solution.py:58
  24.3 3.3 %collective-permute-start.6 = (bf16[4,4,224,128]{3,2,0,1:T(8,128)(2,1)S(1)}, bf16[4,4,224,128]{3,2,0,1:T(8,128)(2,1)S(1)}, u32[]{:S(2)}, u32[]{:S(2)}) collective-permute-start(bf16[4,4,224,128]{3,2,0,1:T(8,128)(2,1)S(1)} %pad_maximum_fusion.6), channel_id=1, source_target_pairs={{0,8},{8,0},{1,9},{9,1},{2,10},{10,2},{3,11},{11,3},{4,12},{12,4},... | collective-permute-start | bytes 2752520 | tf_op jit(solution)/shard_map/a_cores/ppermute | solution.py:62
  28.4 0.7 collective-permute-start.8
  29.1 0.6 collective-permute-done.6
  30.1 1.8 %copy-done = bf16[512,3584]{1,0:T(8,128)(2,1)S(1)} copy-done((bf16[512,3584]{1,0:T(8,128)(2,1)S(1)}, bf16[512,3584]{1,0:T(8,128)(2,1)}, u32[]{:S(2)}) %copy-start) | copy-done | bytes 3670040
  31.9 1.1 fusion.2
  33.1 1.7 %collective-permute-start.7 = (f32[4,32,512]{2,1,0:T(8,128)S(1)}, f32[4,32,512]{2,1,0:T(8,128)S(1)}, u32[]{:S(2)}, u32[]{:S(2)}) collective-permute-start(f32[4,32,512]{2,1,0:T(8,128)S(1)} %dynamic-slice_bitcast_fusion), channel_id=1, source_target_pairs={{0,1},{1,0},{2,3},{3,2},{4,5},{5,4},{6,7},{7,6},{8,9},{9,8},{10,11... | collective-permute-start | bytes 786440 | tf_op jit(solution)/shard_map/act_pairs/ppermute | solution.py:70
  34.9 2.8 %collective-permute-done.8 = bf16[4,256,128]{2,1,0:T(8,128)(2,1)S(1)} collective-permute-done((bf16[4,256,128]{2,1,0:T(8,128)(2,1)S(1)}, bf16[4,256,128]{2,1,0:T(8,128)(2,1)S(1)}, u32[]{:S(2)}, u32[]{:S(2)}) %collective-permute-start.8) | collective-permute-done | bytes 262176 | tf_op jit(solution)/shard_map/b_q/ppermute | solution.py:58
  37.8 3.2 %collective-permute-done.7 = f32[4,32,512]{2,1,0:T(8,128)S(1)} collective-permute-done((f32[4,32,512]{2,1,0:T(8,128)S(1)}, f32[4,32,512]{2,1,0:T(8,128)S(1)}, u32[]{:S(2)}, u32[]{:S(2)}) %collective-permute-start.7) | collective-permute-done | bytes 262176 | tf_op jit(solution)/shard_map/act_pairs/ppermute | solution.py:70
  41.4 1.1 collective-permute-start.11
  42.5 1.1 bitcast_add_fusion
  43.7 3.1 %collective-permute-start.12 = (f32[32,512]{1,0:T(8,128)S(1)}, f32[32,512]{1,0:T(8,128)S(1)}, u32[]{:S(2)}, u32[]{:S(2)}) collective-permute-start(f32[32,512]{1,0:T(8,128)S(1)} %get-tuple-element.92), channel_id=1, source_target_pairs={{0,2},{1,3},{2,4},{3,5},{4,6},{5,7},{6,0},{7,1},{8,10},{9,11},{10,... | collective-permute-start | bytes 196616 | tf_op jit(solution)/shard_map/act_shifts/ppermute | solution.py:66
  46.7 4.9 %collective-permute-start.13 = (f32[32,512]{1,0:T(8,128)S(1)}, f32[32,512]{1,0:T(8,128)S(1)}, u32[]{:S(2)}, u32[]{:S(2)}) collective-permute-start(f32[32,512]{1,0:T(8,128)S(1)} %get-tuple-element.91), channel_id=1, source_target_pairs={{0,4},{1,5},{2,6},{3,7},{4,0},{5,1},{6,2},{7,3},{8,12},{9,13},{10,... | collective-permute-start | bytes 196616 | tf_op jit(solution)/shard_map/act_shifts/ppermute | solution.py:66
  51.7 2.4 %collective-permute-start.14 = (f32[32,512]{1,0:T(8,128)S(1)}, f32[32,512]{1,0:T(8,128)S(1)}, u32[]{:S(2)}, u32[]{:S(2)}) collective-permute-start(f32[32,512]{1,0:T(8,128)S(1)} %get-tuple-element.90), channel_id=1, source_target_pairs={{0,6},{1,7},{2,0},{3,1},{4,2},{5,3},{6,4},{7,5},{8,14},{9,15},{10,... | collective-permute-start | bytes 196616 | tf_op jit(solution)/shard_map/act_shifts/ppermute | solution.py:66
  54.9 1.8 %slice-done.1 = s8[4194304]{0:T(1024)(128)(4,1)S(1)} async-done(((s8[8388608]{0:T(1024)(128)(4,1)}), s8[4194304]{0:T(1024)(128)(4,1)S(1)}, s32[]{:S(2)}) %slice-start.1) | async-done | bytes 4194328
  56.8 2.9 %fusion.4 = bf16[128,512]{1,0:T(8,128)(2,1)S(1)} fusion(bf16[8192,128]{1,0:T(8,128)(2,1)S(1)} %bitcast.264, bf16[512,8192]{1,0:T(8,128)(2,1)S(1)} %bitcast.263), kind=kOutput, calls=%fused_computation.9 | convolution fusion | flops 1073872896 | bytes 10616832 | tf_op jit(solution)/shard_map/back/dot_general | solution.py:176
  59.7 0.8 collective-permute-start.15
  60.6 1.5 %fusion.53 = f32[32,8192]{1,0:T(8,128)S(1)} fusion(bf16[32,512]{1,0:T(8,128)(2,1)S(1)} %fusion.43, bf16[512,8192]{1,0:T(8,128)(2,1)S(1)} %bitcast.263), kind=kOutput, calls=%fused_computation.174 | convolution fusion | flops 268435456 | bytes 9469952 | tf_op jit(solution)/shard_map/grad_b_terms/dot_general | solution.py:185
  62.1 2.7 %collective-permute-done.15 = bf16[128,512]{1,0:T(8,128)(2,1)S(1)} collective-permute-done((bf16[128,512]{1,0:T(8,128)(2,1)S(1)}, bf16[128,512]{1,0:T(8,128)(2,1)S(1)}, u32[]{:S(2)}, u32[]{:S(2)}) %collective-permute-start.15) | collective-permute-done | bytes 131104 | tf_op jit(solution)/shard_map/back_pairs/ppermute | solution.py:74
  65.1 0.6 fusion.55
  65.8 2.3 %collective-permute-start.16 = (f32[128,3584]{1,0:T(8,128)S(1)}, f32[128,3584]{1,0:T(8,128)}, u32[]{:S(2)}, u32[]{:S(2)}) collective-permute-start(f32[128,3584]{1,0:T(8,128)S(1)} %fusion.55), channel_id=1, source_target_pairs={{0,8},{8,0},{1,9},{9,1},{2,10},{10,2},{3,11},{11,3},{4,12},{12,4},... | collective-permute-start | bytes 5505032 | tf_op jit(solution)/shard_map/grad_a_cores/ppermute | solution.py:62
  68.5 2.7 %fusion.54 = f32[128,3584]{1,0:T(8,128)S(1)} fusion(bf16[128,512]{1,0:T(8,128)(2,1)S(1)} %bitcast.277, bf16[512,3584]{1,0:T(8,128)(2,1)} %param.9), kind=kOutput, calls=%fused_computation.175 | convolution fusion | flops 469762048 | bytes 5636096 | tf_op jit(solution)/shard_map/grad_a_terms/dot_general | solution.py:193
  71.2 1.0 collective-permute-done.17
  72.4 1.7 %fusion.13 = (f32[4,224,128]{2,1,0:T(8,128)S(1)}, f32[4,224,128]{2,1,0:T(8,128)S(1)}, f32[4,224,128]{2,1,0:T(8,128)S(1)}, f32[4,224,128]{2,1,0:T(8,128)S(1)}) fusion(f32[128,3584]{1,0:T(8,128)} %collective-permute-done.16, f32[128,3584]{1,0:T(8,128)S(1)} %fusion.54), kind=kLoop, calls=%fused_computation.38 | loop fusion | flops 458752 | bytes 5505024 | tf_op jit(solution)/shard_map/reshape | solution.py:205
  74.6 1.3 collective-permute-start.19
  76.0 0.9 collective-permute-start.18
  76.9 6.4 %collective-permute-done.20 = f32[4,288,128]{2,1,0:T(8,128)S(1)} collective-permute-done((f32[4,288,128]{2,1,0:T(8,128)S(1)}, f32[4,288,128]{2,1,0:T(8,128)S(1)}, u32[]{:S(2)}, u32[]{:S(2)}) %collective-permute-start.20) | collective-permute-done | bytes 589856 | tf_op jit(solution)/shard_map/grads_p/ppermute | solution.py:54
  83.3 2.0 %collective-permute-done.19 = f32[4,288,128]{2,1,0:T(8,128)S(1)} collective-permute-done((f32[4,288,128]{2,1,0:T(8,128)S(1)}, f32[4,288,128]{2,1,0:T(8,128)S(1)}, u32[]{:S(2)}, u32[]{:S(2)}) %collective-permute-start.19) | collective-permute-done | bytes 589856 | tf_op jit(solution)/shard_map/grads_p/ppermute | solution.py:54
  85.3 6.3 %collective-permute-done.18 = f32[4,288,128]{2,1,0:T(8,128)S(1)} collective-permute-done((f32[4,288,128]{2,1,0:T(8,128)S(1)}, f32[4,288,128]{2,1,0:T(8,128)S(1)}, u32[]{:S(2)}, u32[]{:S(2)}) %collective-permute-start.18) | collective-permute-done | bytes 589856 | tf_op jit(solution)/shard_map/grads_p/ppermute | solution.py:54
  91.8 1.6 %collective-permute-start.23 = (f32[288,128]{1,0:T(8,128)S(1)}, f32[288,128]{1,0:T(8,128)S(1)}, u32[]{:S(2)}, u32[]{:S(2)}) collective-permute-start(f32[288,128]{1,0:T(8,128)S(1)} %get-tuple-element.78), channel_id=1, source_target_pairs={{0,192},{8,56},{16,208},{24,8},{32,224},{40,24},{48,240},{56,40},{... | collective-permute-start | bytes 442376 | tf_op jit(solution)/shard_map/grads_q/ppermute | solution.py:58
  93.4 1.3 collective-permute-start.22
  94.6 0.8 collective-permute-start.21
  95.9 3.0 %collective-permute-done.22 = f32[288,128]{1,0:T(8,128)S(1)} collective-permute-done((f32[288,128]{1,0:T(8,128)S(1)}, f32[288,128]{1,0:T(8,128)S(1)}, u32[]{:S(2)}, u32[]{:S(2)}) %collective-permute-start.22) | collective-permute-done | bytes 147488 | tf_op jit(solution)/shard_map/grads_q/ppermute | solution.py:58
  98.9 1.8 %collective-permute-done.21 = f32[288,128]{1,0:T(8,128)S(1)} collective-permute-done((f32[288,128]{1,0:T(8,128)S(1)}, f32[288,128]{1,0:T(8,128)S(1)}, u32[]{:S(2)}, u32[]{:S(2)}) %collective-permute-start.21) | collective-permute-done | bytes 147488 | tf_op jit(solution)/shard_map/grads_q/ppermute | solution.py:58
  100.9 0.7 broadcast_in_dim.7
  101.6 8.1 %all-to-all-start = ((f32[256,1,128]{2,1,0:T(1,128)}), f32[256,1,128]{2,1,0:T(1,128)S(1)}, u32[]{:S(2)}, u32[]{:S(2)}) async-start(f32[256,1,128]{2,1,0:T(1,128)} %broadcast_in_dim.7), calls=%async_computation | async-start | bytes 262144 | tf_op jit(solution)/shard_map/all_to_all | solution.py:221
  109.7 6.3 %collective-permute-start.24 = (f32[64,128]{1,0:T(8,128)S(1)}, f32[64,128]{1,0:T(8,128)S(1)}, u32[]{:S(2)}, u32[]{:S(2)}) collective-permute-start(f32[64,128]{1,0:T(8,128)S(1)} %get-tuple-element.103), channel_id=1, source_target_pairs={{0,4},{1,5},{2,6},{3,7},{4,0},{5,1},{6,2},{7,3},{8,12},{9,13},{10,... | collective-permute-start | bytes 98312 | tf_op jit(solution)/shard_map/ppermute | solution.py:70
  116.4 2.0 %collective-permute-done.24 = f32[64,128]{1,0:T(8,128)S(1)} collective-permute-done((f32[64,128]{1,0:T(8,128)S(1)}, f32[64,128]{1,0:T(8,128)S(1)}, u32[]{:S(2)}, u32[]{:S(2)}) %collective-permute-start.24) | collective-permute-done | bytes 32800 | tf_op jit(solution)/shard_map/ppermute | solution.py:70
  118.4 4.3 %all-to-all-done = f32[256,1,128]{2,1,0:T(1,128)S(1)} async-done(((f32[256,1,128]{2,1,0:T(1,128)}), f32[256,1,128]{2,1,0:T(1,128)S(1)}, u32[]{:S(2)}, u32[]{:S(2)}) %all-to-all-start) | async-done | bytes 131104 | tf_op jit(solution)/shard_map/all_to_all | solution.py:221
  122.7 0.6 reduce_sum.29
  124.2 1.0 broadcast_in_dim.8
  125.3 3.6 %all-to-all-start.1 = ((bf16[16,224,128]{2,1,0:T(8,128)(2,1)}), bf16[16,224,128]{2,1,0:T(8,128)(2,1)S(1)}, u32[]{:S(2)}, u32[]{:S(2)}) async-start(bf16[16,224,128]{2,1,0:T(8,128)(2,1)} %broadcast_in_dim.8), calls=%async_computation.1 | async-start | bytes 1835008 | tf_op jit(solution)/shard_map/all_to_all | solution.py:239
  128.9 0.9 collective-permute-start.25
  129.9 2.5 %collective-permute-start.27 = (f32[128,128]{1,0:T(8,128)S(1)}, f32[128,128]{1,0:T(8,128)S(1)}, u32[]{:S(2)}, u32[]{:S(2)}) collective-permute-start(f32[128,128]{1,0:T(8,128)S(1)} %pad_maximum_fusion.20), channel_id=1, source_target_pairs={{0,7},{1,0},{2,1},{3,2},{4,3},{5,4},{6,5},{7,6},{8,15},{9,8},{10,9... | collective-permute-start | bytes 196616 | tf_op jit(solution)/shard_map/ppermute | solution.py:66
  132.4 0.9 collective-permute-done.25
  133.3 3.0 %collective-permute-done.26 = f32[128,128]{1,0:T(8,128)S(1)} collective-permute-done((f32[128,128]{1,0:T(8,128)S(1)}, f32[128,128]{1,0:T(8,128)S(1)}, u32[]{:S(2)}, u32[]{:S(2)}) %collective-permute-start.26) | collective-permute-done | bytes 65568 | tf_op jit(solution)/shard_map/ppermute | solution.py:66
  136.4 7.4 %all-to-all-done.1 = bf16[16,224,128]{2,1,0:T(8,128)(2,1)S(1)} async-done(((bf16[16,224,128]{2,1,0:T(8,128)(2,1)}), bf16[16,224,128]{2,1,0:T(8,128)(2,1)S(1)}, u32[]{:S(2)}, u32[]{:S(2)}) %all-to-all-start.1) | async-done | bytes 917536 | tf_op jit(solution)/shard_map/all_to_all | solution.py:239
  143.8 2.0 %collective-permute-start.28 = (bf16[16,224,128]{2,1,0:T(8,128)(2,1)S(1)}, bf16[16,224,128]{2,1,0:T(8,128)(2,1)S(1)}, u32[]{:S(2)}, u32[]{:S(2)}) collective-permute-start(bf16[16,224,128]{2,1,0:T(8,128)(2,1)S(1)} %all-to-all-done.1), channel_id=1, source_target_pairs={{0,8},{8,0},{1,9},{9,1},{2,10},{10,2},{3,11},{11,3},{4,12},{12,4},... | collective-permute-start | bytes 2752520 | tf_op jit(solution)/shard_map/ppermute | solution.py:62
  145.9 2.0 %collective-permute-done.28 = bf16[16,224,128]{2,1,0:T(8,128)(2,1)S(1)} collective-permute-done((bf16[16,224,128]{2,1,0:T(8,128)(2,1)S(1)}, bf16[16,224,128]{2,1,0:T(8,128)(2,1)S(1)}, u32[]{:S(2)}, u32[]{:S(2)}) %collective-permute-start.28) | collective-permute-done | bytes 917536 | tf_op jit(solution)/shard_map/ppermute | solution.py:62
  148.2 1.3 copy-done.2
  149.5 2.1 %fusion.1 = bf16[256,3584]{1,0:T(8,128)(2,1)} fusion(bf16[256,3584]{1,0:T(8,128)(2,1)S(1)} %bitcast.265, bf16[256,3584]{1,0:T(8,128)(2,1)S(1)} %copy-done.2, f32[256,256]{1,0:T(8,128)S(1)} %bitcast.269, f32[256,256]{1,0:T(8,128)S(1)} %bitcast.272, f32[256,256]{1,0:T(8,128)S(1)} %bitcast.271, f32[256,256]{1,0:T(8,128)S(1)} %bitcast.270), kind=kOutput, calls=%fused_computation.2 | convolution fusion | flops 474284032 | bytes 6553600 | tf_op jit(solution)/shard_map/dot_general | solution.py:250
  (97 shorter events, 6.4 us)
Async XLA Ops:
  1.9 6.8 %collective-permute-start.2 = (bf16[480,128]{1,0:T(8,128)(2,1)S(1)}, bf16[480,128]{1,0:T(8,128)(2,1)S(1)}, u32[]{:S(2)}, u32[]{:S(2)}) collective-permute-start(bf16[480,128]{1,0:T(8,128)(2,1)S(1)} %pad_maximum_fusion.19), channel_id=1, source_target_pairs={{0,48},{8,200},{16,0},{24,216},{32,16},{40,232},{48,32},{56,248},{... | collective-permute-start | bytes 368648 | tf_op jit(solution)/shard_map/factors_p/ppermute | solution.py:54
  5.5 5.5 %collective-permute-start.1 = (bf16[480,128]{1,0:T(8,128)(2,1)S(1)}, bf16[480,128]{1,0:T(8,128)(2,1)S(1)}, u32[]{:S(2)}, u32[]{:S(2)}) collective-permute-start(bf16[480,128]{1,0:T(8,128)(2,1)S(1)} %pad_maximum_fusion.19), channel_id=1, source_target_pairs={{0,32},{8,136},{16,48},{24,152},{32,0},{40,168},{48,16},{56,184},{... | collective-permute-start | bytes 368648 | tf_op jit(solution)/shard_map/factors_p/ppermute | solution.py:54
  5.8 6.5 %collective-permute-start = (bf16[480,128]{1,0:T(8,128)(2,1)S(1)}, bf16[480,128]{1,0:T(8,128)(2,1)S(1)}, u32[]{:S(2)}, u32[]{:S(2)}) collective-permute-start(bf16[480,128]{1,0:T(8,128)(2,1)S(1)} %pad_maximum_fusion.19), channel_id=1, source_target_pairs={{0,16},{8,72},{16,32},{24,88},{32,48},{40,104},{48,0},{56,120},{64... | collective-permute-start | bytes 368648 | tf_op jit(solution)/shard_map/factors_p/ppermute | solution.py:54
  12.6 7.7 %collective-permute-start.5 = (bf16[4,224,128]{2,1,0:T(8,128)(2,1)S(1)}, bf16[4,224,128]{2,1,0:T(8,128)(2,1)S(1)}, u32[]{:S(2)}, u32[]{:S(2)}) collective-permute-start(bf16[4,224,128]{2,1,0:T(8,128)(2,1)S(1)} %pad_maximum_fusion.15), channel_id=1, source_target_pairs={{0,192},{8,56},{16,208},{24,8},{32,224},{40,24},{48,240},{56,40},{... | collective-permute-start | bytes 688136 | tf_op jit(solution)/shard_map/a_q/ppermute | solution.py:58
  14.8 6.5 %collective-permute-start.4 = (bf16[4,224,128]{2,1,0:T(8,128)(2,1)S(1)}, bf16[4,224,128]{2,1,0:T(8,128)(2,1)S(1)}, u32[]{:S(2)}, u32[]{:S(2)}) collective-permute-start(bf16[4,224,128]{2,1,0:T(8,128)(2,1)S(1)} %pad_maximum_fusion.15), channel_id=1, source_target_pairs={{0,128},{8,40},{16,144},{24,56},{32,160},{40,8},{48,176},{56,24},{... | collective-permute-start | bytes 688136 | tf_op jit(solution)/shard_map/a_q/ppermute | solution.py:58
  15.3 8.6 %collective-permute-start.3 = (bf16[4,224,128]{2,1,0:T(8,128)(2,1)S(1)}, bf16[4,224,128]{2,1,0:T(8,128)(2,1)S(1)}, u32[]{:S(2)}, u32[]{:S(2)}) collective-permute-start(bf16[4,224,128]{2,1,0:T(8,128)(2,1)S(1)} %pad_maximum_fusion.15), channel_id=1, source_target_pairs={{0,64},{8,24},{16,80},{24,40},{32,96},{40,56},{48,112},{56,8},{64,... | collective-permute-start | bytes 688136 | tf_op jit(solution)/shard_map/a_q/ppermute | solution.py:58
  24.3 5.4 %collective-permute-start.6 = (bf16[4,4,224,128]{3,2,0,1:T(8,128)(2,1)S(1)}, bf16[4,4,224,128]{3,2,0,1:T(8,128)(2,1)S(1)}, u32[]{:S(2)}, u32[]{:S(2)}) collective-permute-start(bf16[4,4,224,128]{3,2,0,1:T(8,128)(2,1)S(1)} %pad_maximum_fusion.6), channel_id=1, source_target_pairs={{0,8},{8,0},{1,9},{9,1},{2,10},{10,2},{3,11},{11,3},{4,12},{12,4},... | collective-permute-start | bytes 2752520 | tf_op jit(solution)/shard_map/a_cores/ppermute | solution.py:62
  27.6 7.2 %collective-permute-start.10 = (bf16[4,256,128]{2,1,0:T(8,128)(2,1)S(1)}, bf16[4,256,128]{2,1,0:T(8,128)(2,1)S(1)}, u32[]{:S(2)}, u32[]{:S(2)}) collective-permute-start(bf16[4,256,128]{2,1,0:T(8,128)(2,1)S(1)} %pad_maximum_fusion.11), channel_id=1, source_target_pairs={{0,192},{8,56},{16,208},{24,8},{32,224},{40,24},{48,240},{56,40},{... | collective-permute-start | bytes 786440 | tf_op jit(solution)/shard_map/b_q/ppermute | solution.py:58
  27.9 7.1 %collective-permute-start.9 = (bf16[4,256,128]{2,1,0:T(8,128)(2,1)S(1)}, bf16[4,256,128]{2,1,0:T(8,128)(2,1)S(1)}, u32[]{:S(2)}, u32[]{:S(2)}) collective-permute-start(bf16[4,256,128]{2,1,0:T(8,128)(2,1)S(1)} %pad_maximum_fusion.11), channel_id=1, source_target_pairs={{0,128},{8,40},{16,144},{24,56},{32,160},{40,8},{48,176},{56,24},{... | collective-permute-start | bytes 786440 | tf_op jit(solution)/shard_map/b_q/ppermute | solution.py:58
  28.4 9.3 %collective-permute-start.8 = (bf16[4,256,128]{2,1,0:T(8,128)(2,1)S(1)}, bf16[4,256,128]{2,1,0:T(8,128)(2,1)S(1)}, u32[]{:S(2)}, u32[]{:S(2)}) collective-permute-start(bf16[4,256,128]{2,1,0:T(8,128)(2,1)S(1)} %pad_maximum_fusion.11), channel_id=1, source_target_pairs={{0,64},{8,24},{16,80},{24,40},{32,96},{40,56},{48,112},{56,8},{64,... | collective-permute-start | bytes 786440 | tf_op jit(solution)/shard_map/b_q/ppermute | solution.py:58
  29.9 2.0 %copy-start = (bf16[512,3584]{1,0:T(8,128)(2,1)S(1)}, bf16[512,3584]{1,0:T(8,128)(2,1)}, u32[]{:S(2)}) copy-start(bf16[512,3584]{1,0:T(8,128)(2,1)} %param.9) | copy-start | bytes 11010052
  33.0 8.1 %copy-start.4 = (f32[4,2,32,512]{3,2,1,0:T(8,128)}, f32[4,2,32,512]{3,2,1,0:T(8,128)S(1)}, u32[]{:S(2)}) copy-start(f32[4,2,32,512]{3,2,1,0:T(8,128)S(1)} %fusion.2) | copy-start | bytes 1572868
  33.1 8.0 %collective-permute-start.7 = (f32[4,32,512]{2,1,0:T(8,128)S(1)}, f32[4,32,512]{2,1,0:T(8,128)S(1)}, u32[]{:S(2)}, u32[]{:S(2)}) collective-permute-start(f32[4,32,512]{2,1,0:T(8,128)S(1)} %dynamic-slice_bitcast_fusion), channel_id=1, source_target_pairs={{0,1},{1,0},{2,3},{3,2},{4,5},{5,4},{6,7},{7,6},{8,9},{9,8},{10,11... | collective-permute-start | bytes 786440 | tf_op jit(solution)/shard_map/act_pairs/ppermute | solution.py:70
  41.4 12.7 %collective-permute-start.11 = (bf16[4,4,256,128]{3,2,0,1:T(8,128)(2,1)S(1)}, bf16[4,4,256,128]{3,2,0,1:T(8,128)(2,1)S(1)}, u32[]{:S(2)}, u32[]{:S(2)}) collective-permute-start(bf16[4,4,256,128]{3,2,0,1:T(8,128)(2,1)S(1)} %copy.24), channel_id=1, source_target_pairs={{0,8},{8,0},{1,9},{9,1},{2,10},{10,2},{3,11},{11,3},{4,12},{12,4},... | collective-permute-start | bytes 3145736 | tf_op jit(solution)/shard_map/b_cores/ppermute | solution.py:62
  42.5 12.4 %slice-start = ((s8[8388608]{0:T(1024)(128)(4,1)}), s8[4194304]{0:T(1024)(128)(4,1)S(1)}, s32[]{:S(2)}) async-start(s8[8388608]{0:T(1024)(128)(4,1)} %bitcast.262), calls=%async_computation.2 | async-start | bytes 8388608
  43.7 16.0 %collective-permute-start.12 = (f32[32,512]{1,0:T(8,128)S(1)}, f32[32,512]{1,0:T(8,128)S(1)}, u32[]{:S(2)}, u32[]{:S(2)}) collective-permute-start(f32[32,512]{1,0:T(8,128)S(1)} %get-tuple-element.92), channel_id=1, source_target_pairs={{0,2},{1,3},{2,4},{3,5},{4,6},{5,7},{6,0},{7,1},{8,10},{9,11},{10,... | collective-permute-start | bytes 196616 | tf_op jit(solution)/shard_map/act_shifts/ppermute | solution.py:66
  46.7 12.9 %collective-permute-start.13 = (f32[32,512]{1,0:T(8,128)S(1)}, f32[32,512]{1,0:T(8,128)S(1)}, u32[]{:S(2)}, u32[]{:S(2)}) collective-permute-start(f32[32,512]{1,0:T(8,128)S(1)} %get-tuple-element.91), channel_id=1, source_target_pairs={{0,4},{1,5},{2,6},{3,7},{4,0},{5,1},{6,2},{7,3},{8,12},{9,13},{10,... | collective-permute-start | bytes 196616 | tf_op jit(solution)/shard_map/act_shifts/ppermute | solution.py:66
  51.7 8.0 %collective-permute-start.14 = (f32[32,512]{1,0:T(8,128)S(1)}, f32[32,512]{1,0:T(8,128)S(1)}, u32[]{:S(2)}, u32[]{:S(2)}) collective-permute-start(f32[32,512]{1,0:T(8,128)S(1)} %get-tuple-element.90), channel_id=1, source_target_pairs={{0,6},{1,7},{2,0},{3,1},{4,2},{5,3},{6,4},{7,5},{8,14},{9,15},{10,... | collective-permute-start | bytes 196616 | tf_op jit(solution)/shard_map/act_shifts/ppermute | solution.py:66
  54.6 2.2 %slice-start.1 = ((s8[8388608]{0:T(1024)(128)(4,1)}), s8[4194304]{0:T(1024)(128)(4,1)S(1)}, s32[]{:S(2)}) async-start(s8[8388608]{0:T(1024)(128)(4,1)} %bitcast.262), calls=%async_computation.3 | async-start | bytes 8388608
  59.7 5.1 %collective-permute-start.15 = (bf16[128,512]{1,0:T(8,128)(2,1)S(1)}, bf16[128,512]{1,0:T(8,128)(2,1)S(1)}, u32[]{:S(2)}, u32[]{:S(2)}) collective-permute-start(bf16[128,512]{1,0:T(8,128)(2,1)S(1)} %fusion.4), channel_id=1, source_target_pairs={{0,7},{1,2},{2,1},{3,4},{4,3},{5,6},{6,5},{7,0},{8,15},{9,10},{10,... | collective-permute-start | bytes 393224 | tf_op jit(solution)/shard_map/back_pairs/ppermute | solution.py:74
  62.1 3.0 %copy-start.1 = (bf16[512,3584]{1,0:T(8,128)(2,1)S(1)}, bf16[512,3584]{1,0:T(8,128)(2,1)}, u32[]{:S(2)}) copy-start(bf16[512,3584]{1,0:T(8,128)(2,1)} %param.9) | copy-start | bytes 11010052
  65.8 6.6 %collective-permute-start.16 = (f32[128,3584]{1,0:T(8,128)S(1)}, f32[128,3584]{1,0:T(8,128)}, u32[]{:S(2)}, u32[]{:S(2)}) collective-permute-start(f32[128,3584]{1,0:T(8,128)S(1)} %fusion.55), channel_id=1, source_target_pairs={{0,8},{8,0},{1,9},{9,1},{2,10},{10,2},{3,11},{11,3},{4,12},{12,4},... | collective-permute-start | bytes 5505032 | tf_op jit(solution)/shard_map/grad_a_cores/ppermute | solution.py:62
  68.3 3.9 %collective-permute-start.17 = (f32[4,4,64,128]{3,2,1,0:T(8,128)S(1)}, f32[4,4,64,128]{3,2,1,0:T(8,128)S(1)}, u32[]{:S(2)}, u32[]{:S(2)}) collective-permute-start(f32[4,4,64,128]{3,2,1,0:T(8,128)S(1)} %get-tuple-element.64), channel_id=1, source_target_pairs={{0,8},{8,0},{1,9},{9,1},{2,10},{10,2},{3,11},{11,3},{4,12},{12,4},... | collective-permute-start | bytes 1572872 | tf_op jit(solution)/shard_map/grad_b_cores/ppermute | solution.py:62
  74.2 9.1 %collective-permute-start.20 = (f32[4,288,128]{2,1,0:T(8,128)S(1)}, f32[4,288,128]{2,1,0:T(8,128)S(1)}, u32[]{:S(2)}, u32[]{:S(2)}) collective-permute-start(f32[4,288,128]{2,1,0:T(8,128)S(1)} %maximum_maximum_fusion.2), channel_id=1, source_target_pairs={{0,48},{8,200},{16,0},{24,216},{32,16},{40,232},{48,32},{56,248},{... | collective-permute-start | bytes 1769480 | tf_op jit(solution)/shard_map/grads_p/ppermute | solution.py:54
  74.6 10.7 %collective-permute-start.19 = (f32[4,288,128]{2,1,0:T(8,128)S(1)}, f32[4,288,128]{2,1,0:T(8,128)S(1)}, u32[]{:S(2)}, u32[]{:S(2)}) collective-permute-start(f32[4,288,128]{2,1,0:T(8,128)S(1)} %maximum_maximum_fusion.1), channel_id=1, source_target_pairs={{0,32},{8,136},{16,48},{24,152},{32,0},{40,168},{48,16},{56,184},{... | collective-permute-start | bytes 1769480 | tf_op jit(solution)/shard_map/grads_p/ppermute | solution.py:54
  76.0 15.6 %collective-permute-start.18 = (f32[4,288,128]{2,1,0:T(8,128)S(1)}, f32[4,288,128]{2,1,0:T(8,128)S(1)}, u32[]{:S(2)}, u32[]{:S(2)}) collective-permute-start(f32[4,288,128]{2,1,0:T(8,128)S(1)} %maximum_maximum_fusion), channel_id=1, source_target_pairs={{0,16},{8,72},{16,32},{24,88},{32,48},{40,104},{48,0},{56,120},{64... | collective-permute-start | bytes 1769480 | tf_op jit(solution)/shard_map/grads_p/ppermute | solution.py:54
  91.5 24.5 %copy-start.3 = (f32[256,256]{1,0:T(8,128)S(1)}, f32[256,256]{1,0:T(8,128)}, u32[]{:S(2)}) copy-start(f32[256,256]{1,0:T(8,128)} %param.15) | copy-start | bytes 786436
  91.7 24.4 %copy-start.6 = (f32[256,256]{1,0:T(8,128)S(1)}, f32[256,256]{1,0:T(8,128)}, u32[]{:S(2)}) copy-start(f32[256,256]{1,0:T(8,128)} %param.16) | copy-start | bytes 786436
  91.7 24.6 %copy-start.7 = (f32[256,256]{1,0:T(8,128)S(1)}, f32[256,256]{1,0:T(8,128)}, u32[]{:S(2)}) copy-start(f32[256,256]{1,0:T(8,128)} %param.17) | copy-start | bytes 786436
  91.7 32.4 %copy-start.5 = (f32[8,3584]{1,0:T(8,128)S(1)}, f32[8,3584]{1,0:T(8,128)}, u32[]{:S(2)}) copy-start(f32[8,3584]{1,0:T(8,128)} %param.12) | copy-start | bytes 344068
  91.7 32.4 %copy-start.8 = (f32[8,3584]{1,0:T(8,128)S(1)}, f32[8,3584]{1,0:T(8,128)}, u32[]{:S(2)}) copy-start(f32[8,3584]{1,0:T(8,128)} %param.14) | copy-start | bytes 344068
  91.7 32.4 %copy-start.9 = (f32[8,3584]{1,0:T(8,128)S(1)}, f32[8,3584]{1,0:T(8,128)}, u32[]{:S(2)}) copy-start(f32[8,3584]{1,0:T(8,128)} %param.13) | copy-start | bytes 344068
  91.8 4.1 %collective-permute-start.23 = (f32[288,128]{1,0:T(8,128)S(1)}, f32[288,128]{1,0:T(8,128)S(1)}, u32[]{:S(2)}, u32[]{:S(2)}) collective-permute-start(f32[288,128]{1,0:T(8,128)S(1)} %get-tuple-element.78), channel_id=1, source_target_pairs={{0,192},{8,56},{16,208},{24,8},{32,224},{40,24},{48,240},{56,40},{... | collective-permute-start | bytes 442376 | tf_op jit(solution)/shard_map/grads_q/ppermute | solution.py:58
  93.4 5.6 %collective-permute-start.22 = (f32[288,128]{1,0:T(8,128)S(1)}, f32[288,128]{1,0:T(8,128)S(1)}, u32[]{:S(2)}, u32[]{:S(2)}) collective-permute-start(f32[288,128]{1,0:T(8,128)S(1)} %get-tuple-element.79), channel_id=1, source_target_pairs={{0,128},{8,40},{16,144},{24,56},{32,160},{40,8},{48,176},{56,24},{... | collective-permute-start | bytes 442376 | tf_op jit(solution)/shard_map/grads_q/ppermute | solution.py:58
  94.6 6.1 %collective-permute-start.21 = (f32[288,128]{1,0:T(8,128)S(1)}, f32[288,128]{1,0:T(8,128)S(1)}, u32[]{:S(2)}, u32[]{:S(2)}) collective-permute-start(f32[288,128]{1,0:T(8,128)S(1)} %get-tuple-element.77), channel_id=1, source_target_pairs={{0,64},{8,24},{16,80},{24,40},{32,96},{40,56},{48,112},{56,8},{64,... | collective-permute-start | bytes 442376 | tf_op jit(solution)/shard_map/grads_q/ppermute | solution.py:58
  101.6 21.1 %all-to-all-start = ((f32[256,1,128]{2,1,0:T(1,128)}), f32[256,1,128]{2,1,0:T(1,128)S(1)}, u32[]{:S(2)}, u32[]{:S(2)}) async-start(f32[256,1,128]{2,1,0:T(1,128)} %broadcast_in_dim.7), calls=%async_computation | async-start | bytes 262144 | tf_op jit(solution)/shard_map/all_to_all | solution.py:221
  109.7 8.8 %collective-permute-start.24 = (f32[64,128]{1,0:T(8,128)S(1)}, f32[64,128]{1,0:T(8,128)S(1)}, u32[]{:S(2)}, u32[]{:S(2)}) collective-permute-start(f32[64,128]{1,0:T(8,128)S(1)} %get-tuple-element.103), channel_id=1, source_target_pairs={{0,4},{1,5},{2,6},{3,7},{4,0},{5,1},{6,2},{7,3},{8,12},{9,13},{10,... | collective-permute-start | bytes 98312 | tf_op jit(solution)/shard_map/ppermute | solution.py:70
  125.3 18.5 %all-to-all-start.1 = ((bf16[16,224,128]{2,1,0:T(8,128)(2,1)}), bf16[16,224,128]{2,1,0:T(8,128)(2,1)S(1)}, u32[]{:S(2)}, u32[]{:S(2)}) async-start(bf16[16,224,128]{2,1,0:T(8,128)(2,1)} %broadcast_in_dim.8), calls=%async_computation.1 | async-start | bytes 1835008 | tf_op jit(solution)/shard_map/all_to_all | solution.py:239
  128.9 4.4 %collective-permute-start.25 = (f32[128,128]{1,0:T(8,128)S(1)}, f32[128,128]{1,0:T(8,128)S(1)}, u32[]{:S(2)}, u32[]{:S(2)}) collective-permute-start(f32[128,128]{1,0:T(8,128)S(1)} %pad_maximum_fusion.20), channel_id=1, source_target_pairs={{0,1},{1,2},{2,3},{3,4},{4,5},{5,6},{6,7},{7,0},{8,9},{9,10},{10,1... | collective-permute-start | bytes 196616 | tf_op jit(solution)/shard_map/ppermute | solution.py:66
  129.9 6.5 %collective-permute-start.26 = (f32[128,128]{1,0:T(8,128)S(1)}, f32[128,128]{1,0:T(8,128)S(1)}, u32[]{:S(2)}, u32[]{:S(2)}) collective-permute-start(f32[128,128]{1,0:T(8,128)S(1)} %pad_maximum_fusion.20), channel_id=1, source_target_pairs={{0,2},{1,3},{2,4},{3,5},{4,6},{5,7},{6,0},{7,1},{8,10},{9,11},{10,... | collective-permute-start | bytes 196616 | tf_op jit(solution)/shard_map/ppermute | solution.py:66
  129.9 6.5 %collective-permute-start.27 = (f32[128,128]{1,0:T(8,128)S(1)}, f32[128,128]{1,0:T(8,128)S(1)}, u32[]{:S(2)}, u32[]{:S(2)}) collective-permute-start(f32[128,128]{1,0:T(8,128)S(1)} %pad_maximum_fusion.20), channel_id=1, source_target_pairs={{0,7},{1,0},{2,1},{3,2},{4,3},{5,4},{6,5},{7,6},{8,15},{9,8},{10,9... | collective-permute-start | bytes 196616 | tf_op jit(solution)/shard_map/ppermute | solution.py:66
  143.8 4.1 %collective-permute-start.28 = (bf16[16,224,128]{2,1,0:T(8,128)(2,1)S(1)}, bf16[16,224,128]{2,1,0:T(8,128)(2,1)S(1)}, u32[]{:S(2)}, u32[]{:S(2)}) collective-permute-start(bf16[16,224,128]{2,1,0:T(8,128)(2,1)S(1)} %all-to-all-done.1), channel_id=1, source_target_pairs={{0,8},{8,0},{1,9},{9,1},{2,10},{10,2},{3,11},{11,3},{4,12},{12,4},... | collective-permute-start | bytes 2752520 | tf_op jit(solution)/shard_map/ppermute | solution.py:62
  148.0 1.5 copy-start.2

commit v2 on v1

--- a/solution.py
+++ b/solution.py
@@ -162,7 +162,9 @@
         act_send = lax.dynamic_index_in_dim(act_part, 1 - z % 2, 1, keepdims=False)
         act_keep = lax.dynamic_index_in_dim(act_part, z % 2, 1, keepdims=False)
     with jax.named_scope("act_pairs"):
-        act_got = flip(act_send, "z", 8, 1)
+        act_got = jnp.concatenate(
+            [flip(act_send[..., :256], "z", 8, 1), swap_pairs(act_send[..., 256:])], axis=2
+        )
     act_got, b_stack = lax.optimization_barrier((act_got, b_stack))
     with jax.named_scope("act_shifts"):
         act_pair = act_keep + act_got
@@ -218,9 +220,9 @@
     grad_b = total[224:] * rank_scale
 
     squares = jnp.sum(grad_a * grad_a, axis=0) + jnp.sum(grad_b * grad_b, axis=0)
-    squares = lax.all_to_all(
-        jnp.broadcast_to(squares, (256, 128)), ("y", "x", "core", "z"), 0, 0, tiled=True
-    )
+    squares = jnp.broadcast_to(squares, (128, 128))
+    squares = squares + jnp.broadcast_to(swap_core(squares[:8])[:1], (128, 128))
+    squares = lax.all_to_all(squares, ("y", "x", "z"), 0, 0, tiled=True)
     pair = flip(grad_b, "z", 8, 4)
     right_t = (right_lowrank_factor.T, right_first_moment.T, right_second_moment.T)
     squares, pair, right_t = lax.optimization_barrier((squares, pair, right_t))

time: 152 us -> 151 us (level)
  waiting for transfers between devices: 63 us -> 59.6 us
  starting transfers between devices: 59.1 us -> 61.6 us
    ppermute x1 -> x2, starting transfers between devices: 0.85 us -> 6.1 us  [swap_pairs(): lax.ppermute(v, 'z', [(i, (i + 1) % 8 if i % 2 else (i - 1) % 8) for i in...]
    ppermute x5 -> x6, starting transfers between devices: 8.81 us -> 13.5 us  [swap_core(): return lax.ppermute(v, 'core', [(0, 1), (1, 0)])]
    ppermute x1 -> x2, waiting for transfers between devices: 2.7 us -> 6.47 us  [swap_pairs(): lax.ppermute(v, 'z', [(i, (i + 1) % 8 if i % 2 else (i - 1) % 8) for i in...]
    ppermute x6, starting transfers between devices: 13.9 us -> 10.3 us  [shift_z(): return lax.ppermute(v, 'z', [(i, (i + k) % 8) for i in range(8)])]
    ppermute x2, starting transfers between devices: 8.05 us -> 4.57 us  [flip(): return lax.ppermute(v, axis, [(i, i ^ bit) for i in range(n)])]
    ppermute x9, waiting for transfers between devices: 16.2 us -> 13.3 us  [shift_q(): return lax.ppermute(v, DP, plane_pairs(False, k))]
    ppermute x2, waiting for transfers between devices: 5.24 us -> 3.05 us  [flip(): return lax.ppermute(v, axis, [(i, i ^ bit) for i in range(n)])]
    ppermute x5 -> x6, waiting for transfers between devices: 3.66 us -> 4.49 us  [swap_core(): return lax.ppermute(v, 'core', [(0, 1), (1, 0)])]
  transfers between devices with their start and end apart: 31 -> 33, of which waited for: 24 -> 26; matrix products, arithmetic and copies ran while one was open for 8% -> 8% of each run, Pallas kernels for 0% -> 0%
where the time goes in v2:
time: 151 us
  starting transfers between devices  61.6 us (41%)
  waiting for transfers between devices  59.6 us (39%)
  matrix products  11 us (7%)
  local copies, waits for them, and re-layouts  9.86 us (7%)
  other arithmetic  7.15 us (5%)
    ppermute x6, waiting for transfers between devices, shift_p(): return lax.ppermute(v, DP, plane_pairs(True, k))  19.3 us
    ppermute x6, starting transfers between devices, swap_core(): return lax.ppermute(v, 'core', [(0, 1), (1, 0)])  13.5 us
    ppermute x9, waiting for transfers between devices, shift_q(): return lax.ppermute(v, DP, plane_pairs(False, k))  13.3 us
    ppermute x6, starting transfers between devices, shift_z(): return lax.ppermute(v, 'z', [(i, (i + k) % 8) for i in range(8)])  10.3 us
    ppermute x6, starting transfers between devices, shift_p(): return lax.ppermute(v, DP, plane_pairs(True, k))  8.73 us
    all_to_all x1, starting transfers between devices, local(): squares = lax.all_to_all(squares, ('y', 'x', 'z'), 0, 0, tiled=True)  7.52 us
    ppermute x9, starting transfers between devices, shift_q(): return lax.ppermute(v, DP, plane_pairs(False, k))  7.29 us
    all_to_all x1, waiting for transfers between devices, local(): mine = lax.all_to_all(copies, ('y', 'x'), 0, 0, tiled=True)  6.74 us
  transfers between devices with their start and end apart: 33, of which 26 were waited for; matrix products, arithmetic and copies ran while one was open for 8% of the time, Pallas kernels for 0%

profile of v2, /device:TPU:1, one launch (start us, length us, event | category | flops | bytes accessed | tf_op | source)
XLA Modules:
  0.0 150.7 jit_solution(15748577898288413344)
XLA Ops:
  0.0 0.9 fusion.44
  0.9 0.9 dynamic-slice_convert_fusion
  1.9 3.6 %collective-permute-start.2 = (bf16[480,128]{1,0:T(8,128)(2,1)S(1)}, bf16[480,128]{1,0:T(8,128)(2,1)S(1)}, u32[]{:S(2)}, u32[]{:S(2)}) collective-permute-start(bf16[480,128]{1,0:T(8,128)(2,1)S(1)} %pad_maximum_fusion.20), channel_id=1, source_target_pairs={{0,48},{8,200},{16,0},{24,216},{32,16},{40,232},{48,32},{56,248},{... | collective-permute-start | bytes 368648 | tf_op jit(solution)/shard_map/factors_p/ppermute | solution.py:54
  5.8 0.7 collective-permute-start
  6.5 0.9 fusion.67
  7.4 1.2 collective-permute-done.2
  8.6 2.4 %collective-permute-done.1 = bf16[480,128]{1,0:T(8,128)(2,1)S(1)} collective-permute-done((bf16[480,128]{1,0:T(8,128)(2,1)S(1)}, bf16[480,128]{1,0:T(8,128)(2,1)S(1)}, u32[]{:S(2)}, u32[]{:S(2)}) %collective-permute-start.1) | collective-permute-done | bytes 122912 | tf_op jit(solution)/shard_map/factors_p/ppermute | solution.py:54
  11.0 1.3 collective-permute-done
  12.6 2.3 %collective-permute-start.5 = (bf16[4,224,128]{2,1,0:T(8,128)(2,1)S(1)}, bf16[4,224,128]{2,1,0:T(8,128)(2,1)S(1)}, u32[]{:S(2)}, u32[]{:S(2)}) collective-permute-start(bf16[4,224,128]{2,1,0:T(8,128)(2,1)S(1)} %pad_maximum_fusion.16), channel_id=1, source_target_pairs={{0,192},{8,56},{16,208},{24,8},{32,224},{40,24},{48,240},{56,40},{... | collective-permute-start | bytes 688136 | tf_op jit(solution)/shard_map/a_q/ppermute | solution.py:58
  15.3 0.6 collective-permute-start.3
  15.9 4.3 %collective-permute-done.5 = bf16[4,224,128]{2,1,0:T(8,128)(2,1)S(1)} collective-permute-done((bf16[4,224,128]{2,1,0:T(8,128)(2,1)S(1)}, bf16[4,224,128]{2,1,0:T(8,128)(2,1)S(1)}, u32[]{:S(2)}, u32[]{:S(2)}) %collective-permute-start.5) | collective-permute-done | bytes 229408 | tf_op jit(solution)/shard_map/a_q/ppermute | solution.py:58
  20.2 1.1 collective-permute-done.4
  21.3 2.6 %collective-permute-done.3 = bf16[4,224,128]{2,1,0:T(8,128)(2,1)S(1)} collective-permute-done((bf16[4,224,128]{2,1,0:T(8,128)(2,1)S(1)}, bf16[4,224,128]{2,1,0:T(8,128)(2,1)S(1)}, u32[]{:S(2)}, u32[]{:S(2)}) %collective-permute-start.3) | collective-permute-done | bytes 229408 | tf_op jit(solution)/shard_map/a_q/ppermute | solution.py:58
  24.3 3.3 %collective-permute-start.6 = (bf16[4,4,224,128]{3,2,0,1:T(8,128)(2,1)S(1)}, bf16[4,4,224,128]{3,2,0,1:T(8,128)(2,1)S(1)}, u32[]{:S(2)}, u32[]{:S(2)}) collective-permute-start(bf16[4,4,224,128]{3,2,0,1:T(8,128)(2,1)S(1)} %pad_maximum_fusion.6), channel_id=1, source_target_pairs={{0,8},{8,0},{1,9},{9,1},{2,10},{10,2},{3,11},{11,3},{4,12},{12,4},... | collective-permute-start | bytes 2752520 | tf_op jit(solution)/shard_map/a_cores/ppermute | solution.py:62
  28.4 0.7 collective-permute-start.9
  29.1 0.6 collective-permute-done.6
  30.1 1.8 %copy-done = bf16[512,3584]{1,0:T(8,128)(2,1)S(1)} copy-done((bf16[512,3584]{1,0:T(8,128)(2,1)S(1)}, bf16[512,3584]{1,0:T(8,128)(2,1)}, u32[]{:S(2)}) %copy-start) | copy-done | bytes 3670040
  31.9 1.1 fusion.2
  33.1 5.7 %collective-permute-start.8 = (f32[4,32,256]{2,1,0:T(8,128)S(1)}, f32[4,32,256]{2,1,0:T(8,128)S(1)}, u32[]{:S(2)}, u32[]{:S(2)}) collective-permute-start(f32[4,32,256]{2,1,0:T(8,128)S(1)} %get-tuple-element.94), channel_id=1, source_target_pairs={{0,7},{1,2},{2,1},{3,4},{4,3},{5,6},{6,5},{7,0},{8,15},{9,10},{10,... | collective-permute-start | bytes 393224 | tf_op jit(solution)/shard_map/act_pairs/ppermute | solution.py:74
  38.9 3.4 %collective-permute-done.8 = f32[4,32,256]{2,1,0:T(8,128)S(1)} collective-permute-done((f32[4,32,256]{2,1,0:T(8,128)S(1)}, f32[4,32,256]{2,1,0:T(8,128)S(1)}, u32[]{:S(2)}, u32[]{:S(2)}) %collective-permute-start.8) | collective-permute-done | bytes 131104 | tf_op jit(solution)/shard_map/act_pairs/ppermute | solution.py:74
  42.3 0.8 collective-permute-done.7
  43.6 1.6 %collective-permute-start.12 = (bf16[4,4,256,128]{3,2,0,1:T(8,128)(2,1)S(1)}, bf16[4,4,256,128]{3,2,0,1:T(8,128)(2,1)S(1)}, u32[]{:S(2)}, u32[]{:S(2)}) collective-permute-start(bf16[4,4,256,128]{3,2,0,1:T(8,128)(2,1)S(1)} %copy.24), channel_id=1, source_target_pairs={{0,8},{8,0},{1,9},{9,1},{2,10},{10,2},{3,11},{11,3},{4,12},{12,4},... | collective-permute-start | bytes 3145736 | tf_op jit(solution)/shard_map/b_cores/ppermute | solution.py:62
  45.2 1.1 bitcast_add_fusion
  46.9 2.8 %collective-permute-start.14 = (f32[32,512]{1,0:T(8,128)S(1)}, f32[32,512]{1,0:T(8,128)S(1)}, u32[]{:S(2)}, u32[]{:S(2)}) collective-permute-start(f32[32,512]{1,0:T(8,128)S(1)} %get-tuple-element.91), channel_id=1, source_target_pairs={{0,4},{1,5},{2,6},{3,7},{4,0},{5,1},{6,2},{7,3},{8,12},{9,13},{10,... | collective-permute-start | bytes 196616 | tf_op jit(solution)/shard_map/act_shifts/ppermute | solution.py:66
  49.7 2.9 %collective-permute-start.15 = (f32[32,512]{1,0:T(8,128)S(1)}, f32[32,512]{1,0:T(8,128)S(1)}, u32[]{:S(2)}, u32[]{:S(2)}) collective-permute-start(f32[32,512]{1,0:T(8,128)S(1)} %get-tuple-element.90), channel_id=1, source_target_pairs={{0,6},{1,7},{2,0},{3,1},{4,2},{5,3},{6,4},{7,5},{8,14},{9,15},{10,... | collective-permute-start | bytes 196616 | tf_op jit(solution)/shard_map/act_shifts/ppermute | solution.py:66
  53.4 1.8 %slice-done.1 = s8[4194304]{0:T(1024)(128)(4,1)S(1)} async-done(((s8[8388608]{0:T(1024)(128)(4,1)}), s8[4194304]{0:T(1024)(128)(4,1)S(1)}, s32[]{:S(2)}) %slice-start.1) | async-done | bytes 4194328
  55.2 2.9 %fusion.4 = bf16[128,512]{1,0:T(8,128)(2,1)S(1)} fusion(bf16[8192,128]{1,0:T(8,128)(2,1)S(1)} %bitcast.266, bf16[512,8192]{1,0:T(8,128)(2,1)S(1)} %bitcast.265), kind=kOutput, calls=%fused_computation.9 | convolution fusion | flops 1073872896 | bytes 10616832 | tf_op jit(solution)/shard_map/back/dot_general | solution.py:178
  58.7 1.5 %fusion.54 = f32[32,8192]{1,0:T(8,128)S(1)} fusion(bf16[32,512]{1,0:T(8,128)(2,1)S(1)} %fusion.43, bf16[512,8192]{1,0:T(8,128)(2,1)S(1)} %bitcast.265), kind=kOutput, calls=%fused_computation.177 | convolution fusion | flops 268435456 | bytes 9469952 | tf_op jit(solution)/shard_map/grad_b_terms/dot_general | solution.py:187
  60.2 3.1 %collective-permute-done.16 = bf16[128,512]{1,0:T(8,128)(2,1)S(1)} collective-permute-done((bf16[128,512]{1,0:T(8,128)(2,1)S(1)}, bf16[128,512]{1,0:T(8,128)(2,1)S(1)}, u32[]{:S(2)}, u32[]{:S(2)}) %collective-permute-start.16) | collective-permute-done | bytes 131104 | tf_op jit(solution)/shard_map/back_pairs/ppermute | solution.py:74
  63.6 0.7 fusion.56
  64.2 2.3 %collective-permute-start.17 = (f32[128,3584]{1,0:T(8,128)S(1)}, f32[128,3584]{1,0:T(8,128)}, u32[]{:S(2)}, u32[]{:S(2)}) collective-permute-start(f32[128,3584]{1,0:T(8,128)S(1)} %fusion.56), channel_id=1, source_target_pairs={{0,8},{8,0},{1,9},{9,1},{2,10},{10,2},{3,11},{11,3},{4,12},{12,4},... | collective-permute-start | bytes 5505032 | tf_op jit(solution)/shard_map/grad_a_cores/ppermute | solution.py:62
  67.0 2.7 %fusion.55 = f32[128,3584]{1,0:T(8,128)S(1)} fusion(bf16[128,512]{1,0:T(8,128)(2,1)S(1)} %bitcast.279, bf16[512,3584]{1,0:T(8,128)(2,1)} %param.9), kind=kOutput, calls=%fused_computation.178 | convolution fusion | flops 469762048 | bytes 5636096 | tf_op jit(solution)/shard_map/grad_a_terms/dot_general | solution.py:195
  69.7 1.0 collective-permute-done.18
  70.9 1.7 %fusion.13 = (f32[4,224,128]{2,1,0:T(8,128)S(1)}, f32[4,224,128]{2,1,0:T(8,128)S(1)}, f32[4,224,128]{2,1,0:T(8,128)S(1)}, f32[4,224,128]{2,1,0:T(8,128)S(1)}) fusion(f32[128,3584]{1,0:T(8,128)} %collective-permute-done.17, f32[128,3584]{1,0:T(8,128)S(1)} %fusion.55), kind=kLoop, calls=%fused_computation.38 | loop fusion | flops 458752 | bytes 5505024 | tf_op jit(solution)/shard_map/reshape | solution.py:207
  72.6 1.6 %collective-permute-start.21 = (f32[4,288,128]{2,1,0:T(8,128)S(1)}, f32[4,288,128]{2,1,0:T(8,128)S(1)}, u32[]{:S(2)}, u32[]{:S(2)}) collective-permute-start(f32[4,288,128]{2,1,0:T(8,128)S(1)} %maximum_maximum_fusion.2), channel_id=1, source_target_pairs={{0,48},{8,200},{16,0},{24,216},{32,16},{40,232},{48,32},{56,248},{... | collective-permute-start | bytes 1769480 | tf_op jit(solution)/shard_map/grads_p/ppermute | solution.py:54
  74.2 1.6 %collective-permute-start.20 = (f32[4,288,128]{2,1,0:T(8,128)S(1)}, f32[4,288,128]{2,1,0:T(8,128)S(1)}, u32[]{:S(2)}, u32[]{:S(2)}) collective-permute-start(f32[4,288,128]{2,1,0:T(8,128)S(1)} %maximum_maximum_fusion.1), channel_id=1, source_target_pairs={{0,32},{8,136},{16,48},{24,152},{32,0},{40,168},{48,16},{56,184},{... | collective-permute-start | bytes 1769480 | tf_op jit(solution)/shard_map/grads_p/ppermute | solution.py:54
  75.8 0.9 collective-permute-start.19
  76.8 5.0 %collective-permute-done.21 = f32[4,288,128]{2,1,0:T(8,128)S(1)} collective-permute-done((f32[4,288,128]{2,1,0:T(8,128)S(1)}, f32[4,288,128]{2,1,0:T(8,128)S(1)}, u32[]{:S(2)}, u32[]{:S(2)}) %collective-permute-start.21) | collective-permute-done | bytes 589856 | tf_op jit(solution)/shard_map/grads_p/ppermute | solution.py:54
  81.7 3.2 %collective-permute-done.20 = f32[4,288,128]{2,1,0:T(8,128)S(1)} collective-permute-done((f32[4,288,128]{2,1,0:T(8,128)S(1)}, f32[4,288,128]{2,1,0:T(8,128)S(1)}, u32[]{:S(2)}, u32[]{:S(2)}) %collective-permute-start.20) | collective-permute-done | bytes 589856 | tf_op jit(solution)/shard_map/grads_p/ppermute | solution.py:54
  84.9 6.3 %collective-permute-done.19 = f32[4,288,128]{2,1,0:T(8,128)S(1)} collective-permute-done((f32[4,288,128]{2,1,0:T(8,128)S(1)}, f32[4,288,128]{2,1,0:T(8,128)S(1)}, u32[]{:S(2)}, u32[]{:S(2)}) %collective-permute-start.19) | collective-permute-done | bytes 589856 | tf_op jit(solution)/shard_map/grads_p/ppermute | solution.py:54
  91.8 1.3 collective-permute-start.23
  93.1 0.8 collective-permute-start.22
  93.8 1.9 %collective-permute-done.24 = f32[288,128]{1,0:T(8,128)S(1)} collective-permute-done((f32[288,128]{1,0:T(8,128)S(1)}, f32[288,128]{1,0:T(8,128)S(1)}, u32[]{:S(2)}, u32[]{:S(2)}) %collective-permute-start.24) | collective-permute-done | bytes 147488 | tf_op jit(solution)/shard_map/grads_q/ppermute | solution.py:58
  95.8 1.6 %collective-permute-done.23 = f32[288,128]{1,0:T(8,128)S(1)} collective-permute-done((f32[288,128]{1,0:T(8,128)S(1)}, f32[288,128]{1,0:T(8,128)S(1)}, u32[]{:S(2)}, u32[]{:S(2)}) %collective-permute-start.23) | collective-permute-done | bytes 147488 | tf_op jit(solution)/shard_map/grads_q/ppermute | solution.py:58
  97.4 1.8 %collective-permute-done.22 = f32[288,128]{1,0:T(8,128)S(1)} collective-permute-done((f32[288,128]{1,0:T(8,128)S(1)}, f32[288,128]{1,0:T(8,128)S(1)}, u32[]{:S(2)}, u32[]{:S(2)}) %collective-permute-start.22) | collective-permute-done | bytes 147488 | tf_op jit(solution)/shard_map/grads_q/ppermute | solution.py:58
  99.3 3.0 %collective-permute-start.25 = (f32[8,128]{1,0:T(8,128)S(1)}, f32[8,128]{1,0:T(8,128)S(1)}, u32[]{:S(2)}, u32[]{:S(2)}) collective-permute-start(f32[8,128]{1,0:T(8,128)S(1)} %slice.94), channel_id=1, source_target_pairs={{0,8},{8,0},{1,9},{9,1},{2,10},{10,2},{3,11},{11,3},{4,12},{12,4},... | collective-permute-start | bytes 12296 | tf_op jit(solution)/shard_map/ppermute | solution.py:62
  102.3 0.8 collective-permute-done.25
  103.2 0.7 broadcast_in_dim.13
  103.8 7.5 %all-to-all-start = ((f32[128,1,128]{2,1,0:T(1,128)}), f32[128,1,128]{2,1,0:T(1,128)S(1)}, u32[]{:S(2)}, u32[]{:S(2)}) async-start(f32[128,1,128]{2,1,0:T(1,128)} %broadcast_in_dim.13), calls=%async_computation | async-start | bytes 131072 | tf_op jit(solution)/shard_map/all_to_all | solution.py:225
  111.4 4.6 %collective-permute-start.26 = (f32[64,128]{1,0:T(8,128)S(1)}, f32[64,128]{1,0:T(8,128)S(1)}, u32[]{:S(2)}, u32[]{:S(2)}) collective-permute-start(f32[64,128]{1,0:T(8,128)S(1)} %get-tuple-element.105), channel_id=1, source_target_pairs={{0,4},{1,5},{2,6},{3,7},{4,0},{5,1},{6,2},{7,3},{8,12},{9,13},{10,... | collective-permute-start | bytes 98312 | tf_op jit(solution)/shard_map/ppermute | solution.py:70
  116.4 2.2 %collective-permute-done.26 = f32[64,128]{1,0:T(8,128)S(1)} collective-permute-done((f32[64,128]{1,0:T(8,128)S(1)}, f32[64,128]{1,0:T(8,128)S(1)}, u32[]{:S(2)}, u32[]{:S(2)}) %collective-permute-start.26) | collective-permute-done | bytes 32800 | tf_op jit(solution)/shard_map/ppermute | solution.py:70
  118.6 3.2 %all-to-all-done = f32[128,1,128]{2,1,0:T(1,128)S(1)} async-done(((f32[128,1,128]{2,1,0:T(1,128)}), f32[128,1,128]{2,1,0:T(1,128)S(1)}, u32[]{:S(2)}, u32[]{:S(2)}) %all-to-all-start) | async-done | bytes 65568 | tf_op jit(solution)/shard_map/all_to_all | solution.py:225
  121.8 0.6 reduce_sum.29
  123.4 1.0 broadcast_in_dim.14
  124.4 3.6 %all-to-all-start.1 = ((bf16[16,224,128]{2,1,0:T(8,128)(2,1)}), bf16[16,224,128]{2,1,0:T(8,128)(2,1)S(1)}, u32[]{:S(2)}, u32[]{:S(2)}) async-start(bf16[16,224,128]{2,1,0:T(8,128)(2,1)} %broadcast_in_dim.14), calls=%async_computation.1 | async-start | bytes 1835008 | tf_op jit(solution)/shard_map/all_to_all | solution.py:241
  128.5 1.8 %collective-permute-start.28 = (f32[128,128]{1,0:T(8,128)S(1)}, f32[128,128]{1,0:T(8,128)S(1)}, u32[]{:S(2)}, u32[]{:S(2)}) collective-permute-start(f32[128,128]{1,0:T(8,128)S(1)} %pad_maximum_fusion.21), channel_id=1, source_target_pairs={{0,2},{1,3},{2,4},{3,5},{4,6},{5,7},{6,0},{7,1},{8,10},{9,11},{10,... | collective-permute-start | bytes 196616 | tf_op jit(solution)/shard_map/ppermute | solution.py:66
  130.3 1.8 %collective-permute-start.29 = (f32[128,128]{1,0:T(8,128)S(1)}, f32[128,128]{1,0:T(8,128)S(1)}, u32[]{:S(2)}, u32[]{:S(2)}) collective-permute-start(f32[128,128]{1,0:T(8,128)S(1)} %pad_maximum_fusion.21), channel_id=1, source_target_pairs={{0,7},{1,0},{2,1},{3,2},{4,3},{5,4},{6,5},{7,6},{8,15},{9,8},{10,9... | collective-permute-start | bytes 196616 | tf_op jit(solution)/shard_map/ppermute | solution.py:66
  132.4 1.4 collective-permute-done.28
  133.9 1.2 collective-permute-done.29
  135.0 6.7 %all-to-all-done.1 = bf16[16,224,128]{2,1,0:T(8,128)(2,1)S(1)} async-done(((bf16[16,224,128]{2,1,0:T(8,128)(2,1)}), bf16[16,224,128]{2,1,0:T(8,128)(2,1)S(1)}, u32[]{:S(2)}, u32[]{:S(2)}) %all-to-all-start.1) | async-done | bytes 917536 | tf_op jit(solution)/shard_map/all_to_all | solution.py:241
  141.8 3.1 %collective-permute-start.30 = (bf16[16,224,128]{2,1,0:T(8,128)(2,1)S(1)}, bf16[16,224,128]{2,1,0:T(8,128)(2,1)S(1)}, u32[]{:S(2)}, u32[]{:S(2)}) collective-permute-start(bf16[16,224,128]{2,1,0:T(8,128)(2,1)S(1)} %all-to-all-done.1), channel_id=1, source_target_pairs={{0,8},{8,0},{1,9},{9,1},{2,10},{10,2},{3,11},{11,3},{4,12},{12,4},... | collective-permute-start | bytes 2752520 | tf_op jit(solution)/shard_map/ppermute | solution.py:62
  145.0 2.0 %collective-permute-done.30 = bf16[16,224,128]{2,1,0:T(8,128)(2,1)S(1)} collective-permute-done((bf16[16,224,128]{2,1,0:T(8,128)(2,1)S(1)}, bf16[16,224,128]{2,1,0:T(8,128)(2,1)S(1)}, u32[]{:S(2)}, u32[]{:S(2)}) %collective-permute-start.30) | collective-permute-done | bytes 917536 | tf_op jit(solution)/shard_map/ppermute | solution.py:62
  147.3 1.3 copy-done.2
  148.6 2.1 %fusion.1 = bf16[256,3584]{1,0:T(8,128)(2,1)} fusion(bf16[256,3584]{1,0:T(8,128)(2,1)S(1)} %bitcast.267, bf16[256,3584]{1,0:T(8,128)(2,1)S(1)} %copy-done.2, f32[256,256]{1,0:T(8,128)S(1)} %bitcast.271, f32[256,256]{1,0:T(8,128)S(1)} %bitcast.274, f32[256,256]{1,0:T(8,128)S(1)} %bitcast.273, f32[256,256]{1,0:T(8,128)S(1)} %bitcast.272), kind=kOutput, calls=%fused_computation.2 | convolution fusion | flops 474284032 | bytes 6553600 | tf_op jit(solution)/shard_map/dot_general | solution.py:252
  (105 shorter events, 8.2 us)
Async XLA Ops:
  1.9 6.8 %collective-permute-start.2 = (bf16[480,128]{1,0:T(8,128)(2,1)S(1)}, bf16[480,128]{1,0:T(8,128)(2,1)S(1)}, u32[]{:S(2)}, u32[]{:S(2)}) collective-permute-start(bf16[480,128]{1,0:T(8,128)(2,1)S(1)} %pad_maximum_fusion.20), channel_id=1, source_target_pairs={{0,48},{8,200},{16,0},{24,216},{32,16},{40,232},{48,32},{56,248},{... | collective-permute-start | bytes 368648 | tf_op jit(solution)/shard_map/factors_p/ppermute | solution.py:54
  5.5 5.5 %collective-permute-start.1 = (bf16[480,128]{1,0:T(8,128)(2,1)S(1)}, bf16[480,128]{1,0:T(8,128)(2,1)S(1)}, u32[]{:S(2)}, u32[]{:S(2)}) collective-permute-start(bf16[480,128]{1,0:T(8,128)(2,1)S(1)} %pad_maximum_fusion.20), channel_id=1, source_target_pairs={{0,32},{8,136},{16,48},{24,152},{32,0},{40,168},{48,16},{56,184},{... | collective-permute-start | bytes 368648 | tf_op jit(solution)/shard_map/factors_p/ppermute | solution.py:54
  5.8 6.5 %collective-permute-start = (bf16[480,128]{1,0:T(8,128)(2,1)S(1)}, bf16[480,128]{1,0:T(8,128)(2,1)S(1)}, u32[]{:S(2)}, u32[]{:S(2)}) collective-permute-start(bf16[480,128]{1,0:T(8,128)(2,1)S(1)} %pad_maximum_fusion.20), channel_id=1, source_target_pairs={{0,16},{8,72},{16,32},{24,88},{32,48},{40,104},{48,0},{56,120},{64... | collective-permute-start | bytes 368648 | tf_op jit(solution)/shard_map/factors_p/ppermute | solution.py:54
  12.6 7.7 %collective-permute-start.5 = (bf16[4,224,128]{2,1,0:T(8,128)(2,1)S(1)}, bf16[4,224,128]{2,1,0:T(8,128)(2,1)S(1)}, u32[]{:S(2)}, u32[]{:S(2)}) collective-permute-start(bf16[4,224,128]{2,1,0:T(8,128)(2,1)S(1)} %pad_maximum_fusion.16), channel_id=1, source_target_pairs={{0,192},{8,56},{16,208},{24,8},{32,224},{40,24},{48,240},{56,40},{... | collective-permute-start | bytes 688136 | tf_op jit(solution)/shard_map/a_q/ppermute | solution.py:58
  14.8 6.5 %collective-permute-start.4 = (bf16[4,224,128]{2,1,0:T(8,128)(2,1)S(1)}, bf16[4,224,128]{2,1,0:T(8,128)(2,1)S(1)}, u32[]{:S(2)}, u32[]{:S(2)}) collective-permute-start(bf16[4,224,128]{2,1,0:T(8,128)(2,1)S(1)} %pad_maximum_fusion.16), channel_id=1, source_target_pairs={{0,128},{8,40},{16,144},{24,56},{32,160},{40,8},{48,176},{56,24},{... | collective-permute-start | bytes 688136 | tf_op jit(solution)/shard_map/a_q/ppermute | solution.py:58
  15.3 8.6 %collective-permute-start.3 = (bf16[4,224,128]{2,1,0:T(8,128)(2,1)S(1)}, bf16[4,224,128]{2,1,0:T(8,128)(2,1)S(1)}, u32[]{:S(2)}, u32[]{:S(2)}) collective-permute-start(bf16[4,224,128]{2,1,0:T(8,128)(2,1)S(1)} %pad_maximum_fusion.16), channel_id=1, source_target_pairs={{0,64},{8,24},{16,80},{24,40},{32,96},{40,56},{48,112},{56,8},{64,... | collective-permute-start | bytes 688136 | tf_op jit(solution)/shard_map/a_q/ppermute | solution.py:58
  24.3 5.4 %collective-permute-start.6 = (bf16[4,4,224,128]{3,2,0,1:T(8,128)(2,1)S(1)}, bf16[4,4,224,128]{3,2,0,1:T(8,128)(2,1)S(1)}, u32[]{:S(2)}, u32[]{:S(2)}) collective-permute-start(bf16[4,4,224,128]{3,2,0,1:T(8,128)(2,1)S(1)} %pad_maximum_fusion.6), channel_id=1, source_target_pairs={{0,8},{8,0},{1,9},{9,1},{2,10},{10,2},{3,11},{11,3},{4,12},{12,4},... | collective-permute-start | bytes 2752520 | tf_op jit(solution)/shard_map/a_cores/ppermute | solution.py:62
  27.6 11.2 %collective-permute-start.11 = (bf16[4,256,128]{2,1,0:T(8,128)(2,1)S(1)}, bf16[4,256,128]{2,1,0:T(8,128)(2,1)S(1)}, u32[]{:S(2)}, u32[]{:S(2)}) collective-permute-start(bf16[4,256,128]{2,1,0:T(8,128)(2,1)S(1)} %pad_maximum_fusion.11), channel_id=1, source_target_pairs={{0,192},{8,56},{16,208},{24,8},{32,224},{40,24},{48,240},{56,40},{... | collective-permute-start | bytes 786440 | tf_op jit(solution)/shard_map/b_q/ppermute | solution.py:58
  27.9 10.9 %collective-permute-start.10 = (bf16[4,256,128]{2,1,0:T(8,128)(2,1)S(1)}, bf16[4,256,128]{2,1,0:T(8,128)(2,1)S(1)}, u32[]{:S(2)}, u32[]{:S(2)}) collective-permute-start(bf16[4,256,128]{2,1,0:T(8,128)(2,1)S(1)} %pad_maximum_fusion.11), channel_id=1, source_target_pairs={{0,128},{8,40},{16,144},{24,56},{32,160},{40,8},{48,176},{56,24},{... | collective-permute-start | bytes 786440 | tf_op jit(solution)/shard_map/b_q/ppermute | solution.py:58
  28.4 10.4 %collective-permute-start.9 = (bf16[4,256,128]{2,1,0:T(8,128)(2,1)S(1)}, bf16[4,256,128]{2,1,0:T(8,128)(2,1)S(1)}, u32[]{:S(2)}, u32[]{:S(2)}) collective-permute-start(bf16[4,256,128]{2,1,0:T(8,128)(2,1)S(1)} %pad_maximum_fusion.11), channel_id=1, source_target_pairs={{0,64},{8,24},{16,80},{24,40},{32,96},{40,56},{48,112},{56,8},{64,... | collective-permute-start | bytes 786440 | tf_op jit(solution)/shard_map/b_q/ppermute | solution.py:58
  29.9 2.0 %copy-start = (bf16[512,3584]{1,0:T(8,128)(2,1)S(1)}, bf16[512,3584]{1,0:T(8,128)(2,1)}, u32[]{:S(2)}) copy-start(bf16[512,3584]{1,0:T(8,128)(2,1)} %param.9) | copy-start | bytes 11010052
  33.0 10.3 %copy-start.4 = (f32[4,2,32,512]{3,2,1,0:T(8,128)}, f32[4,2,32,512]{3,2,1,0:T(8,128)S(1)}, u32[]{:S(2)}) copy-start(f32[4,2,32,512]{3,2,1,0:T(8,128)S(1)} %fusion.2) | copy-start | bytes 1572868
  33.1 9.2 %collective-permute-start.8 = (f32[4,32,256]{2,1,0:T(8,128)S(1)}, f32[4,32,256]{2,1,0:T(8,128)S(1)}, u32[]{:S(2)}, u32[]{:S(2)}) collective-permute-start(f32[4,32,256]{2,1,0:T(8,128)S(1)} %get-tuple-element.94), channel_id=1, source_target_pairs={{0,7},{1,2},{2,1},{3,4},{4,3},{5,6},{6,5},{7,0},{8,15},{9,10},{10,... | collective-permute-start | bytes 393224 | tf_op jit(solution)/shard_map/act_pairs/ppermute | solution.py:74
  38.8 4.4 %collective-permute-start.7 = (f32[4,32,256]{2,1,0:T(8,128)S(1)}, f32[4,32,256]{2,1,0:T(8,128)S(1)}, u32[]{:S(2)}, u32[]{:S(2)}) collective-permute-start(f32[4,32,256]{2,1,0:T(8,128)S(1)} %get-tuple-element.93), channel_id=1, source_target_pairs={{0,1},{1,0},{2,3},{3,2},{4,5},{5,4},{6,7},{7,6},{8,9},{9,8},{10,11... | collective-permute-start | bytes 393224 | tf_op jit(solution)/shard_map/act_pairs/ppermute | solution.py:70
  43.6 9.0 %collective-permute-start.12 = (bf16[4,4,256,128]{3,2,0,1:T(8,128)(2,1)S(1)}, bf16[4,4,256,128]{3,2,0,1:T(8,128)(2,1)S(1)}, u32[]{:S(2)}, u32[]{:S(2)}) collective-permute-start(bf16[4,4,256,128]{3,2,0,1:T(8,128)(2,1)S(1)} %copy.24), channel_id=1, source_target_pairs={{0,8},{8,0},{1,9},{9,1},{2,10},{10,2},{3,11},{11,3},{4,12},{12,4},... | collective-permute-start | bytes 3145736 | tf_op jit(solution)/shard_map/b_cores/ppermute | solution.py:62
  45.2 8.2 %slice-start = ((s8[8388608]{0:T(1024)(128)(4,1)}), s8[4194304]{0:T(1024)(128)(4,1)S(1)}, s32[]{:S(2)}) async-start(s8[8388608]{0:T(1024)(128)(4,1)} %bitcast.264), calls=%async_computation.2 | async-start | bytes 8388608
  46.3 11.8 %collective-permute-start.13 = (f32[32,512]{1,0:T(8,128)S(1)}, f32[32,512]{1,0:T(8,128)S(1)}, u32[]{:S(2)}, u32[]{:S(2)}) collective-permute-start(f32[32,512]{1,0:T(8,128)S(1)} %get-tuple-element.92), channel_id=1, source_target_pairs={{0,2},{1,3},{2,4},{3,5},{4,6},{5,7},{6,0},{7,1},{8,10},{9,11},{10,... | collective-permute-start | bytes 196616 | tf_op jit(solution)/shard_map/act_shifts/ppermute | solution.py:66
  46.9 11.3 %collective-permute-start.14 = (f32[32,512]{1,0:T(8,128)S(1)}, f32[32,512]{1,0:T(8,128)S(1)}, u32[]{:S(2)}, u32[]{:S(2)}) collective-permute-start(f32[32,512]{1,0:T(8,128)S(1)} %get-tuple-element.91), channel_id=1, source_target_pairs={{0,4},{1,5},{2,6},{3,7},{4,0},{5,1},{6,2},{7,3},{8,12},{9,13},{10,... | collective-permute-start | bytes 196616 | tf_op jit(solution)/shard_map/act_shifts/ppermute | solution.py:66
  49.7 8.5 %collective-permute-start.15 = (f32[32,512]{1,0:T(8,128)S(1)}, f32[32,512]{1,0:T(8,128)S(1)}, u32[]{:S(2)}, u32[]{:S(2)}) collective-permute-start(f32[32,512]{1,0:T(8,128)S(1)} %get-tuple-element.90), channel_id=1, source_target_pairs={{0,6},{1,7},{2,0},{3,1},{4,2},{5,3},{6,4},{7,5},{8,14},{9,15},{10,... | collective-permute-start | bytes 196616 | tf_op jit(solution)/shard_map/act_shifts/ppermute | solution.py:66
  53.0 2.2 %slice-start.1 = ((s8[8388608]{0:T(1024)(128)(4,1)}), s8[4194304]{0:T(1024)(128)(4,1)S(1)}, s32[]{:S(2)}) async-start(s8[8388608]{0:T(1024)(128)(4,1)} %bitcast.264), calls=%async_computation.3 | async-start | bytes 8388608
  58.2 5.1 %collective-permute-start.16 = (bf16[128,512]{1,0:T(8,128)(2,1)S(1)}, bf16[128,512]{1,0:T(8,128)(2,1)S(1)}, u32[]{:S(2)}, u32[]{:S(2)}) collective-permute-start(bf16[128,512]{1,0:T(8,128)(2,1)S(1)} %fusion.4), channel_id=1, source_target_pairs={{0,7},{1,2},{2,1},{3,4},{4,3},{5,6},{6,5},{7,0},{8,15},{9,10},{10,... | collective-permute-start | bytes 393224 | tf_op jit(solution)/shard_map/back_pairs/ppermute | solution.py:74
  60.2 3.4 %copy-start.1 = (bf16[512,3584]{1,0:T(8,128)(2,1)S(1)}, bf16[512,3584]{1,0:T(8,128)(2,1)}, u32[]{:S(2)}) copy-start(bf16[512,3584]{1,0:T(8,128)(2,1)} %param.9) | copy-start | bytes 11010052
  64.2 6.6 %collective-permute-start.17 = (f32[128,3584]{1,0:T(8,128)S(1)}, f32[128,3584]{1,0:T(8,128)}, u32[]{:S(2)}, u32[]{:S(2)}) collective-permute-start(f32[128,3584]{1,0:T(8,128)S(1)} %fusion.56), channel_id=1, source_target_pairs={{0,8},{8,0},{1,9},{9,1},{2,10},{10,2},{3,11},{11,3},{4,12},{12,4},... | collective-permute-start | bytes 5505032 | tf_op jit(solution)/shard_map/grad_a_cores/ppermute | solution.py:62
  66.8 3.9 %collective-permute-start.18 = (f32[4,4,64,128]{3,2,1,0:T(8,128)S(1)}, f32[4,4,64,128]{3,2,1,0:T(8,128)S(1)}, u32[]{:S(2)}, u32[]{:S(2)}) collective-permute-start(f32[4,4,64,128]{3,2,1,0:T(8,128)S(1)} %get-tuple-element.64), channel_id=1, source_target_pairs={{0,8},{8,0},{1,9},{9,1},{2,10},{10,2},{3,11},{11,3},{4,12},{12,4},... | collective-permute-start | bytes 1572872 | tf_op jit(solution)/shard_map/grad_b_cores/ppermute | solution.py:62
  72.6 9.1 %collective-permute-start.21 = (f32[4,288,128]{2,1,0:T(8,128)S(1)}, f32[4,288,128]{2,1,0:T(8,128)S(1)}, u32[]{:S(2)}, u32[]{:S(2)}) collective-permute-start(f32[4,288,128]{2,1,0:T(8,128)S(1)} %maximum_maximum_fusion.2), channel_id=1, source_target_pairs={{0,48},{8,200},{16,0},{24,216},{32,16},{40,232},{48,32},{56,248},{... | collective-permute-start | bytes 1769480 | tf_op jit(solution)/shard_map/grads_p/ppermute | solution.py:54
  74.2 10.7 %collective-permute-start.20 = (f32[4,288,128]{2,1,0:T(8,128)S(1)}, f32[4,288,128]{2,1,0:T(8,128)S(1)}, u32[]{:S(2)}, u32[]{:S(2)}) collective-permute-start(f32[4,288,128]{2,1,0:T(8,128)S(1)} %maximum_maximum_fusion.1), channel_id=1, source_target_pairs={{0,32},{8,136},{16,48},{24,152},{32,0},{40,168},{48,16},{56,184},{... | collective-permute-start | bytes 1769480 | tf_op jit(solution)/shard_map/grads_p/ppermute | solution.py:54
  75.8 15.3 %collective-permute-start.19 = (f32[4,288,128]{2,1,0:T(8,128)S(1)}, f32[4,288,128]{2,1,0:T(8,128)S(1)}, u32[]{:S(2)}, u32[]{:S(2)}) collective-permute-start(f32[4,288,128]{2,1,0:T(8,128)S(1)} %maximum_maximum_fusion), channel_id=1, source_target_pairs={{0,16},{8,72},{16,32},{24,88},{32,48},{40,104},{48,0},{56,120},{64... | collective-permute-start | bytes 1769480 | tf_op jit(solution)/shard_map/grads_p/ppermute | solution.py:54
  91.2 24.8 %copy-start.3 = (f32[256,256]{1,0:T(8,128)S(1)}, f32[256,256]{1,0:T(8,128)}, u32[]{:S(2)}) copy-start(f32[256,256]{1,0:T(8,128)} %param.15) | copy-start | bytes 786436
  91.2 24.9 %copy-start.6 = (f32[256,256]{1,0:T(8,128)S(1)}, f32[256,256]{1,0:T(8,128)}, u32[]{:S(2)}) copy-start(f32[256,256]{1,0:T(8,128)} %param.16) | copy-start | bytes 786436
  91.3 24.9 %copy-start.7 = (f32[256,256]{1,0:T(8,128)S(1)}, f32[256,256]{1,0:T(8,128)}, u32[]{:S(2)}) copy-start(f32[256,256]{1,0:T(8,128)} %param.17) | copy-start | bytes 786436
  91.3 31.9 %copy-start.5 = (f32[8,3584]{1,0:T(8,128)S(1)}, f32[8,3584]{1,0:T(8,128)}, u32[]{:S(2)}) copy-start(f32[8,3584]{1,0:T(8,128)} %param.12) | copy-start | bytes 344068
  91.3 31.9 %copy-start.8 = (f32[8,3584]{1,0:T(8,128)S(1)}, f32[8,3584]{1,0:T(8,128)}, u32[]{:S(2)}) copy-start(f32[8,3584]{1,0:T(8,128)} %param.14) | copy-start | bytes 344068
  91.4 31.9 %copy-start.9 = (f32[8,3584]{1,0:T(8,128)S(1)}, f32[8,3584]{1,0:T(8,128)}, u32[]{:S(2)}) copy-start(f32[8,3584]{1,0:T(8,128)} %param.13) | copy-start | bytes 344068
  91.4 4.4 %collective-permute-start.24 = (f32[288,128]{1,0:T(8,128)S(1)}, f32[288,128]{1,0:T(8,128)S(1)}, u32[]{:S(2)}, u32[]{:S(2)}) collective-permute-start(f32[288,128]{1,0:T(8,128)S(1)} %get-tuple-element.78), channel_id=1, source_target_pairs={{0,192},{8,56},{16,208},{24,8},{32,224},{40,24},{48,240},{56,40},{... | collective-permute-start | bytes 442376 | tf_op jit(solution)/shard_map/grads_q/ppermute | solution.py:58
  91.8 5.6 %collective-permute-start.23 = (f32[288,128]{1,0:T(8,128)S(1)}, f32[288,128]{1,0:T(8,128)S(1)}, u32[]{:S(2)}, u32[]{:S(2)}) collective-permute-start(f32[288,128]{1,0:T(8,128)S(1)} %get-tuple-element.79), channel_id=1, source_target_pairs={{0,128},{8,40},{16,144},{24,56},{32,160},{40,8},{48,176},{56,24},{... | collective-permute-start | bytes 442376 | tf_op jit(solution)/shard_map/grads_q/ppermute | solution.py:58
  93.1 6.1 %collective-permute-start.22 = (f32[288,128]{1,0:T(8,128)S(1)}, f32[288,128]{1,0:T(8,128)S(1)}, u32[]{:S(2)}, u32[]{:S(2)}) collective-permute-start(f32[288,128]{1,0:T(8,128)S(1)} %get-tuple-element.77), channel_id=1, source_target_pairs={{0,64},{8,24},{16,80},{24,40},{32,96},{40,56},{48,112},{56,8},{64,... | collective-permute-start | bytes 442376 | tf_op jit(solution)/shard_map/grads_q/ppermute | solution.py:58
  99.3 3.8 %collective-permute-start.25 = (f32[8,128]{1,0:T(8,128)S(1)}, f32[8,128]{1,0:T(8,128)S(1)}, u32[]{:S(2)}, u32[]{:S(2)}) collective-permute-start(f32[8,128]{1,0:T(8,128)S(1)} %slice.94), channel_id=1, source_target_pairs={{0,8},{8,0},{1,9},{9,1},{2,10},{10,2},{3,11},{11,3},{4,12},{12,4},... | collective-permute-start | bytes 12296 | tf_op jit(solution)/shard_map/ppermute | solution.py:62
  103.8 18.0 %all-to-all-start = ((f32[128,1,128]{2,1,0:T(1,128)}), f32[128,1,128]{2,1,0:T(1,128)S(1)}, u32[]{:S(2)}, u32[]{:S(2)}) async-start(f32[128,1,128]{2,1,0:T(1,128)} %broadcast_in_dim.13), calls=%async_computation | async-start | bytes 131072 | tf_op jit(solution)/shard_map/all_to_all | solution.py:225
  111.4 7.2 %collective-permute-start.26 = (f32[64,128]{1,0:T(8,128)S(1)}, f32[64,128]{1,0:T(8,128)S(1)}, u32[]{:S(2)}, u32[]{:S(2)}) collective-permute-start(f32[64,128]{1,0:T(8,128)S(1)} %get-tuple-element.105), channel_id=1, source_target_pairs={{0,4},{1,5},{2,6},{3,7},{4,0},{5,1},{6,2},{7,3},{8,12},{9,13},{10,... | collective-permute-start | bytes 98312 | tf_op jit(solution)/shard_map/ppermute | solution.py:70
  124.4 17.4 %all-to-all-start.1 = ((bf16[16,224,128]{2,1,0:T(8,128)(2,1)}), bf16[16,224,128]{2,1,0:T(8,128)(2,1)S(1)}, u32[]{:S(2)}, u32[]{:S(2)}) async-start(bf16[16,224,128]{2,1,0:T(8,128)(2,1)} %broadcast_in_dim.14), calls=%async_computation.1 | async-start | bytes 1835008 | tf_op jit(solution)/shard_map/all_to_all | solution.py:241
  128.0 4.4 %collective-permute-start.27 = (f32[128,128]{1,0:T(8,128)S(1)}, f32[128,128]{1,0:T(8,128)S(1)}, u32[]{:S(2)}, u32[]{:S(2)}) collective-permute-start(f32[128,128]{1,0:T(8,128)S(1)} %pad_maximum_fusion.21), channel_id=1, source_target_pairs={{0,1},{1,2},{2,3},{3,4},{4,5},{5,6},{6,7},{7,0},{8,9},{9,10},{10,1... | collective-permute-start | bytes 196616 | tf_op jit(solution)/shard_map/ppermute | solution.py:66
  128.5 5.3 %collective-permute-start.28 = (f32[128,128]{1,0:T(8,128)S(1)}, f32[128,128]{1,0:T(8,128)S(1)}, u32[]{:S(2)}, u32[]{:S(2)}) collective-permute-start(f32[128,128]{1,0:T(8,128)S(1)} %pad_maximum_fusion.21), channel_id=1, source_target_pairs={{0,2},{1,3},{2,4},{3,5},{4,6},{5,7},{6,0},{7,1},{8,10},{9,11},{10,... | collective-permute-start | bytes 196616 | tf_op jit(solution)/shard_map/ppermute | solution.py:66
  130.3 4.7 %collective-permute-start.29 = (f32[128,128]{1,0:T(8,128)S(1)}, f32[128,128]{1,0:T(8,128)S(1)}, u32[]{:S(2)}, u32[]{:S(2)}) collective-permute-start(f32[128,128]{1,0:T(8,128)S(1)} %pad_maximum_fusion.21), channel_id=1, source_target_pairs={{0,7},{1,0},{2,1},{3,2},{4,3},{5,4},{6,5},{7,6},{8,15},{9,8},{10,9... | collective-permute-start | bytes 196616 | tf_op jit(solution)/shard_map/ppermute | solution.py:66
  141.8 5.2 %collective-permute-start.30 = (bf16[16,224,128]{2,1,0:T(8,128)(2,1)S(1)}, bf16[16,224,128]{2,1,0:T(8,128)(2,1)S(1)}, u32[]{:S(2)}, u32[]{:S(2)}) collective-permute-start(bf16[16,224,128]{2,1,0:T(8,128)(2,1)S(1)} %all-to-all-done.1), channel_id=1, source_target_pairs={{0,8},{8,0},{1,9},{9,1},{2,10},{10,2},{3,11},{11,3},{4,12},{12,4},... | collective-permute-start | bytes 2752520 | tf_op jit(solution)/shard_map/ppermute | solution.py:62
  147.1 1.5 copy-start.2

commit v3 on v2

--- a/solution.py
+++ b/solution.py
@@ -56,6 +56,11 @@
 
 def shift_q(v, k):
     return lax.ppermute(v, DP, plane_pairs(False, k))
+
+
+def shifts(shift, v):
+    one, three, two = (shift(v, k) for k in (1, 3, 2))
+    return jnp.stack([v, one, two, three])
 
 
 def swap_core(v):
@@ -140,19 +145,19 @@
     b_block = lax.dynamic_slice_in_dim(right_lowrank_factor, (z % 2) * 128, 128, 1)
     block = jnp.concatenate([tiles(left_lowrank_factor), b_block], axis=0).astype(bf16)
     with jax.named_scope("factors_p"):
-        stack = jnp.stack([block] + [shift_p(block, k) for k in (1, 2, 3)])
+        stack = shifts(shift_p, block)
         a_stack = by_offset(stack[:, :224], p)
         b_stack = by_offset(stack[:, 224:], p)
         tokens, grads, base = input_token_rows, output_gradient_rows, frozen_base_matrix
         a_stack, b_stack = lax.optimization_barrier((a_stack, b_stack))
     with jax.named_scope("a_q"):
-        a_stack = jnp.stack([a_stack] + [shift_q(a_stack, k) for k in (1, 2, 3)])
+        a_stack = shifts(shift_q, a_stack)
     a_stack, b_stack = lax.optimization_barrier((a_stack, b_stack))
     with jax.named_scope("a_cores"):
         a_stack = by_offset(a_stack, q)
         a_other = swap_core(a_stack)
     with jax.named_scope("b_q"):
-        b_stack = jnp.stack([b_stack] + [shift_q(b_stack, k) for k in (1, 2, 3)])
+        b_stack = shifts(shift_q, b_stack)
     with jax.named_scope("act_terms"):
         a_rows = join_cores(a_stack, a_other, core).reshape(32, 224, 128)
         a_rows = untile(a_rows, 8, 3584).reshape(256, 3584)
@@ -209,12 +214,12 @@
         parts.append(jnp.concatenate([a_part, b_part], axis=1))
     with jax.named_scope("grads_p"):
         total = parts[0]
-        for k in (1, 2, 3):
+        for k in (1, 3, 2):
             total = total + shift_p(parts[k], k)
     with jax.named_scope("grads_q"):
         parts = [total[k] for k in range(4)]
         total = parts[0]
-        for k in (1, 2, 3):
+        for k in (1, 3, 2):
             total = total + shift_q(parts[k], k)
     grad_a = total[:224] * hidden_scale
     grad_b = total[224:] * rank_scale
@@ -223,10 +228,10 @@
     squares = jnp.broadcast_to(squares, (128, 128))
     squares = squares + jnp.broadcast_to(swap_core(squares[:8])[:1], (128, 128))
     squares = lax.all_to_all(squares, ("y", "x", "z"), 0, 0, tiled=True)
-    pair = flip(grad_b, "z", 8, 4)
+    pair = flip(grad_b, "z", 8, 1)
     right_t = (right_lowrank_factor.T, right_first_moment.T, right_second_moment.T)
     squares, pair, right_t = lax.optimization_barrier((squares, pair, right_t))
-    pair = join_ranks(grad_b, pair, z, 4)
+    pair = join_ranks(grad_b, pair, z, 1)
     squares = jnp.sum(squares, keepdims=True)
     clipper = jnp.minimum(1.0, clip_limit / (jnp.sqrt(squares) + norm_epsilon))
 
@@ -239,11 +244,11 @@
     copies = jnp.broadcast_to(new_a, (16, 224, 128))
     copies, pair = lax.optimization_barrier((copies, pair))
     mine = lax.all_to_all(copies, ("y", "x"), 0, 0, tiled=True)
-    pairs = [pair, shift_z(pair, 1), shift_z(pair, 2), shift_z(pair, -1)]
+    pairs = [pair] + [shift_z(pair, 2 * k) for k in (1, 2, 3)]
     mine, pairs = lax.optimization_barrier((mine, pairs))
     other = swap_core(mine)
-    whole_grad_b = by_offset(jnp.stack(pairs), z % 4).reshape(4, 2, 64, 128).swapaxes(0, 1)
-    whole_grad_b = untile(whole_grad_b.reshape(8, 64, 128), 32, 256).reshape(256, 256)
+    whole_grad_b = by_offset(jnp.stack(pairs), z // 2).reshape(8, 64, 128)
+    whole_grad_b = untile(whole_grad_b, 32, 256).reshape(256, 256)
     new_b = moment_update_step(
         *right_t, clipper * whole_grad_b
     ).astype(bf16)

time: 151 us -> 150 us (level)
  starting transfers between devices: 61.6 us -> 59.6 us
    all_to_all x1, waiting for transfers between devices: 6.74 us -> 2.43 us  [local(): mine = lax.all_to_all(copies, ('y', 'x'), 0, 0, tiled=True)]
    ppermute x6, waiting for transfers between devices: 2.99 us -> 7.23 us  [shift_z(): return lax.ppermute(v, 'z', [(i, (i + k) % 8) for i in range(8)])]
    ppermute x2, starting transfers between devices: 4.57 us -> 0.66 us  [flip(): return lax.ppermute(v, axis, [(i, i ^ bit) for i in range(n)])]
    all_to_all x1, waiting for transfers between devices: 3.25 us -> 7.04 us  [local(): squares = lax.all_to_all(squares, ('y', 'x', 'z'), 0, 0, tiled=True)]
    ppermute x6, waiting for transfers between devices: 19.3 us -> 17.1 us  [shift_p(): return lax.ppermute(v, DP, plane_pairs(True, k))]
  transfers between devices with their start and end apart: 33 -> 33, of which waited for: 26 -> 24; matrix products, arithmetic and copies ran while one was open for 8% -> 8% of each run, Pallas kernels for 0% -> 0%
where the time goes in v3:
time: 150 us
  waiting for transfers between devices  60.9 us (41%)
  starting transfers between devices  59.6 us (40%)
  matrix products  11 us (7%)
  local copies, waits for them, and re-layouts  9.84 us (7%)
  other arithmetic  7.15 us (5%)
    ppermute x6, waiting for transfers between devices, shift_p(): return lax.ppermute(v, DP, plane_pairs(True, k))  17.1 us
    ppermute x6, starting transfers between devices, swap_core(): return lax.ppermute(v, 'core', [(0, 1), (1, 0)])  14.6 us
    ppermute x9, waiting for transfers between devices, shift_q(): return lax.ppermute(v, DP, plane_pairs(False, k))  13 us
    ppermute x6, starting transfers between devices, shift_z(): return lax.ppermute(v, 'z', [(i, (i + k) % 8) for i in range(8)])  10.3 us
    ppermute x6, starting transfers between devices, shift_p(): return lax.ppermute(v, DP, plane_pairs(True, k))  9.33 us
    all_to_all x1, starting transfers between devices, local(): squares = lax.all_to_all(squares, ('y', 'x', 'z'), 0, 0, tiled=True)  7.55 us
    ppermute x9, starting transfers between devices, shift_q(): return lax.ppermute(v, DP, plane_pairs(False, k))  7.33 us
    ppermute x6, waiting for transfers between devices, shift_z(): return lax.ppermute(v, 'z', [(i, (i + k) % 8) for i in range(8)])  7.23 us
  transfers between devices with their start and end apart: 33, of which 24 were waited for; matrix products, arithmetic and copies ran while one was open for 8% of the time, Pallas kernels for 0%

profile of v3, /device:TPU:1, one launch (start us, length us, event | category | flops | bytes accessed | tf_op | source)
XLA Modules:
  0.0 149.9 jit_solution(17839268817559443575)
XLA Ops:
  0.0 0.9 fusion.44
  0.9 0.9 dynamic-slice_convert_fusion
  1.9 3.6 %collective-permute-start.2 = (bf16[480,128]{1,0:T(8,128)(2,1)S(1)}, bf16[480,128]{1,0:T(8,128)(2,1)S(1)}, u32[]{:S(2)}, u32[]{:S(2)}) collective-permute-start(bf16[480,128]{1,0:T(8,128)(2,1)S(1)} %pad_maximum_fusion.20), channel_id=1, source_target_pairs={{0,48},{8,200},{16,0},{24,216},{32,16},{40,232},{48,32},{56,248},{... | collective-permute-start | bytes 368648 | tf_op jit(solution)/shard_map/factors_p/ppermute | solution.py:54
  5.8 0.7 collective-permute-start
  6.5 0.9 fusion.67
  7.4 1.2 collective-permute-done.2
  8.6 2.4 %collective-permute-done.1 = bf16[480,128]{1,0:T(8,128)(2,1)S(1)} collective-permute-done((bf16[480,128]{1,0:T(8,128)(2,1)S(1)}, bf16[480,128]{1,0:T(8,128)(2,1)S(1)}, u32[]{:S(2)}, u32[]{:S(2)}) %collective-permute-start.1) | collective-permute-done | bytes 122912 | tf_op jit(solution)/shard_map/factors_p/ppermute | solution.py:54
  11.0 1.3 collective-permute-done
  12.6 2.3 %collective-permute-start.5 = (bf16[4,224,128]{2,1,0:T(8,128)(2,1)S(1)}, bf16[4,224,128]{2,1,0:T(8,128)(2,1)S(1)}, u32[]{:S(2)}, u32[]{:S(2)}) collective-permute-start(bf16[4,224,128]{2,1,0:T(8,128)(2,1)S(1)} %pad_maximum_fusion.16), channel_id=1, source_target_pairs={{0,192},{8,56},{16,208},{24,8},{32,224},{40,24},{48,240},{56,40},{... | collective-permute-start | bytes 688136 | tf_op jit(solution)/shard_map/a_q/ppermute | solution.py:58
  15.3 0.6 collective-permute-start.3
  15.9 4.3 %collective-permute-done.5 = bf16[4,224,128]{2,1,0:T(8,128)(2,1)S(1)} collective-permute-done((bf16[4,224,128]{2,1,0:T(8,128)(2,1)S(1)}, bf16[4,224,128]{2,1,0:T(8,128)(2,1)S(1)}, u32[]{:S(2)}, u32[]{:S(2)}) %collective-permute-start.5) | collective-permute-done | bytes 229408 | tf_op jit(solution)/shard_map/a_q/ppermute | solution.py:58
  20.2 1.1 collective-permute-done.4
  21.3 2.6 %collective-permute-done.3 = bf16[4,224,128]{2,1,0:T(8,128)(2,1)S(1)} collective-permute-done((bf16[4,224,128]{2,1,0:T(8,128)(2,1)S(1)}, bf16[4,224,128]{2,1,0:T(8,128)(2,1)S(1)}, u32[]{:S(2)}, u32[]{:S(2)}) %collective-permute-start.3) | collective-permute-done | bytes 229408 | tf_op jit(solution)/shard_map/a_q/ppermute | solution.py:58
  24.3 3.3 %collective-permute-start.6 = (bf16[4,4,224,128]{3,2,0,1:T(8,128)(2,1)S(1)}, bf16[4,4,224,128]{3,2,0,1:T(8,128)(2,1)S(1)}, u32[]{:S(2)}, u32[]{:S(2)}) collective-permute-start(bf16[4,4,224,128]{3,2,0,1:T(8,128)(2,1)S(1)} %pad_maximum_fusion.6), channel_id=1, source_target_pairs={{0,8},{8,0},{1,9},{9,1},{2,10},{10,2},{3,11},{11,3},{4,12},{12,4},... | collective-permute-start | bytes 2752520 | tf_op jit(solution)/shard_map/a_cores/ppermute | solution.py:67
  28.4 0.7 collective-permute-start.9
  29.1 0.6 collective-permute-done.6
  30.1 1.8 %copy-done = bf16[512,3584]{1,0:T(8,128)(2,1)S(1)} copy-done((bf16[512,3584]{1,0:T(8,128)(2,1)S(1)}, bf16[512,3584]{1,0:T(8,128)(2,1)}, u32[]{:S(2)}) %copy-start) | copy-done | bytes 3670040
  31.9 1.1 fusion.2
  33.1 5.7 %collective-permute-start.8 = (f32[4,32,256]{2,1,0:T(8,128)S(1)}, f32[4,32,256]{2,1,0:T(8,128)S(1)}, u32[]{:S(2)}, u32[]{:S(2)}) collective-permute-start(f32[4,32,256]{2,1,0:T(8,128)S(1)} %get-tuple-element.94), channel_id=1, source_target_pairs={{0,7},{1,2},{2,1},{3,4},{4,3},{5,6},{6,5},{7,0},{8,15},{9,10},{10,... | collective-permute-start | bytes 393224 | tf_op jit(solution)/shard_map/act_pairs/ppermute | solution.py:79
  38.9 3.4 %collective-permute-done.8 = f32[4,32,256]{2,1,0:T(8,128)S(1)} collective-permute-done((f32[4,32,256]{2,1,0:T(8,128)S(1)}, f32[4,32,256]{2,1,0:T(8,128)S(1)}, u32[]{:S(2)}, u32[]{:S(2)}) %collective-permute-start.8) | collective-permute-done | bytes 131104 | tf_op jit(solution)/shard_map/act_pairs/ppermute | solution.py:79
  42.3 0.8 collective-permute-done.7
  43.6 1.6 %collective-permute-start.12 = (bf16[4,4,256,128]{3,2,0,1:T(8,128)(2,1)S(1)}, bf16[4,4,256,128]{3,2,0,1:T(8,128)(2,1)S(1)}, u32[]{:S(2)}, u32[]{:S(2)}) collective-permute-start(bf16[4,4,256,128]{3,2,0,1:T(8,128)(2,1)S(1)} %copy.25), channel_id=1, source_target_pairs={{0,8},{8,0},{1,9},{9,1},{2,10},{10,2},{3,11},{11,3},{4,12},{12,4},... | collective-permute-start | bytes 3145736 | tf_op jit(solution)/shard_map/b_cores/ppermute | solution.py:67
  45.2 1.1 bitcast_add_fusion
  46.9 2.8 %collective-permute-start.14 = (f32[32,512]{1,0:T(8,128)S(1)}, f32[32,512]{1,0:T(8,128)S(1)}, u32[]{:S(2)}, u32[]{:S(2)}) collective-permute-start(f32[32,512]{1,0:T(8,128)S(1)} %get-tuple-element.91), channel_id=1, source_target_pairs={{0,4},{1,5},{2,6},{3,7},{4,0},{5,1},{6,2},{7,3},{8,12},{9,13},{10,... | collective-permute-start | bytes 196616 | tf_op jit(solution)/shard_map/act_shifts/ppermute | solution.py:71
  49.7 2.9 %collective-permute-start.15 = (f32[32,512]{1,0:T(8,128)S(1)}, f32[32,512]{1,0:T(8,128)S(1)}, u32[]{:S(2)}, u32[]{:S(2)}) collective-permute-start(f32[32,512]{1,0:T(8,128)S(1)} %get-tuple-element.90), channel_id=1, source_target_pairs={{0,6},{1,7},{2,0},{3,1},{4,2},{5,3},{6,4},{7,5},{8,14},{9,15},{10,... | collective-permute-start | bytes 196616 | tf_op jit(solution)/shard_map/act_shifts/ppermute | solution.py:71
  53.4 1.8 %slice-done.1 = s8[4194304]{0:T(1024)(128)(4,1)S(1)} async-done(((s8[8388608]{0:T(1024)(128)(4,1)}), s8[4194304]{0:T(1024)(128)(4,1)S(1)}, s32[]{:S(2)}) %slice-start.1) | async-done | bytes 4194328
  55.2 2.9 %fusion.4 = bf16[128,512]{1,0:T(8,128)(2,1)S(1)} fusion(bf16[8192,128]{1,0:T(8,128)(2,1)S(1)} %bitcast.263, bf16[512,8192]{1,0:T(8,128)(2,1)S(1)} %bitcast.262), kind=kOutput, calls=%fused_computation.9 | convolution fusion | flops 1073872896 | bytes 10616832 | tf_op jit(solution)/shard_map/back/dot_general | solution.py:183
  58.7 1.5 %fusion.54 = f32[32,8192]{1,0:T(8,128)S(1)} fusion(bf16[32,512]{1,0:T(8,128)(2,1)S(1)} %fusion.43, bf16[512,8192]{1,0:T(8,128)(2,1)S(1)} %bitcast.262), kind=kOutput, calls=%fused_computation.177 | convolution fusion | flops 268435456 | bytes 9469952 | tf_op jit(solution)/shard_map/grad_b_terms/dot_general | solution.py:192
  60.2 3.1 %collective-permute-done.16 = bf16[128,512]{1,0:T(8,128)(2,1)S(1)} collective-permute-done((bf16[128,512]{1,0:T(8,128)(2,1)S(1)}, bf16[128,512]{1,0:T(8,128)(2,1)S(1)}, u32[]{:S(2)}, u32[]{:S(2)}) %collective-permute-start.16) | collective-permute-done | bytes 131104 | tf_op jit(solution)/shard_map/back_pairs/ppermute | solution.py:79
  63.6 0.6 fusion.56
  64.2 2.3 %collective-permute-start.17 = (f32[128,3584]{1,0:T(8,128)S(1)}, f32[128,3584]{1,0:T(8,128)}, u32[]{:S(2)}, u32[]{:S(2)}) collective-permute-start(f32[128,3584]{1,0:T(8,128)S(1)} %fusion.56), channel_id=1, source_target_pairs={{0,8},{8,0},{1,9},{9,1},{2,10},{10,2},{3,11},{11,3},{4,12},{12,4},... | collective-permute-start | bytes 5505032 | tf_op jit(solution)/shard_map/grad_a_cores/ppermute | solution.py:67
  67.0 2.7 %fusion.55 = f32[128,3584]{1,0:T(8,128)S(1)} fusion(bf16[128,512]{1,0:T(8,128)(2,1)S(1)} %bitcast.275, bf16[512,3584]{1,0:T(8,128)(2,1)} %param.9), kind=kOutput, calls=%fused_computation.178 | convolution fusion | flops 469762048 | bytes 5636096 | tf_op jit(solution)/shard_map/grad_a_terms/dot_general | solution.py:200
  69.7 1.0 collective-permute-done.18
  70.9 1.7 %fusion.13 = (f32[4,224,128]{2,1,0:T(8,128)S(1)}, f32[4,224,128]{2,1,0:T(8,128)S(1)}, f32[4,224,128]{2,1,0:T(8,128)S(1)}, f32[4,224,128]{2,1,0:T(8,128)S(1)}) fusion(f32[128,3584]{1,0:T(8,128)} %collective-permute-done.17, f32[128,3584]{1,0:T(8,128)S(1)} %fusion.55), kind=kLoop, calls=%fused_computation.38 | loop fusion | flops 458752 | bytes 5505024 | tf_op jit(solution)/shard_map/reshape | solution.py:212
  72.6 3.0 %collective-permute-start.21 = (f32[4,288,128]{2,1,0:T(8,128)S(1)}, f32[4,288,128]{2,1,0:T(8,128)S(1)}, u32[]{:S(2)}, u32[]{:S(2)}) collective-permute-start(f32[4,288,128]{2,1,0:T(8,128)S(1)} %maximum_maximum_fusion.2), channel_id=1, source_target_pairs={{0,32},{8,136},{16,48},{24,152},{32,0},{40,168},{48,16},{56,184},{... | collective-permute-start | bytes 1769480 | tf_op jit(solution)/shard_map/grads_p/ppermute | solution.py:54
  76.1 1.2 collective-permute-start.19
  77.4 5.9 %collective-permute-done.21 = f32[4,288,128]{2,1,0:T(8,128)S(1)} collective-permute-done((f32[4,288,128]{2,1,0:T(8,128)S(1)}, f32[4,288,128]{2,1,0:T(8,128)S(1)}, u32[]{:S(2)}, u32[]{:S(2)}) %collective-permute-start.21) | collective-permute-done | bytes 589856 | tf_op jit(solution)/shard_map/grads_p/ppermute | solution.py:54
  83.3 5.4 %collective-permute-done.20 = f32[4,288,128]{2,1,0:T(8,128)S(1)} collective-permute-done((f32[4,288,128]{2,1,0:T(8,128)S(1)}, f32[4,288,128]{2,1,0:T(8,128)S(1)}, u32[]{:S(2)}, u32[]{:S(2)}) %collective-permute-start.20) | collective-permute-done | bytes 589856 | tf_op jit(solution)/shard_map/grads_p/ppermute | solution.py:54
  88.7 0.9 collective-permute-done.19
  89.8 1.0 collective-permute-start.24
  90.8 0.6 collective-permute-start.23
  91.4 0.9 collective-permute-start.22
  92.3 3.1 %collective-permute-done.24 = f32[288,128]{1,0:T(8,128)S(1)} collective-permute-done((f32[288,128]{1,0:T(8,128)S(1)}, f32[288,128]{1,0:T(8,128)S(1)}, u32[]{:S(2)}, u32[]{:S(2)}) %collective-permute-start.24) | collective-permute-done | bytes 147488 | tf_op jit(solution)/shard_map/grads_q/ppermute | solution.py:58
  95.4 1.8 %collective-permute-done.22 = f32[288,128]{1,0:T(8,128)S(1)} collective-permute-done((f32[288,128]{1,0:T(8,128)S(1)}, f32[288,128]{1,0:T(8,128)S(1)}, u32[]{:S(2)}, u32[]{:S(2)}) %collective-permute-start.22) | collective-permute-done | bytes 147488 | tf_op jit(solution)/shard_map/grads_q/ppermute | solution.py:58
  97.4 4.1 %collective-permute-start.25 = (f32[8,128]{1,0:T(8,128)S(1)}, f32[8,128]{1,0:T(8,128)S(1)}, u32[]{:S(2)}, u32[]{:S(2)}) collective-permute-start(f32[8,128]{1,0:T(8,128)S(1)} %slice.94), channel_id=1, source_target_pairs={{0,8},{8,0},{1,9},{9,1},{2,10},{10,2},{3,11},{11,3},{4,12},{12,4},... | collective-permute-start | bytes 12296 | tf_op jit(solution)/shard_map/ppermute | solution.py:67
  101.5 0.8 collective-permute-done.25
  102.4 0.7 broadcast_in_dim.13
  103.0 7.6 %all-to-all-start = ((f32[128,1,128]{2,1,0:T(1,128)}), f32[128,1,128]{2,1,0:T(1,128)S(1)}, u32[]{:S(2)}, u32[]{:S(2)}) async-start(f32[128,1,128]{2,1,0:T(1,128)} %broadcast_in_dim.13), calls=%async_computation | async-start | bytes 131072 | tf_op jit(solution)/shard_map/all_to_all | solution.py:230
  110.6 0.7 collective-permute-start.26
  111.7 2.4 %collective-permute-done.26 = f32[64,128]{1,0:T(8,128)S(1)} collective-permute-done((f32[64,128]{1,0:T(8,128)S(1)}, f32[64,128]{1,0:T(8,128)S(1)}, u32[]{:S(2)}, u32[]{:S(2)}) %collective-permute-start.26) | collective-permute-done | bytes 32800 | tf_op jit(solution)/shard_map/ppermute | solution.py:75
  114.0 7.0 %all-to-all-done = f32[128,1,128]{2,1,0:T(1,128)S(1)} async-done(((f32[128,1,128]{2,1,0:T(1,128)}), f32[128,1,128]{2,1,0:T(1,128)S(1)}, u32[]{:S(2)}, u32[]{:S(2)}) %all-to-all-start) | async-done | bytes 65568 | tf_op jit(solution)/shard_map/all_to_all | solution.py:230
  121.1 0.6 reduce_sum.29
  122.6 1.0 broadcast_in_dim.14
  123.6 3.6 %all-to-all-start.1 = ((bf16[16,224,128]{2,1,0:T(8,128)(2,1)}), bf16[16,224,128]{2,1,0:T(8,128)(2,1)S(1)}, u32[]{:S(2)}, u32[]{:S(2)}) async-start(bf16[16,224,128]{2,1,0:T(8,128)(2,1)} %broadcast_in_dim.14), calls=%async_computation.1 | async-start | bytes 1835008 | tf_op jit(solution)/shard_map/all_to_all | solution.py:246
  127.7 2.1 %collective-permute-start.28 = (f32[128,128]{1,0:T(8,128)S(1)}, f32[128,128]{1,0:T(8,128)S(1)}, u32[]{:S(2)}, u32[]{:S(2)}) collective-permute-start(f32[128,128]{1,0:T(8,128)S(1)} %pad_maximum_fusion.21), channel_id=1, source_target_pairs={{0,4},{1,5},{2,6},{3,7},{4,0},{5,1},{6,2},{7,3},{8,12},{9,13},{10,... | collective-permute-start | bytes 196616 | tf_op jit(solution)/shard_map/ppermute | solution.py:71
  129.8 1.6 %collective-permute-start.29 = (f32[128,128]{1,0:T(8,128)S(1)}, f32[128,128]{1,0:T(8,128)S(1)}, u32[]{:S(2)}, u32[]{:S(2)}) collective-permute-start(f32[128,128]{1,0:T(8,128)S(1)} %pad_maximum_fusion.21), channel_id=1, source_target_pairs={{0,6},{1,7},{2,0},{3,1},{4,2},{5,3},{6,4},{7,5},{8,14},{9,15},{10,... | collective-permute-start | bytes 196616 | tf_op jit(solution)/shard_map/ppermute | solution.py:71
  131.4 1.5 collective-permute-done.27
  132.8 2.3 %collective-permute-done.28 = f32[128,128]{1,0:T(8,128)S(1)} collective-permute-done((f32[128,128]{1,0:T(8,128)S(1)}, f32[128,128]{1,0:T(8,128)S(1)}, u32[]{:S(2)}, u32[]{:S(2)}) %collective-permute-start.28) | collective-permute-done | bytes 65568 | tf_op jit(solution)/shard_map/ppermute | solution.py:71
  135.2 3.4 %collective-permute-done.29 = f32[128,128]{1,0:T(8,128)S(1)} collective-permute-done((f32[128,128]{1,0:T(8,128)S(1)}, f32[128,128]{1,0:T(8,128)S(1)}, u32[]{:S(2)}, u32[]{:S(2)}) %collective-permute-start.29) | collective-permute-done | bytes 65568 | tf_op jit(solution)/shard_map/ppermute | solution.py:71
  138.6 2.4 %all-to-all-done.1 = bf16[16,224,128]{2,1,0:T(8,128)(2,1)S(1)} async-done(((bf16[16,224,128]{2,1,0:T(8,128)(2,1)}), bf16[16,224,128]{2,1,0:T(8,128)(2,1)S(1)}, u32[]{:S(2)}, u32[]{:S(2)}) %all-to-all-start.1) | async-done | bytes 917536 | tf_op jit(solution)/shard_map/all_to_all | solution.py:246
  141.0 3.1 %collective-permute-start.30 = (bf16[16,224,128]{2,1,0:T(8,128)(2,1)S(1)}, bf16[16,224,128]{2,1,0:T(8,128)(2,1)S(1)}, u32[]{:S(2)}, u32[]{:S(2)}) collective-permute-start(bf16[16,224,128]{2,1,0:T(8,128)(2,1)S(1)} %all-to-all-done.1), channel_id=1, source_target_pairs={{0,8},{8,0},{1,9},{9,1},{2,10},{10,2},{3,11},{11,3},{4,12},{12,4},... | collective-permute-start | bytes 2752520 | tf_op jit(solution)/shard_map/ppermute | solution.py:67
  144.2 2.0 %collective-permute-done.30 = bf16[16,224,128]{2,1,0:T(8,128)(2,1)S(1)} collective-permute-done((bf16[16,224,128]{2,1,0:T(8,128)(2,1)S(1)}, bf16[16,224,128]{2,1,0:T(8,128)(2,1)S(1)}, u32[]{:S(2)}, u32[]{:S(2)}) %collective-permute-start.30) | collective-permute-done | bytes 917536 | tf_op jit(solution)/shard_map/ppermute | solution.py:67
  146.6 1.3 copy-done.2
  147.9 2.1 %fusion.1 = bf16[256,3584]{1,0:T(8,128)(2,1)} fusion(bf16[256,3584]{1,0:T(8,128)(2,1)S(1)} %bitcast.264, bf16[256,3584]{1,0:T(8,128)(2,1)S(1)} %copy-done.2, f32[256,256]{1,0:T(8,128)S(1)} %bitcast.269, f32[256,256]{1,0:T(8,128)S(1)} %bitcast.268, f32[256,256]{1,0:T(8,128)S(1)} %bitcast.271, f32[256,256]{1,0:T(8,128)S(1)} %bitcast.270), kind=kOutput, calls=%fused_computation.2 | convolution fusion | flops 474284032 | bytes 6553600 | tf_op jit(solution)/shard_map/dot_general | solution.py:257
  (104 shorter events, 7.8 us)
Async XLA Ops:
  1.9 6.8 %collective-permute-start.2 = (bf16[480,128]{1,0:T(8,128)(2,1)S(1)}, bf16[480,128]{1,0:T(8,128)(2,1)S(1)}, u32[]{:S(2)}, u32[]{:S(2)}) collective-permute-start(bf16[480,128]{1,0:T(8,128)(2,1)S(1)} %pad_maximum_fusion.20), channel_id=1, source_target_pairs={{0,48},{8,200},{16,0},{24,216},{32,16},{40,232},{48,32},{56,248},{... | collective-permute-start | bytes 368648 | tf_op jit(solution)/shard_map/factors_p/ppermute | solution.py:54
  5.5 5.5 %collective-permute-start.1 = (bf16[480,128]{1,0:T(8,128)(2,1)S(1)}, bf16[480,128]{1,0:T(8,128)(2,1)S(1)}, u32[]{:S(2)}, u32[]{:S(2)}) collective-permute-start(bf16[480,128]{1,0:T(8,128)(2,1)S(1)} %pad_maximum_fusion.20), channel_id=1, source_target_pairs={{0,32},{8,136},{16,48},{24,152},{32,0},{40,168},{48,16},{56,184},{... | collective-permute-start | bytes 368648 | tf_op jit(solution)/shard_map/factors_p/ppermute | solution.py:54
  5.8 6.5 %collective-permute-start = (bf16[480,128]{1,0:T(8,128)(2,1)S(1)}, bf16[480,128]{1,0:T(8,128)(2,1)S(1)}, u32[]{:S(2)}, u32[]{:S(2)}) collective-permute-start(bf16[480,128]{1,0:T(8,128)(2,1)S(1)} %pad_maximum_fusion.20), channel_id=1, source_target_pairs={{0,16},{8,72},{16,32},{24,88},{32,48},{40,104},{48,0},{56,120},{64... | collective-permute-start | bytes 368648 | tf_op jit(solution)/shard_map/factors_p/ppermute | solution.py:54
  12.6 7.7 %collective-permute-start.5 = (bf16[4,224,128]{2,1,0:T(8,128)(2,1)S(1)}, bf16[4,224,128]{2,1,0:T(8,128)(2,1)S(1)}, u32[]{:S(2)}, u32[]{:S(2)}) collective-permute-start(bf16[4,224,128]{2,1,0:T(8,128)(2,1)S(1)} %pad_maximum_fusion.16), channel_id=1, source_target_pairs={{0,192},{8,56},{16,208},{24,8},{32,224},{40,24},{48,240},{56,40},{... | collective-permute-start | bytes 688136 | tf_op jit(solution)/shard_map/a_q/ppermute | solution.py:58
  14.8 6.5 %collective-permute-start.4 = (bf16[4,224,128]{2,1,0:T(8,128)(2,1)S(1)}, bf16[4,224,128]{2,1,0:T(8,128)(2,1)S(1)}, u32[]{:S(2)}, u32[]{:S(2)}) collective-permute-start(bf16[4,224,128]{2,1,0:T(8,128)(2,1)S(1)} %pad_maximum_fusion.16), channel_id=1, source_target_pairs={{0,128},{8,40},{16,144},{24,56},{32,160},{40,8},{48,176},{56,24},{... | collective-permute-start | bytes 688136 | tf_op jit(solution)/shard_map/a_q/ppermute | solution.py:58
  15.3 8.6 %collective-permute-start.3 = (bf16[4,224,128]{2,1,0:T(8,128)(2,1)S(1)}, bf16[4,224,128]{2,1,0:T(8,128)(2,1)S(1)}, u32[]{:S(2)}, u32[]{:S(2)}) collective-permute-start(bf16[4,224,128]{2,1,0:T(8,128)(2,1)S(1)} %pad_maximum_fusion.16), channel_id=1, source_target_pairs={{0,64},{8,24},{16,80},{24,40},{32,96},{40,56},{48,112},{56,8},{64,... | collective-permute-start | bytes 688136 | tf_op jit(solution)/shard_map/a_q/ppermute | solution.py:58
  24.3 5.4 %collective-permute-start.6 = (bf16[4,4,224,128]{3,2,0,1:T(8,128)(2,1)S(1)}, bf16[4,4,224,128]{3,2,0,1:T(8,128)(2,1)S(1)}, u32[]{:S(2)}, u32[]{:S(2)}) collective-permute-start(bf16[4,4,224,128]{3,2,0,1:T(8,128)(2,1)S(1)} %pad_maximum_fusion.6), channel_id=1, source_target_pairs={{0,8},{8,0},{1,9},{9,1},{2,10},{10,2},{3,11},{11,3},{4,12},{12,4},... | collective-permute-start | bytes 2752520 | tf_op jit(solution)/shard_map/a_cores/ppermute | solution.py:67
  27.6 11.2 %collective-permute-start.11 = (bf16[4,256,128]{2,1,0:T(8,128)(2,1)S(1)}, bf16[4,256,128]{2,1,0:T(8,128)(2,1)S(1)}, u32[]{:S(2)}, u32[]{:S(2)}) collective-permute-start(bf16[4,256,128]{2,1,0:T(8,128)(2,1)S(1)} %pad_maximum_fusion.11), channel_id=1, source_target_pairs={{0,192},{8,56},{16,208},{24,8},{32,224},{40,24},{48,240},{56,40},{... | collective-permute-start | bytes 786440 | tf_op jit(solution)/shard_map/b_q/ppermute | solution.py:58
  27.9 10.9 %collective-permute-start.10 = (bf16[4,256,128]{2,1,0:T(8,128)(2,1)S(1)}, bf16[4,256,128]{2,1,0:T(8,128)(2,1)S(1)}, u32[]{:S(2)}, u32[]{:S(2)}) collective-permute-start(bf16[4,256,128]{2,1,0:T(8,128)(2,1)S(1)} %pad_maximum_fusion.11), channel_id=1, source_target_pairs={{0,128},{8,40},{16,144},{24,56},{32,160},{40,8},{48,176},{56,24},{... | collective-permute-start | bytes 786440 | tf_op jit(solution)/shard_map/b_q/ppermute | solution.py:58
  28.4 10.4 %collective-permute-start.9 = (bf16[4,256,128]{2,1,0:T(8,128)(2,1)S(1)}, bf16[4,256,128]{2,1,0:T(8,128)(2,1)S(1)}, u32[]{:S(2)}, u32[]{:S(2)}) collective-permute-start(bf16[4,256,128]{2,1,0:T(8,128)(2,1)S(1)} %pad_maximum_fusion.11), channel_id=1, source_target_pairs={{0,64},{8,24},{16,80},{24,40},{32,96},{40,56},{48,112},{56,8},{64,... | collective-permute-start | bytes 786440 | tf_op jit(solution)/shard_map/b_q/ppermute | solution.py:58
  29.9 2.0 %copy-start = (bf16[512,3584]{1,0:T(8,128)(2,1)S(1)}, bf16[512,3584]{1,0:T(8,128)(2,1)}, u32[]{:S(2)}) copy-start(bf16[512,3584]{1,0:T(8,128)(2,1)} %param.9) | copy-start | bytes 11010052
  33.0 10.3 %copy-start.4 = (f32[4,2,32,512]{3,2,1,0:T(8,128)}, f32[4,2,32,512]{3,2,1,0:T(8,128)S(1)}, u32[]{:S(2)}) copy-start(f32[4,2,32,512]{3,2,1,0:T(8,128)S(1)} %fusion.2) | copy-start | bytes 1572868
  33.1 9.2 %collective-permute-start.8 = (f32[4,32,256]{2,1,0:T(8,128)S(1)}, f32[4,32,256]{2,1,0:T(8,128)S(1)}, u32[]{:S(2)}, u32[]{:S(2)}) collective-permute-start(f32[4,32,256]{2,1,0:T(8,128)S(1)} %get-tuple-element.94), channel_id=1, source_target_pairs={{0,7},{1,2},{2,1},{3,4},{4,3},{5,6},{6,5},{7,0},{8,15},{9,10},{10,... | collective-permute-start | bytes 393224 | tf_op jit(solution)/shard_map/act_pairs/ppermute | solution.py:79
  38.8 4.4 %collective-permute-start.7 = (f32[4,32,256]{2,1,0:T(8,128)S(1)}, f32[4,32,256]{2,1,0:T(8,128)S(1)}, u32[]{:S(2)}, u32[]{:S(2)}) collective-permute-start(f32[4,32,256]{2,1,0:T(8,128)S(1)} %get-tuple-element.93), channel_id=1, source_target_pairs={{0,1},{1,0},{2,3},{3,2},{4,5},{5,4},{6,7},{7,6},{8,9},{9,8},{10,11... | collective-permute-start | bytes 393224 | tf_op jit(solution)/shard_map/act_pairs/ppermute | solution.py:75
  43.6 9.0 %collective-permute-start.12 = (bf16[4,4,256,128]{3,2,0,1:T(8,128)(2,1)S(1)}, bf16[4,4,256,128]{3,2,0,1:T(8,128)(2,1)S(1)}, u32[]{:S(2)}, u32[]{:S(2)}) collective-permute-start(bf16[4,4,256,128]{3,2,0,1:T(8,128)(2,1)S(1)} %copy.25), channel_id=1, source_target_pairs={{0,8},{8,0},{1,9},{9,1},{2,10},{10,2},{3,11},{11,3},{4,12},{12,4},... | collective-permute-start | bytes 3145736 | tf_op jit(solution)/shard_map/b_cores/ppermute | solution.py:67
  45.2 8.2 %slice-start = ((s8[8388608]{0:T(1024)(128)(4,1)}), s8[4194304]{0:T(1024)(128)(4,1)S(1)}, s32[]{:S(2)}) async-start(s8[8388608]{0:T(1024)(128)(4,1)} %bitcast.261), calls=%async_computation.2 | async-start | bytes 8388608
  46.3 11.8 %collective-permute-start.13 = (f32[32,512]{1,0:T(8,128)S(1)}, f32[32,512]{1,0:T(8,128)S(1)}, u32[]{:S(2)}, u32[]{:S(2)}) collective-permute-start(f32[32,512]{1,0:T(8,128)S(1)} %get-tuple-element.92), channel_id=1, source_target_pairs={{0,2},{1,3},{2,4},{3,5},{4,6},{5,7},{6,0},{7,1},{8,10},{9,11},{10,... | collective-permute-start | bytes 196616 | tf_op jit(solution)/shard_map/act_shifts/ppermute | solution.py:71
  46.9 11.3 %collective-permute-start.14 = (f32[32,512]{1,0:T(8,128)S(1)}, f32[32,512]{1,0:T(8,128)S(1)}, u32[]{:S(2)}, u32[]{:S(2)}) collective-permute-start(f32[32,512]{1,0:T(8,128)S(1)} %get-tuple-element.91), channel_id=1, source_target_pairs={{0,4},{1,5},{2,6},{3,7},{4,0},{5,1},{6,2},{7,3},{8,12},{9,13},{10,... | collective-permute-start | bytes 196616 | tf_op jit(solution)/shard_map/act_shifts/ppermute | solution.py:71
  49.7 8.5 %collective-permute-start.15 = (f32[32,512]{1,0:T(8,128)S(1)}, f32[32,512]{1,0:T(8,128)S(1)}, u32[]{:S(2)}, u32[]{:S(2)}) collective-permute-start(f32[32,512]{1,0:T(8,128)S(1)} %get-tuple-element.90), channel_id=1, source_target_pairs={{0,6},{1,7},{2,0},{3,1},{4,2},{5,3},{6,4},{7,5},{8,14},{9,15},{10,... | collective-permute-start | bytes 196616 | tf_op jit(solution)/shard_map/act_shifts/ppermute | solution.py:71
  53.0 2.2 %slice-start.1 = ((s8[8388608]{0:T(1024)(128)(4,1)}), s8[4194304]{0:T(1024)(128)(4,1)S(1)}, s32[]{:S(2)}) async-start(s8[8388608]{0:T(1024)(128)(4,1)} %bitcast.261), calls=%async_computation.3 | async-start | bytes 8388608
  58.2 5.1 %collective-permute-start.16 = (bf16[128,512]{1,0:T(8,128)(2,1)S(1)}, bf16[128,512]{1,0:T(8,128)(2,1)S(1)}, u32[]{:S(2)}, u32[]{:S(2)}) collective-permute-start(bf16[128,512]{1,0:T(8,128)(2,1)S(1)} %fusion.4), channel_id=1, source_target_pairs={{0,7},{1,2},{2,1},{3,4},{4,3},{5,6},{6,5},{7,0},{8,15},{9,10},{10,... | collective-permute-start | bytes 393224 | tf_op jit(solution)/shard_map/back_pairs/ppermute | solution.py:79
  60.2 3.4 %copy-start.1 = (bf16[512,3584]{1,0:T(8,128)(2,1)S(1)}, bf16[512,3584]{1,0:T(8,128)(2,1)}, u32[]{:S(2)}) copy-start(bf16[512,3584]{1,0:T(8,128)(2,1)} %param.9) | copy-start | bytes 11010052
  64.2 6.6 %collective-permute-start.17 = (f32[128,3584]{1,0:T(8,128)S(1)}, f32[128,3584]{1,0:T(8,128)}, u32[]{:S(2)}, u32[]{:S(2)}) collective-permute-start(f32[128,3584]{1,0:T(8,128)S(1)} %fusion.56), channel_id=1, source_target_pairs={{0,8},{8,0},{1,9},{9,1},{2,10},{10,2},{3,11},{11,3},{4,12},{12,4},... | collective-permute-start | bytes 5505032 | tf_op jit(solution)/shard_map/grad_a_cores/ppermute | solution.py:67
  66.8 3.9 %collective-permute-start.18 = (f32[4,4,64,128]{3,2,1,0:T(8,128)S(1)}, f32[4,4,64,128]{3,2,1,0:T(8,128)S(1)}, u32[]{:S(2)}, u32[]{:S(2)}) collective-permute-start(f32[4,4,64,128]{3,2,1,0:T(8,128)S(1)} %get-tuple-element.64), channel_id=1, source_target_pairs={{0,8},{8,0},{1,9},{9,1},{2,10},{10,2},{3,11},{11,3},{4,12},{12,4},... | collective-permute-start | bytes 1572872 | tf_op jit(solution)/shard_map/grad_b_cores/ppermute | solution.py:67
  72.6 10.7 %collective-permute-start.21 = (f32[4,288,128]{2,1,0:T(8,128)S(1)}, f32[4,288,128]{2,1,0:T(8,128)S(1)}, u32[]{:S(2)}, u32[]{:S(2)}) collective-permute-start(f32[4,288,128]{2,1,0:T(8,128)S(1)} %maximum_maximum_fusion.2), channel_id=1, source_target_pairs={{0,32},{8,136},{16,48},{24,152},{32,0},{40,168},{48,16},{56,184},{... | collective-permute-start | bytes 1769480 | tf_op jit(solution)/shard_map/grads_p/ppermute | solution.py:54
  75.7 13.0 %collective-permute-start.20 = (f32[4,288,128]{2,1,0:T(8,128)S(1)}, f32[4,288,128]{2,1,0:T(8,128)S(1)}, u32[]{:S(2)}, u32[]{:S(2)}) collective-permute-start(f32[4,288,128]{2,1,0:T(8,128)S(1)} %maximum_maximum_fusion.1), channel_id=1, source_target_pairs={{0,48},{8,200},{16,0},{24,216},{32,16},{40,232},{48,32},{56,248},{... | collective-permute-start | bytes 1769480 | tf_op jit(solution)/shard_map/grads_p/ppermute | solution.py:54
  76.1 13.4 %collective-permute-start.19 = (f32[4,288,128]{2,1,0:T(8,128)S(1)}, f32[4,288,128]{2,1,0:T(8,128)S(1)}, u32[]{:S(2)}, u32[]{:S(2)}) collective-permute-start(f32[4,288,128]{2,1,0:T(8,128)S(1)} %maximum_maximum_fusion), channel_id=1, source_target_pairs={{0,16},{8,72},{16,32},{24,88},{32,48},{40,104},{48,0},{56,120},{64... | collective-permute-start | bytes 1769480 | tf_op jit(solution)/shard_map/grads_p/ppermute | solution.py:54
  89.6 21.7 %copy-start.3 = (f32[256,256]{1,0:T(8,128)S(1)}, f32[256,256]{1,0:T(8,128)}, u32[]{:S(2)}) copy-start(f32[256,256]{1,0:T(8,128)} %param.15) | copy-start | bytes 786436
  89.6 21.8 %copy-start.6 = (f32[256,256]{1,0:T(8,128)S(1)}, f32[256,256]{1,0:T(8,128)}, u32[]{:S(2)}) copy-start(f32[256,256]{1,0:T(8,128)} %param.16) | copy-start | bytes 786436
  89.7 21.8 %copy-start.7 = (f32[256,256]{1,0:T(8,128)S(1)}, f32[256,256]{1,0:T(8,128)}, u32[]{:S(2)}) copy-start(f32[256,256]{1,0:T(8,128)} %param.17) | copy-start | bytes 786436
  89.7 32.7 %copy-start.5 = (f32[8,3584]{1,0:T(8,128)S(1)}, f32[8,3584]{1,0:T(8,128)}, u32[]{:S(2)}) copy-start(f32[8,3584]{1,0:T(8,128)} %param.12) | copy-start | bytes 344068
  89.7 32.7 %copy-start.8 = (f32[8,3584]{1,0:T(8,128)S(1)}, f32[8,3584]{1,0:T(8,128)}, u32[]{:S(2)}) copy-start(f32[8,3584]{1,0:T(8,128)} %param.14) | copy-start | bytes 344068
  89.8 32.7 %copy-start.9 = (f32[8,3584]{1,0:T(8,128)S(1)}, f32[8,3584]{1,0:T(8,128)}, u32[]{:S(2)}) copy-start(f32[8,3584]{1,0:T(8,128)} %param.13) | copy-start | bytes 344068
  89.8 5.6 %collective-permute-start.24 = (f32[288,128]{1,0:T(8,128)S(1)}, f32[288,128]{1,0:T(8,128)S(1)}, u32[]{:S(2)}, u32[]{:S(2)}) collective-permute-start(f32[288,128]{1,0:T(8,128)S(1)} %get-tuple-element.78), channel_id=1, source_target_pairs={{0,128},{8,40},{16,144},{24,56},{32,160},{40,8},{48,176},{56,24},{... | collective-permute-start | bytes 442376 | tf_op jit(solution)/shard_map/grads_q/ppermute | solution.py:58
  90.8 4.6 %collective-permute-start.23 = (f32[288,128]{1,0:T(8,128)S(1)}, f32[288,128]{1,0:T(8,128)S(1)}, u32[]{:S(2)}, u32[]{:S(2)}) collective-permute-start(f32[288,128]{1,0:T(8,128)S(1)} %get-tuple-element.79), channel_id=1, source_target_pairs={{0,192},{8,56},{16,208},{24,8},{32,224},{40,24},{48,240},{56,40},{... | collective-permute-start | bytes 442376 | tf_op jit(solution)/shard_map/grads_q/ppermute | solution.py:58
  91.4 5.9 %collective-permute-start.22 = (f32[288,128]{1,0:T(8,128)S(1)}, f32[288,128]{1,0:T(8,128)S(1)}, u32[]{:S(2)}, u32[]{:S(2)}) collective-permute-start(f32[288,128]{1,0:T(8,128)S(1)} %get-tuple-element.77), channel_id=1, source_target_pairs={{0,64},{8,24},{16,80},{24,40},{32,96},{40,56},{48,112},{56,8},{64,... | collective-permute-start | bytes 442376 | tf_op jit(solution)/shard_map/grads_q/ppermute | solution.py:58
  97.4 5.0 %collective-permute-start.25 = (f32[8,128]{1,0:T(8,128)S(1)}, f32[8,128]{1,0:T(8,128)S(1)}, u32[]{:S(2)}, u32[]{:S(2)}) collective-permute-start(f32[8,128]{1,0:T(8,128)S(1)} %slice.94), channel_id=1, source_target_pairs={{0,8},{8,0},{1,9},{9,1},{2,10},{10,2},{3,11},{11,3},{4,12},{12,4},... | collective-permute-start | bytes 12296 | tf_op jit(solution)/shard_map/ppermute | solution.py:67
  103.0 18.0 %all-to-all-start = ((f32[128,1,128]{2,1,0:T(1,128)}), f32[128,1,128]{2,1,0:T(1,128)S(1)}, u32[]{:S(2)}, u32[]{:S(2)}) async-start(f32[128,1,128]{2,1,0:T(1,128)} %broadcast_in_dim.13), calls=%async_computation | async-start | bytes 131072 | tf_op jit(solution)/shard_map/all_to_all | solution.py:230
  110.6 3.4 %collective-permute-start.26 = (f32[64,128]{1,0:T(8,128)S(1)}, f32[64,128]{1,0:T(8,128)S(1)}, u32[]{:S(2)}, u32[]{:S(2)}) collective-permute-start(f32[64,128]{1,0:T(8,128)S(1)} %get-tuple-element.105), channel_id=1, source_target_pairs={{0,1},{1,0},{2,3},{3,2},{4,5},{5,4},{6,7},{7,6},{8,9},{9,8},{10,11... | collective-permute-start | bytes 98312 | tf_op jit(solution)/shard_map/ppermute | solution.py:75
  123.6 17.4 %all-to-all-start.1 = ((bf16[16,224,128]{2,1,0:T(8,128)(2,1)}), bf16[16,224,128]{2,1,0:T(8,128)(2,1)S(1)}, u32[]{:S(2)}, u32[]{:S(2)}) async-start(bf16[16,224,128]{2,1,0:T(8,128)(2,1)} %broadcast_in_dim.14), calls=%async_computation.1 | async-start | bytes 1835008 | tf_op jit(solution)/shard_map/all_to_all | solution.py:246
  127.3 5.6 %collective-permute-start.27 = (f32[128,128]{1,0:T(8,128)S(1)}, f32[128,128]{1,0:T(8,128)S(1)}, u32[]{:S(2)}, u32[]{:S(2)}) collective-permute-start(f32[128,128]{1,0:T(8,128)S(1)} %pad_maximum_fusion.21), channel_id=1, source_target_pairs={{0,2},{1,3},{2,4},{3,5},{4,6},{5,7},{6,0},{7,1},{8,10},{9,11},{10,... | collective-permute-start | bytes 196616 | tf_op jit(solution)/shard_map/ppermute | solution.py:71
  127.7 7.5 %collective-permute-start.28 = (f32[128,128]{1,0:T(8,128)S(1)}, f32[128,128]{1,0:T(8,128)S(1)}, u32[]{:S(2)}, u32[]{:S(2)}) collective-permute-start(f32[128,128]{1,0:T(8,128)S(1)} %pad_maximum_fusion.21), channel_id=1, source_target_pairs={{0,4},{1,5},{2,6},{3,7},{4,0},{5,1},{6,2},{7,3},{8,12},{9,13},{10,... | collective-permute-start | bytes 196616 | tf_op jit(solution)/shard_map/ppermute | solution.py:71
  129.8 8.8 %collective-permute-start.29 = (f32[128,128]{1,0:T(8,128)S(1)}, f32[128,128]{1,0:T(8,128)S(1)}, u32[]{:S(2)}, u32[]{:S(2)}) collective-permute-start(f32[128,128]{1,0:T(8,128)S(1)} %pad_maximum_fusion.21), channel_id=1, source_target_pairs={{0,6},{1,7},{2,0},{3,1},{4,2},{5,3},{6,4},{7,5},{8,14},{9,15},{10,... | collective-permute-start | bytes 196616 | tf_op jit(solution)/shard_map/ppermute | solution.py:71
  141.0 5.2 %collective-permute-start.30 = (bf16[16,224,128]{2,1,0:T(8,128)(2,1)S(1)}, bf16[16,224,128]{2,1,0:T(8,128)(2,1)S(1)}, u32[]{:S(2)}, u32[]{:S(2)}) collective-permute-start(bf16[16,224,128]{2,1,0:T(8,128)(2,1)S(1)} %all-to-all-done.1), channel_id=1, source_target_pairs={{0,8},{8,0},{1,9},{9,1},{2,10},{10,2},{3,11},{11,3},{4,12},{12,4},... | collective-permute-start | bytes 2752520 | tf_op jit(solution)/shard_map/ppermute | solution.py:67
  146.4 1.5 %copy-start.2 = (bf16[256,3584]{1,0:T(8,128)(2,1)S(1)}, bf16[256,3584]{1,0:T(8,128)(2,1)}, u32[]{:S(2)}) copy-start(bf16[256,3584]{1,0:T(8,128)(2,1)} %param.11) | copy-start | bytes 5505028

commit v4 on v3

--- a/solution.py
+++ b/solution.py
@@ -174,7 +174,7 @@
     with jax.named_scope("act_shifts"):
         act_pair = act_keep + act_got
         act_pieces = [pick(act_pair, (z // 2 + k) % 4) for k in range(4)]
-        act_gots = [shift_z(act_pieces[k], 2 * k) for k in range(1, 4)]
+        act_gots = [shift_z(act_pieces[k], 2 * k) for k in (1, 3, 2)]
     with jax.named_scope("b_cores"):
         b_stack = by_offset(b_stack, q)
         b_rows = join_cores(b_stack, swap_core(b_stack), core).reshape(8192, 128)
@@ -244,10 +244,10 @@
     copies = jnp.broadcast_to(new_a, (16, 224, 128))
     copies, pair = lax.optimization_barrier((copies, pair))
     mine = lax.all_to_all(copies, ("y", "x"), 0, 0, tiled=True)
-    pairs = [pair] + [shift_z(pair, 2 * k) for k in (1, 2, 3)]
+    pairs = shifts(lambda v, k: shift_z(v, 2 * k), pair)
     mine, pairs = lax.optimization_barrier((mine, pairs))
     other = swap_core(mine)
-    whole_grad_b = by_offset(jnp.stack(pairs), z // 2).reshape(8, 64, 128)
+    whole_grad_b = by_offset(pairs, z // 2).reshape(8, 64, 128)
     whole_grad_b = untile(whole_grad_b, 32, 256).reshape(256, 256)
     new_b = moment_update_step(
         *right_t, clipper * whole_grad_b

time: 150 us -> 150 us (level)
  transfers between devices with their start and end apart: 33 -> 33, of which waited for: 24 -> 25; matrix products, arithmetic and copies ran while one was open for 8% -> 8% of each run, Pallas kernels for 0% -> 0%
where the time goes in v4:
time: 150 us
  waiting for transfers between devices  62.1 us (41%)
  starting transfers between devices  58.5 us (39%)
  matrix products  11 us (7%)
  local copies, waits for them, and re-layouts  9.83 us (7%)
  other arithmetic  7.15 us (5%)
    ppermute x6, waiting for transfers between devices, shift_p(): return lax.ppermute(v, DP, plane_pairs(True, k))  17.1 us
    ppermute x6, starting transfers between devices, swap_core(): return lax.ppermute(v, 'core', [(0, 1), (1, 0)])  14.8 us
    ppermute x9, waiting for transfers between devices, shift_q(): return lax.ppermute(v, DP, plane_pairs(False, k))  13.1 us
    ppermute x6, starting transfers between devices, shift_z(): return lax.ppermute(v, 'z', [(i, (i + k) % 8) for i in range(8)])  9.89 us
    ppermute x6, starting transfers between devices, shift_p(): return lax.ppermute(v, DP, plane_pairs(True, k))  9.61 us
    all_to_all x1, starting transfers between devices, local(): squares = lax.all_to_all(squares, ('y', 'x', 'z'), 0, 0, tiled=True)  7.14 us
    ppermute x9, starting transfers between devices, shift_q(): return lax.ppermute(v, DP, plane_pairs(False, k))  7.08 us
    all_to_all x1, waiting for transfers between devices, local(): squares = lax.all_to_all(squares, ('y', 'x', 'z'), 0, 0, tiled=True)  7.04 us
  transfers between devices with their start and end apart: 33, of which 25 were waited for; matrix products, arithmetic and copies ran while one was open for 8% of the time, Pallas kernels for 0%

profile of v4, /device:TPU:1, one launch (start us, length us, event | category | flops | bytes accessed | tf_op | source)
XLA Modules:
  0.0 150.0 jit_solution(14667948311937449036)
XLA Ops:
  0.0 0.9 fusion.44
  0.9 0.9 dynamic-slice_convert_fusion
  1.9 3.6 %collective-permute-start.2 = (bf16[480,128]{1,0:T(8,128)(2,1)S(1)}, bf16[480,128]{1,0:T(8,128)(2,1)S(1)}, u32[]{:S(2)}, u32[]{:S(2)}) collective-permute-start(bf16[480,128]{1,0:T(8,128)(2,1)S(1)} %pad_maximum_fusion.20), channel_id=1, source_target_pairs={{0,48},{8,200},{16,0},{24,216},{32,16},{40,232},{48,32},{56,248},{... | collective-permute-start | bytes 368648 | tf_op jit(solution)/shard_map/factors_p/ppermute | solution.py:54
  5.8 0.7 collective-permute-start
  6.5 0.9 fusion.67
  7.4 1.2 collective-permute-done.2
  8.6 2.4 %collective-permute-done.1 = bf16[480,128]{1,0:T(8,128)(2,1)S(1)} collective-permute-done((bf16[480,128]{1,0:T(8,128)(2,1)S(1)}, bf16[480,128]{1,0:T(8,128)(2,1)S(1)}, u32[]{:S(2)}, u32[]{:S(2)}) %collective-permute-start.1) | collective-permute-done | bytes 122912 | tf_op jit(solution)/shard_map/factors_p/ppermute | solution.py:54
  11.0 1.3 collective-permute-done
  12.6 2.3 %collective-permute-start.5 = (bf16[4,224,128]{2,1,0:T(8,128)(2,1)S(1)}, bf16[4,224,128]{2,1,0:T(8,128)(2,1)S(1)}, u32[]{:S(2)}, u32[]{:S(2)}) collective-permute-start(bf16[4,224,128]{2,1,0:T(8,128)(2,1)S(1)} %pad_maximum_fusion.16), channel_id=1, source_target_pairs={{0,192},{8,56},{16,208},{24,8},{32,224},{40,24},{48,240},{56,40},{... | collective-permute-start | bytes 688136 | tf_op jit(solution)/shard_map/a_q/ppermute | solution.py:58
  14.8 0.5 collective-permute-start.4
  15.3 0.6 collective-permute-start.3
  15.9 4.3 %collective-permute-done.5 = bf16[4,224,128]{2,1,0:T(8,128)(2,1)S(1)} collective-permute-done((bf16[4,224,128]{2,1,0:T(8,128)(2,1)S(1)}, bf16[4,224,128]{2,1,0:T(8,128)(2,1)S(1)}, u32[]{:S(2)}, u32[]{:S(2)}) %collective-permute-start.5) | collective-permute-done | bytes 229408 | tf_op jit(solution)/shard_map/a_q/ppermute | solution.py:58
  20.2 1.1 collective-permute-done.4
  21.3 2.6 %collective-permute-done.3 = bf16[4,224,128]{2,1,0:T(8,128)(2,1)S(1)} collective-permute-done((bf16[4,224,128]{2,1,0:T(8,128)(2,1)S(1)}, bf16[4,224,128]{2,1,0:T(8,128)(2,1)S(1)}, u32[]{:S(2)}, u32[]{:S(2)}) %collective-permute-start.3) | collective-permute-done | bytes 229408 | tf_op jit(solution)/shard_map/a_q/ppermute | solution.py:58
  24.3 3.3 %collective-permute-start.6 = (bf16[4,4,224,128]{3,2,0,1:T(8,128)(2,1)S(1)}, bf16[4,4,224,128]{3,2,0,1:T(8,128)(2,1)S(1)}, u32[]{:S(2)}, u32[]{:S(2)}) collective-permute-start(bf16[4,4,224,128]{3,2,0,1:T(8,128)(2,1)S(1)} %pad_maximum_fusion.6), channel_id=1, source_target_pairs={{0,8},{8,0},{1,9},{9,1},{2,10},{10,2},{3,11},{11,3},{4,12},{12,4},... | collective-permute-start | bytes 2752520 | tf_op jit(solution)/shard_map/a_cores/ppermute | solution.py:67
  28.4 0.7 collective-permute-start.9
  29.1 0.6 collective-permute-done.6
  30.1 1.8 %copy-done = bf16[512,3584]{1,0:T(8,128)(2,1)S(1)} copy-done((bf16[512,3584]{1,0:T(8,128)(2,1)S(1)}, bf16[512,3584]{1,0:T(8,128)(2,1)}, u32[]{:S(2)}) %copy-start) | copy-done | bytes 3670040
  31.9 1.1 fusion.2
  33.1 5.7 %collective-permute-start.8 = (f32[4,32,256]{2,1,0:T(8,128)S(1)}, f32[4,32,256]{2,1,0:T(8,128)S(1)}, u32[]{:S(2)}, u32[]{:S(2)}) collective-permute-start(f32[4,32,256]{2,1,0:T(8,128)S(1)} %get-tuple-element.88), channel_id=1, source_target_pairs={{0,7},{1,2},{2,1},{3,4},{4,3},{5,6},{6,5},{7,0},{8,15},{9,10},{10,... | collective-permute-start | bytes 393224 | tf_op jit(solution)/shard_map/act_pairs/ppermute | solution.py:79
  38.9 3.4 %collective-permute-done.8 = f32[4,32,256]{2,1,0:T(8,128)S(1)} collective-permute-done((f32[4,32,256]{2,1,0:T(8,128)S(1)}, f32[4,32,256]{2,1,0:T(8,128)S(1)}, u32[]{:S(2)}, u32[]{:S(2)}) %collective-permute-start.8) | collective-permute-done | bytes 131104 | tf_op jit(solution)/shard_map/act_pairs/ppermute | solution.py:79
  42.3 0.8 collective-permute-done.7
  43.6 1.6 %collective-permute-start.12 = (bf16[4,4,256,128]{3,2,0,1:T(8,128)(2,1)S(1)}, bf16[4,4,256,128]{3,2,0,1:T(8,128)(2,1)S(1)}, u32[]{:S(2)}, u32[]{:S(2)}) collective-permute-start(bf16[4,4,256,128]{3,2,0,1:T(8,128)(2,1)S(1)} %copy.25), channel_id=1, source_target_pairs={{0,8},{8,0},{1,9},{9,1},{2,10},{10,2},{3,11},{11,3},{4,12},{12,4},... | collective-permute-start | bytes 3145736 | tf_op jit(solution)/shard_map/b_cores/ppermute | solution.py:67
  45.2 1.1 bitcast_add_fusion
  46.9 3.1 %collective-permute-start.14 = (f32[32,512]{1,0:T(8,128)S(1)}, f32[32,512]{1,0:T(8,128)S(1)}, u32[]{:S(2)}, u32[]{:S(2)}) collective-permute-start(f32[32,512]{1,0:T(8,128)S(1)} %get-tuple-element.85), channel_id=1, source_target_pairs={{0,6},{1,7},{2,0},{3,1},{4,2},{5,3},{6,4},{7,5},{8,14},{9,15},{10,... | collective-permute-start | bytes 196616 | tf_op jit(solution)/shard_map/act_shifts/ppermute | solution.py:71
  50.0 2.6 %collective-permute-start.15 = (f32[32,512]{1,0:T(8,128)S(1)}, f32[32,512]{1,0:T(8,128)S(1)}, u32[]{:S(2)}, u32[]{:S(2)}) collective-permute-start(f32[32,512]{1,0:T(8,128)S(1)} %get-tuple-element.84), channel_id=1, source_target_pairs={{0,4},{1,5},{2,6},{3,7},{4,0},{5,1},{6,2},{7,3},{8,12},{9,13},{10,... | collective-permute-start | bytes 196616 | tf_op jit(solution)/shard_map/act_shifts/ppermute | solution.py:71
  53.4 1.8 %slice-done.1 = s8[4194304]{0:T(1024)(128)(4,1)S(1)} async-done(((s8[8388608]{0:T(1024)(128)(4,1)}), s8[4194304]{0:T(1024)(128)(4,1)S(1)}, s32[]{:S(2)}) %slice-start.1) | async-done | bytes 4194328
  55.2 2.9 %fusion.4 = bf16[128,512]{1,0:T(8,128)(2,1)S(1)} fusion(bf16[8192,128]{1,0:T(8,128)(2,1)S(1)} %bitcast.263, bf16[512,8192]{1,0:T(8,128)(2,1)S(1)} %bitcast.262), kind=kOutput, calls=%fused_computation.9 | convolution fusion | flops 1073872896 | bytes 10616832 | tf_op jit(solution)/shard_map/back/dot_general | solution.py:183
  58.5 1.5 %fusion.54 = f32[32,8192]{1,0:T(8,128)S(1)} fusion(bf16[32,512]{1,0:T(8,128)(2,1)S(1)} %fusion.43, bf16[512,8192]{1,0:T(8,128)(2,1)S(1)} %bitcast.262), kind=kOutput, calls=%fused_computation.177 | convolution fusion | flops 268435456 | bytes 9469952 | tf_op jit(solution)/shard_map/grad_b_terms/dot_general | solution.py:192
  60.1 3.4 %collective-permute-done.16 = bf16[128,512]{1,0:T(8,128)(2,1)S(1)} collective-permute-done((bf16[128,512]{1,0:T(8,128)(2,1)S(1)}, bf16[128,512]{1,0:T(8,128)(2,1)S(1)}, u32[]{:S(2)}, u32[]{:S(2)}) %collective-permute-start.16) | collective-permute-done | bytes 131104 | tf_op jit(solution)/shard_map/back_pairs/ppermute | solution.py:79
  63.8 0.6 fusion.56
  64.5 2.3 %collective-permute-start.17 = (f32[128,3584]{1,0:T(8,128)S(1)}, f32[128,3584]{1,0:T(8,128)}, u32[]{:S(2)}, u32[]{:S(2)}) collective-permute-start(f32[128,3584]{1,0:T(8,128)S(1)} %fusion.56), channel_id=1, source_target_pairs={{0,8},{8,0},{1,9},{9,1},{2,10},{10,2},{3,11},{11,3},{4,12},{12,4},... | collective-permute-start | bytes 5505032 | tf_op jit(solution)/shard_map/grad_a_cores/ppermute | solution.py:67
  67.2 2.7 %fusion.55 = f32[128,3584]{1,0:T(8,128)S(1)} fusion(bf16[128,512]{1,0:T(8,128)(2,1)S(1)} %bitcast.275, bf16[512,3584]{1,0:T(8,128)(2,1)} %param.9), kind=kOutput, calls=%fused_computation.178 | convolution fusion | flops 469762048 | bytes 5636096 | tf_op jit(solution)/shard_map/grad_a_terms/dot_general | solution.py:200
  69.9 1.0 collective-permute-done.18
  71.1 1.7 %fusion.13 = (f32[4,224,128]{2,1,0:T(8,128)S(1)}, f32[4,224,128]{2,1,0:T(8,128)S(1)}, f32[4,224,128]{2,1,0:T(8,128)S(1)}, f32[4,224,128]{2,1,0:T(8,128)S(1)}) fusion(f32[128,3584]{1,0:T(8,128)} %collective-permute-done.17, f32[128,3584]{1,0:T(8,128)S(1)} %fusion.55), kind=kLoop, calls=%fused_computation.38 | loop fusion | flops 458752 | bytes 5505024 | tf_op jit(solution)/shard_map/reshape | solution.py:212
  72.8 3.3 %collective-permute-start.21 = (f32[4,288,128]{2,1,0:T(8,128)S(1)}, f32[4,288,128]{2,1,0:T(8,128)S(1)}, u32[]{:S(2)}, u32[]{:S(2)}) collective-permute-start(f32[4,288,128]{2,1,0:T(8,128)S(1)} %maximum_maximum_fusion.2), channel_id=1, source_target_pairs={{0,32},{8,136},{16,48},{24,152},{32,0},{40,168},{48,16},{56,184},{... | collective-permute-start | bytes 1769480 | tf_op jit(solution)/shard_map/grads_p/ppermute | solution.py:54
  76.6 1.2 collective-permute-start.19
  77.8 5.9 %collective-permute-done.21 = f32[4,288,128]{2,1,0:T(8,128)S(1)} collective-permute-done((f32[4,288,128]{2,1,0:T(8,128)S(1)}, f32[4,288,128]{2,1,0:T(8,128)S(1)}, u32[]{:S(2)}, u32[]{:S(2)}) %collective-permute-start.21) | collective-permute-done | bytes 589856 | tf_op jit(solution)/shard_map/grads_p/ppermute | solution.py:54
  83.7 5.4 %collective-permute-done.20 = f32[4,288,128]{2,1,0:T(8,128)S(1)} collective-permute-done((f32[4,288,128]{2,1,0:T(8,128)S(1)}, f32[4,288,128]{2,1,0:T(8,128)S(1)}, u32[]{:S(2)}, u32[]{:S(2)}) %collective-permute-start.20) | collective-permute-done | bytes 589856 | tf_op jit(solution)/shard_map/grads_p/ppermute | solution.py:54
  89.2 0.8 collective-permute-done.19
  90.2 0.8 collective-permute-start.24
  91.0 0.9 collective-permute-start.23
  91.9 0.6 collective-permute-start.22
  92.5 3.7 %collective-permute-done.24 = f32[288,128]{1,0:T(8,128)S(1)} collective-permute-done((f32[288,128]{1,0:T(8,128)S(1)}, f32[288,128]{1,0:T(8,128)S(1)}, u32[]{:S(2)}, u32[]{:S(2)}) %collective-permute-start.24) | collective-permute-done | bytes 147488 | tf_op jit(solution)/shard_map/grads_q/ppermute | solution.py:58
  96.2 1.4 collective-permute-done.22
  97.7 4.3 %collective-permute-start.25 = (f32[8,128]{1,0:T(8,128)S(1)}, f32[8,128]{1,0:T(8,128)S(1)}, u32[]{:S(2)}, u32[]{:S(2)}) collective-permute-start(f32[8,128]{1,0:T(8,128)S(1)} %slice.94), channel_id=1, source_target_pairs={{0,8},{8,0},{1,9},{9,1},{2,10},{10,2},{3,11},{11,3},{4,12},{12,4},... | collective-permute-start | bytes 12296 | tf_op jit(solution)/shard_map/ppermute | solution.py:67
  102.0 0.8 collective-permute-done.25
  102.8 0.7 broadcast_in_dim.13
  103.5 7.1 %all-to-all-start = ((f32[128,1,128]{2,1,0:T(1,128)}), f32[128,1,128]{2,1,0:T(1,128)S(1)}, u32[]{:S(2)}, u32[]{:S(2)}) async-start(f32[128,1,128]{2,1,0:T(1,128)} %broadcast_in_dim.13), calls=%async_computation | async-start | bytes 131072 | tf_op jit(solution)/shard_map/all_to_all | solution.py:230
  110.6 0.7 collective-permute-start.26
  111.7 2.4 %collective-permute-done.26 = f32[64,128]{1,0:T(8,128)S(1)} collective-permute-done((f32[64,128]{1,0:T(8,128)S(1)}, f32[64,128]{1,0:T(8,128)S(1)}, u32[]{:S(2)}, u32[]{:S(2)}) %collective-permute-start.26) | collective-permute-done | bytes 32800 | tf_op jit(solution)/shard_map/ppermute | solution.py:75
  114.1 7.0 %all-to-all-done = f32[128,1,128]{2,1,0:T(1,128)S(1)} async-done(((f32[128,1,128]{2,1,0:T(1,128)}), f32[128,1,128]{2,1,0:T(1,128)S(1)}, u32[]{:S(2)}, u32[]{:S(2)}) %all-to-all-start) | async-done | bytes 65568 | tf_op jit(solution)/shard_map/all_to_all | solution.py:230
  121.1 0.6 reduce_sum.29
  122.6 1.0 broadcast_in_dim.14
  123.7 3.6 %all-to-all-start.1 = ((bf16[16,224,128]{2,1,0:T(8,128)(2,1)}), bf16[16,224,128]{2,1,0:T(8,128)(2,1)S(1)}, u32[]{:S(2)}, u32[]{:S(2)}) async-start(bf16[16,224,128]{2,1,0:T(8,128)(2,1)} %broadcast_in_dim.14), calls=%async_computation.1 | async-start | bytes 1835008 | tf_op jit(solution)/shard_map/all_to_all | solution.py:246
  127.8 3.2 %collective-permute-start.28 = (f32[128,128]{1,0:T(8,128)S(1)}, f32[128,128]{1,0:T(8,128)S(1)}, u32[]{:S(2)}, u32[]{:S(2)}) collective-permute-start(f32[128,128]{1,0:T(8,128)S(1)} %pad_maximum_fusion.21), channel_id=1, source_target_pairs={{0,4},{1,5},{2,6},{3,7},{4,0},{5,1},{6,2},{7,3},{8,12},{9,13},{10,... | collective-permute-start | bytes 196616 | tf_op jit(solution)/shard_map/ppermute | solution.py:71
  131.0 1.1 collective-permute-done.29
  132.1 3.4 %collective-permute-done.28 = f32[128,128]{1,0:T(8,128)S(1)} collective-permute-done((f32[128,128]{1,0:T(8,128)S(1)}, f32[128,128]{1,0:T(8,128)S(1)}, u32[]{:S(2)}, u32[]{:S(2)}) %collective-permute-start.28) | collective-permute-done | bytes 65568 | tf_op jit(solution)/shard_map/ppermute | solution.py:71
  135.5 2.1 %collective-permute-done.27 = f32[128,128]{1,0:T(8,128)S(1)} collective-permute-done((f32[128,128]{1,0:T(8,128)S(1)}, f32[128,128]{1,0:T(8,128)S(1)}, u32[]{:S(2)}, u32[]{:S(2)}) %collective-permute-start.27) | collective-permute-done | bytes 65568 | tf_op jit(solution)/shard_map/ppermute | solution.py:71
  137.7 3.4 %all-to-all-done.1 = bf16[16,224,128]{2,1,0:T(8,128)(2,1)S(1)} async-done(((bf16[16,224,128]{2,1,0:T(8,128)(2,1)}), bf16[16,224,128]{2,1,0:T(8,128)(2,1)S(1)}, u32[]{:S(2)}, u32[]{:S(2)}) %all-to-all-start.1) | async-done | bytes 917536 | tf_op jit(solution)/shard_map/all_to_all | solution.py:246
  141.0 3.1 %collective-permute-start.30 = (bf16[16,224,128]{2,1,0:T(8,128)(2,1)S(1)}, bf16[16,224,128]{2,1,0:T(8,128)(2,1)S(1)}, u32[]{:S(2)}, u32[]{:S(2)}) collective-permute-start(bf16[16,224,128]{2,1,0:T(8,128)(2,1)S(1)} %all-to-all-done.1), channel_id=1, source_target_pairs={{0,8},{8,0},{1,9},{9,1},{2,10},{10,2},{3,11},{11,3},{4,12},{12,4},... | collective-permute-start | bytes 2752520 | tf_op jit(solution)/shard_map/ppermute | solution.py:67
  144.2 2.0 %collective-permute-done.30 = bf16[16,224,128]{2,1,0:T(8,128)(2,1)S(1)} collective-permute-done((bf16[16,224,128]{2,1,0:T(8,128)(2,1)S(1)}, bf16[16,224,128]{2,1,0:T(8,128)(2,1)S(1)}, u32[]{:S(2)}, u32[]{:S(2)}) %collective-permute-start.30) | collective-permute-done | bytes 917536 | tf_op jit(solution)/shard_map/ppermute | solution.py:67
  146.6 1.3 copy-done.2
  147.9 2.1 %fusion.1 = bf16[256,3584]{1,0:T(8,128)(2,1)} fusion(bf16[256,3584]{1,0:T(8,128)(2,1)S(1)} %bitcast.264, bf16[256,3584]{1,0:T(8,128)(2,1)S(1)} %copy-done.2, f32[256,256]{1,0:T(8,128)S(1)} %bitcast.269, f32[256,256]{1,0:T(8,128)S(1)} %bitcast.268, f32[256,256]{1,0:T(8,128)S(1)} %bitcast.271, f32[256,256]{1,0:T(8,128)S(1)} %bitcast.270), kind=kOutput, calls=%fused_computation.2 | convolution fusion | flops 474284032 | bytes 6553600 | tf_op jit(solution)/shard_map/dot_general | solution.py:257
  (104 shorter events, 7.2 us)
Async XLA Ops:
  1.9 6.8 %collective-permute-start.2 = (bf16[480,128]{1,0:T(8,128)(2,1)S(1)}, bf16[480,128]{1,0:T(8,128)(2,1)S(1)}, u32[]{:S(2)}, u32[]{:S(2)}) collective-permute-start(bf16[480,128]{1,0:T(8,128)(2,1)S(1)} %pad_maximum_fusion.20), channel_id=1, source_target_pairs={{0,48},{8,200},{16,0},{24,216},{32,16},{40,232},{48,32},{56,248},{... | collective-permute-start | bytes 368648 | tf_op jit(solution)/shard_map/factors_p/ppermute | solution.py:54
  5.5 5.5 %collective-permute-start.1 = (bf16[480,128]{1,0:T(8,128)(2,1)S(1)}, bf16[480,128]{1,0:T(8,128)(2,1)S(1)}, u32[]{:S(2)}, u32[]{:S(2)}) collective-permute-start(bf16[480,128]{1,0:T(8,128)(2,1)S(1)} %pad_maximum_fusion.20), channel_id=1, source_target_pairs={{0,32},{8,136},{16,48},{24,152},{32,0},{40,168},{48,16},{56,184},{... | collective-permute-start | bytes 368648 | tf_op jit(solution)/shard_map/factors_p/ppermute | solution.py:54
  5.8 6.5 %collective-permute-start = (bf16[480,128]{1,0:T(8,128)(2,1)S(1)}, bf16[480,128]{1,0:T(8,128)(2,1)S(1)}, u32[]{:S(2)}, u32[]{:S(2)}) collective-permute-start(bf16[480,128]{1,0:T(8,128)(2,1)S(1)} %pad_maximum_fusion.20), channel_id=1, source_target_pairs={{0,16},{8,72},{16,32},{24,88},{32,48},{40,104},{48,0},{56,120},{64... | collective-permute-start | bytes 368648 | tf_op jit(solution)/shard_map/factors_p/ppermute | solution.py:54
  12.6 7.7 %collective-permute-start.5 = (bf16[4,224,128]{2,1,0:T(8,128)(2,1)S(1)}, bf16[4,224,128]{2,1,0:T(8,128)(2,1)S(1)}, u32[]{:S(2)}, u32[]{:S(2)}) collective-permute-start(bf16[4,224,128]{2,1,0:T(8,128)(2,1)S(1)} %pad_maximum_fusion.16), channel_id=1, source_target_pairs={{0,192},{8,56},{16,208},{24,8},{32,224},{40,24},{48,240},{56,40},{... | collective-permute-start | bytes 688136 | tf_op jit(solution)/shard_map/a_q/ppermute | solution.py:58
  14.8 6.5 %collective-permute-start.4 = (bf16[4,224,128]{2,1,0:T(8,128)(2,1)S(1)}, bf16[4,224,128]{2,1,0:T(8,128)(2,1)S(1)}, u32[]{:S(2)}, u32[]{:S(2)}) collective-permute-start(bf16[4,224,128]{2,1,0:T(8,128)(2,1)S(1)} %pad_maximum_fusion.16), channel_id=1, source_target_pairs={{0,128},{8,40},{16,144},{24,56},{32,160},{40,8},{48,176},{56,24},{... | collective-permute-start | bytes 688136 | tf_op jit(solution)/shard_map/a_q/ppermute | solution.py:58
  15.3 8.6 %collective-permute-start.3 = (bf16[4,224,128]{2,1,0:T(8,128)(2,1)S(1)}, bf16[4,224,128]{2,1,0:T(8,128)(2,1)S(1)}, u32[]{:S(2)}, u32[]{:S(2)}) collective-permute-start(bf16[4,224,128]{2,1,0:T(8,128)(2,1)S(1)} %pad_maximum_fusion.16), channel_id=1, source_target_pairs={{0,64},{8,24},{16,80},{24,40},{32,96},{40,56},{48,112},{56,8},{64,... | collective-permute-start | bytes 688136 | tf_op jit(solution)/shard_map/a_q/ppermute | solution.py:58
  24.3 5.4 %collective-permute-start.6 = (bf16[4,4,224,128]{3,2,0,1:T(8,128)(2,1)S(1)}, bf16[4,4,224,128]{3,2,0,1:T(8,128)(2,1)S(1)}, u32[]{:S(2)}, u32[]{:S(2)}) collective-permute-start(bf16[4,4,224,128]{3,2,0,1:T(8,128)(2,1)S(1)} %pad_maximum_fusion.6), channel_id=1, source_target_pairs={{0,8},{8,0},{1,9},{9,1},{2,10},{10,2},{3,11},{11,3},{4,12},{12,4},... | collective-permute-start | bytes 2752520 | tf_op jit(solution)/shard_map/a_cores/ppermute | solution.py:67
  27.6 11.2 %collective-permute-start.11 = (bf16[4,256,128]{2,1,0:T(8,128)(2,1)S(1)}, bf16[4,256,128]{2,1,0:T(8,128)(2,1)S(1)}, u32[]{:S(2)}, u32[]{:S(2)}) collective-permute-start(bf16[4,256,128]{2,1,0:T(8,128)(2,1)S(1)} %pad_maximum_fusion.11), channel_id=1, source_target_pairs={{0,192},{8,56},{16,208},{24,8},{32,224},{40,24},{48,240},{56,40},{... | collective-permute-start | bytes 786440 | tf_op jit(solution)/shard_map/b_q/ppermute | solution.py:58
  27.9 10.9 %collective-permute-start.10 = (bf16[4,256,128]{2,1,0:T(8,128)(2,1)S(1)}, bf16[4,256,128]{2,1,0:T(8,128)(2,1)S(1)}, u32[]{:S(2)}, u32[]{:S(2)}) collective-permute-start(bf16[4,256,128]{2,1,0:T(8,128)(2,1)S(1)} %pad_maximum_fusion.11), channel_id=1, source_target_pairs={{0,128},{8,40},{16,144},{24,56},{32,160},{40,8},{48,176},{56,24},{... | collective-permute-start | bytes 786440 | tf_op jit(solution)/shard_map/b_q/ppermute | solution.py:58
  28.4 10.4 %collective-permute-start.9 = (bf16[4,256,128]{2,1,0:T(8,128)(2,1)S(1)}, bf16[4,256,128]{2,1,0:T(8,128)(2,1)S(1)}, u32[]{:S(2)}, u32[]{:S(2)}) collective-permute-start(bf16[4,256,128]{2,1,0:T(8,128)(2,1)S(1)} %pad_maximum_fusion.11), channel_id=1, source_target_pairs={{0,64},{8,24},{16,80},{24,40},{32,96},{40,56},{48,112},{56,8},{64,... | collective-permute-start | bytes 786440 | tf_op jit(solution)/shard_map/b_q/ppermute | solution.py:58
  29.9 2.0 %copy-start = (bf16[512,3584]{1,0:T(8,128)(2,1)S(1)}, bf16[512,3584]{1,0:T(8,128)(2,1)}, u32[]{:S(2)}) copy-start(bf16[512,3584]{1,0:T(8,128)(2,1)} %param.9) | copy-start | bytes 11010052
  33.0 10.3 %copy-start.4 = (f32[4,2,32,512]{3,2,1,0:T(8,128)}, f32[4,2,32,512]{3,2,1,0:T(8,128)S(1)}, u32[]{:S(2)}) copy-start(f32[4,2,32,512]{3,2,1,0:T(8,128)S(1)} %fusion.2) | copy-start | bytes 1572868
  33.1 9.2 %collective-permute-start.8 = (f32[4,32,256]{2,1,0:T(8,128)S(1)}, f32[4,32,256]{2,1,0:T(8,128)S(1)}, u32[]{:S(2)}, u32[]{:S(2)}) collective-permute-start(f32[4,32,256]{2,1,0:T(8,128)S(1)} %get-tuple-element.88), channel_id=1, source_target_pairs={{0,7},{1,2},{2,1},{3,4},{4,3},{5,6},{6,5},{7,0},{8,15},{9,10},{10,... | collective-permute-start | bytes 393224 | tf_op jit(solution)/shard_map/act_pairs/ppermute | solution.py:79
  38.8 4.4 %collective-permute-start.7 = (f32[4,32,256]{2,1,0:T(8,128)S(1)}, f32[4,32,256]{2,1,0:T(8,128)S(1)}, u32[]{:S(2)}, u32[]{:S(2)}) collective-permute-start(f32[4,32,256]{2,1,0:T(8,128)S(1)} %get-tuple-element.87), channel_id=1, source_target_pairs={{0,1},{1,0},{2,3},{3,2},{4,5},{5,4},{6,7},{7,6},{8,9},{9,8},{10,11... | collective-permute-start | bytes 393224 | tf_op jit(solution)/shard_map/act_pairs/ppermute | solution.py:75
  43.6 9.0 %collective-permute-start.12 = (bf16[4,4,256,128]{3,2,0,1:T(8,128)(2,1)S(1)}, bf16[4,4,256,128]{3,2,0,1:T(8,128)(2,1)S(1)}, u32[]{:S(2)}, u32[]{:S(2)}) collective-permute-start(bf16[4,4,256,128]{3,2,0,1:T(8,128)(2,1)S(1)} %copy.25), channel_id=1, source_target_pairs={{0,8},{8,0},{1,9},{9,1},{2,10},{10,2},{3,11},{11,3},{4,12},{12,4},... | collective-permute-start | bytes 3145736 | tf_op jit(solution)/shard_map/b_cores/ppermute | solution.py:67
  45.2 8.2 %slice-start = ((s8[8388608]{0:T(1024)(128)(4,1)}), s8[4194304]{0:T(1024)(128)(4,1)S(1)}, s32[]{:S(2)}) async-start(s8[8388608]{0:T(1024)(128)(4,1)} %bitcast.261), calls=%async_computation.2 | async-start | bytes 8388608
  46.3 11.8 %collective-permute-start.13 = (f32[32,512]{1,0:T(8,128)S(1)}, f32[32,512]{1,0:T(8,128)S(1)}, u32[]{:S(2)}, u32[]{:S(2)}) collective-permute-start(f32[32,512]{1,0:T(8,128)S(1)} %get-tuple-element.86), channel_id=1, source_target_pairs={{0,2},{1,3},{2,4},{3,5},{4,6},{5,7},{6,0},{7,1},{8,10},{9,11},{10,... | collective-permute-start | bytes 196616 | tf_op jit(solution)/shard_map/act_shifts/ppermute | solution.py:71
  46.9 11.3 %collective-permute-start.14 = (f32[32,512]{1,0:T(8,128)S(1)}, f32[32,512]{1,0:T(8,128)S(1)}, u32[]{:S(2)}, u32[]{:S(2)}) collective-permute-start(f32[32,512]{1,0:T(8,128)S(1)} %get-tuple-element.85), channel_id=1, source_target_pairs={{0,6},{1,7},{2,0},{3,1},{4,2},{5,3},{6,4},{7,5},{8,14},{9,15},{10,... | collective-permute-start | bytes 196616 | tf_op jit(solution)/shard_map/act_shifts/ppermute | solution.py:71
  50.0 8.5 %collective-permute-start.15 = (f32[32,512]{1,0:T(8,128)S(1)}, f32[32,512]{1,0:T(8,128)S(1)}, u32[]{:S(2)}, u32[]{:S(2)}) collective-permute-start(f32[32,512]{1,0:T(8,128)S(1)} %get-tuple-element.84), channel_id=1, source_target_pairs={{0,4},{1,5},{2,6},{3,7},{4,0},{5,1},{6,2},{7,3},{8,12},{9,13},{10,... | collective-permute-start | bytes 196616 | tf_op jit(solution)/shard_map/act_shifts/ppermute | solution.py:71
  53.0 2.2 %slice-start.1 = ((s8[8388608]{0:T(1024)(128)(4,1)}), s8[4194304]{0:T(1024)(128)(4,1)S(1)}, s32[]{:S(2)}) async-start(s8[8388608]{0:T(1024)(128)(4,1)} %bitcast.261), calls=%async_computation.3 | async-start | bytes 8388608
  58.5 5.0 %collective-permute-start.16 = (bf16[128,512]{1,0:T(8,128)(2,1)S(1)}, bf16[128,512]{1,0:T(8,128)(2,1)S(1)}, u32[]{:S(2)}, u32[]{:S(2)}) collective-permute-start(bf16[128,512]{1,0:T(8,128)(2,1)S(1)} %fusion.4), channel_id=1, source_target_pairs={{0,7},{1,2},{2,1},{3,4},{4,3},{5,6},{6,5},{7,0},{8,15},{9,10},{10,... | collective-permute-start | bytes 393224 | tf_op jit(solution)/shard_map/back_pairs/ppermute | solution.py:79
  60.1 3.7 %copy-start.1 = (bf16[512,3584]{1,0:T(8,128)(2,1)S(1)}, bf16[512,3584]{1,0:T(8,128)(2,1)}, u32[]{:S(2)}) copy-start(bf16[512,3584]{1,0:T(8,128)(2,1)} %param.9) | copy-start | bytes 11010052
  64.5 6.6 %collective-permute-start.17 = (f32[128,3584]{1,0:T(8,128)S(1)}, f32[128,3584]{1,0:T(8,128)}, u32[]{:S(2)}, u32[]{:S(2)}) collective-permute-start(f32[128,3584]{1,0:T(8,128)S(1)} %fusion.56), channel_id=1, source_target_pairs={{0,8},{8,0},{1,9},{9,1},{2,10},{10,2},{3,11},{11,3},{4,12},{12,4},... | collective-permute-start | bytes 5505032 | tf_op jit(solution)/shard_map/grad_a_cores/ppermute | solution.py:67
  67.0 3.9 %collective-permute-start.18 = (f32[4,4,64,128]{3,2,1,0:T(8,128)S(1)}, f32[4,4,64,128]{3,2,1,0:T(8,128)S(1)}, u32[]{:S(2)}, u32[]{:S(2)}) collective-permute-start(f32[4,4,64,128]{3,2,1,0:T(8,128)S(1)} %get-tuple-element.58), channel_id=1, source_target_pairs={{0,8},{8,0},{1,9},{9,1},{2,10},{10,2},{3,11},{11,3},{4,12},{12,4},... | collective-permute-start | bytes 1572872 | tf_op jit(solution)/shard_map/grad_b_cores/ppermute | solution.py:67
  72.8 10.9 %collective-permute-start.21 = (f32[4,288,128]{2,1,0:T(8,128)S(1)}, f32[4,288,128]{2,1,0:T(8,128)S(1)}, u32[]{:S(2)}, u32[]{:S(2)}) collective-permute-start(f32[4,288,128]{2,1,0:T(8,128)S(1)} %maximum_maximum_fusion.2), channel_id=1, source_target_pairs={{0,32},{8,136},{16,48},{24,152},{32,0},{40,168},{48,16},{56,184},{... | collective-permute-start | bytes 1769480 | tf_op jit(solution)/shard_map/grads_p/ppermute | solution.py:54
  76.2 13.0 %collective-permute-start.20 = (f32[4,288,128]{2,1,0:T(8,128)S(1)}, f32[4,288,128]{2,1,0:T(8,128)S(1)}, u32[]{:S(2)}, u32[]{:S(2)}) collective-permute-start(f32[4,288,128]{2,1,0:T(8,128)S(1)} %maximum_maximum_fusion.1), channel_id=1, source_target_pairs={{0,48},{8,200},{16,0},{24,216},{32,16},{40,232},{48,32},{56,248},{... | collective-permute-start | bytes 1769480 | tf_op jit(solution)/shard_map/grads_p/ppermute | solution.py:54
  76.6 13.4 %collective-permute-start.19 = (f32[4,288,128]{2,1,0:T(8,128)S(1)}, f32[4,288,128]{2,1,0:T(8,128)S(1)}, u32[]{:S(2)}, u32[]{:S(2)}) collective-permute-start(f32[4,288,128]{2,1,0:T(8,128)S(1)} %maximum_maximum_fusion), channel_id=1, source_target_pairs={{0,16},{8,72},{16,32},{24,88},{32,48},{40,104},{48,0},{56,120},{64... | collective-permute-start | bytes 1769480 | tf_op jit(solution)/shard_map/grads_p/ppermute | solution.py:54
  90.0 21.3 %copy-start.3 = (f32[256,256]{1,0:T(8,128)S(1)}, f32[256,256]{1,0:T(8,128)}, u32[]{:S(2)}) copy-start(f32[256,256]{1,0:T(8,128)} %param.15) | copy-start | bytes 786436
  90.0 21.4 %copy-start.6 = (f32[256,256]{1,0:T(8,128)S(1)}, f32[256,256]{1,0:T(8,128)}, u32[]{:S(2)}) copy-start(f32[256,256]{1,0:T(8,128)} %param.16) | copy-start | bytes 786436
  90.2 21.4 %copy-start.7 = (f32[256,256]{1,0:T(8,128)S(1)}, f32[256,256]{1,0:T(8,128)}, u32[]{:S(2)}) copy-start(f32[256,256]{1,0:T(8,128)} %param.17) | copy-start | bytes 786436
  90.2 32.3 %copy-start.5 = (f32[8,3584]{1,0:T(8,128)S(1)}, f32[8,3584]{1,0:T(8,128)}, u32[]{:S(2)}) copy-start(f32[8,3584]{1,0:T(8,128)} %param.12) | copy-start | bytes 344068
  90.2 32.3 %copy-start.8 = (f32[8,3584]{1,0:T(8,128)S(1)}, f32[8,3584]{1,0:T(8,128)}, u32[]{:S(2)}) copy-start(f32[8,3584]{1,0:T(8,128)} %param.14) | copy-start | bytes 344068
  90.2 32.3 %copy-start.9 = (f32[8,3584]{1,0:T(8,128)S(1)}, f32[8,3584]{1,0:T(8,128)}, u32[]{:S(2)}) copy-start(f32[8,3584]{1,0:T(8,128)} %param.13) | copy-start | bytes 344068
  90.2 5.9 %collective-permute-start.24 = (f32[288,128]{1,0:T(8,128)S(1)}, f32[288,128]{1,0:T(8,128)S(1)}, u32[]{:S(2)}, u32[]{:S(2)}) collective-permute-start(f32[288,128]{1,0:T(8,128)S(1)} %get-tuple-element.72), channel_id=1, source_target_pairs={{0,128},{8,40},{16,144},{24,56},{32,160},{40,8},{48,176},{56,24},{... | collective-permute-start | bytes 442376 | tf_op jit(solution)/shard_map/grads_q/ppermute | solution.py:58
  91.0 5.2 %collective-permute-start.23 = (f32[288,128]{1,0:T(8,128)S(1)}, f32[288,128]{1,0:T(8,128)S(1)}, u32[]{:S(2)}, u32[]{:S(2)}) collective-permute-start(f32[288,128]{1,0:T(8,128)S(1)} %get-tuple-element.73), channel_id=1, source_target_pairs={{0,192},{8,56},{16,208},{24,8},{32,224},{40,24},{48,240},{56,40},{... | collective-permute-start | bytes 442376 | tf_op jit(solution)/shard_map/grads_q/ppermute | solution.py:58
  91.9 5.7 %collective-permute-start.22 = (f32[288,128]{1,0:T(8,128)S(1)}, f32[288,128]{1,0:T(8,128)S(1)}, u32[]{:S(2)}, u32[]{:S(2)}) collective-permute-start(f32[288,128]{1,0:T(8,128)S(1)} %get-tuple-element.71), channel_id=1, source_target_pairs={{0,64},{8,24},{16,80},{24,40},{32,96},{40,56},{48,112},{56,8},{64,... | collective-permute-start | bytes 442376 | tf_op jit(solution)/shard_map/grads_q/ppermute | solution.py:58
  97.7 5.1 %collective-permute-start.25 = (f32[8,128]{1,0:T(8,128)S(1)}, f32[8,128]{1,0:T(8,128)S(1)}, u32[]{:S(2)}, u32[]{:S(2)}) collective-permute-start(f32[8,128]{1,0:T(8,128)S(1)} %slice.94), channel_id=1, source_target_pairs={{0,8},{8,0},{1,9},{9,1},{2,10},{10,2},{3,11},{11,3},{4,12},{12,4},... | collective-permute-start | bytes 12296 | tf_op jit(solution)/shard_map/ppermute | solution.py:67
  103.5 17.6 %all-to-all-start = ((f32[128,1,128]{2,1,0:T(1,128)}), f32[128,1,128]{2,1,0:T(1,128)S(1)}, u32[]{:S(2)}, u32[]{:S(2)}) async-start(f32[128,1,128]{2,1,0:T(1,128)} %broadcast_in_dim.13), calls=%async_computation | async-start | bytes 131072 | tf_op jit(solution)/shard_map/all_to_all | solution.py:230
  110.6 3.4 %collective-permute-start.26 = (f32[64,128]{1,0:T(8,128)S(1)}, f32[64,128]{1,0:T(8,128)S(1)}, u32[]{:S(2)}, u32[]{:S(2)}) collective-permute-start(f32[64,128]{1,0:T(8,128)S(1)} %get-tuple-element.99), channel_id=1, source_target_pairs={{0,1},{1,0},{2,3},{3,2},{4,5},{5,4},{6,7},{7,6},{8,9},{9,8},{10,11... | collective-permute-start | bytes 98312 | tf_op jit(solution)/shard_map/ppermute | solution.py:75
  123.7 17.4 %all-to-all-start.1 = ((bf16[16,224,128]{2,1,0:T(8,128)(2,1)}), bf16[16,224,128]{2,1,0:T(8,128)(2,1)S(1)}, u32[]{:S(2)}, u32[]{:S(2)}) async-start(bf16[16,224,128]{2,1,0:T(8,128)(2,1)} %broadcast_in_dim.14), calls=%async_computation.1 | async-start | bytes 1835008 | tf_op jit(solution)/shard_map/all_to_all | solution.py:246
  127.3 4.8 %collective-permute-start.29 = (f32[128,128]{1,0:T(8,128)S(1)}, f32[128,128]{1,0:T(8,128)S(1)}, u32[]{:S(2)}, u32[]{:S(2)}) collective-permute-start(f32[128,128]{1,0:T(8,128)S(1)} %pad_maximum_fusion.21), channel_id=1, source_target_pairs={{0,6},{1,7},{2,0},{3,1},{4,2},{5,3},{6,4},{7,5},{8,14},{9,15},{10,... | collective-permute-start | bytes 196616 | tf_op jit(solution)/shard_map/ppermute | solution.py:71
  127.8 7.8 %collective-permute-start.28 = (f32[128,128]{1,0:T(8,128)S(1)}, f32[128,128]{1,0:T(8,128)S(1)}, u32[]{:S(2)}, u32[]{:S(2)}) collective-permute-start(f32[128,128]{1,0:T(8,128)S(1)} %pad_maximum_fusion.21), channel_id=1, source_target_pairs={{0,4},{1,5},{2,6},{3,7},{4,0},{5,1},{6,2},{7,3},{8,12},{9,13},{10,... | collective-permute-start | bytes 196616 | tf_op jit(solution)/shard_map/ppermute | solution.py:71
  131.0 6.6 %collective-permute-start.27 = (f32[128,128]{1,0:T(8,128)S(1)}, f32[128,128]{1,0:T(8,128)S(1)}, u32[]{:S(2)}, u32[]{:S(2)}) collective-permute-start(f32[128,128]{1,0:T(8,128)S(1)} %pad_maximum_fusion.21), channel_id=1, source_target_pairs={{0,2},{1,3},{2,4},{3,5},{4,6},{5,7},{6,0},{7,1},{8,10},{9,11},{10,... | collective-permute-start | bytes 196616 | tf_op jit(solution)/shard_map/ppermute | solution.py:71
  141.0 5.2 %collective-permute-start.30 = (bf16[16,224,128]{2,1,0:T(8,128)(2,1)S(1)}, bf16[16,224,128]{2,1,0:T(8,128)(2,1)S(1)}, u32[]{:S(2)}, u32[]{:S(2)}) collective-permute-start(bf16[16,224,128]{2,1,0:T(8,128)(2,1)S(1)} %all-to-all-done.1), channel_id=1, source_target_pairs={{0,8},{8,0},{1,9},{9,1},{2,10},{10,2},{3,11},{11,3},{4,12},{12,4},... | collective-permute-start | bytes 2752520 | tf_op jit(solution)/shard_map/ppermute | solution.py:67
  146.4 1.5 %copy-start.2 = (bf16[256,3584]{1,0:T(8,128)(2,1)S(1)}, bf16[256,3584]{1,0:T(8,128)(2,1)}, u32[]{:S(2)}) copy-start(bf16[256,3584]{1,0:T(8,128)(2,1)} %param.11) | copy-start | bytes 5505028
